TPU v7x, 32 devices: a whole 2x2x4 slice. The times are simulated.
32 devices in a mesh: dp: 8 (over y, x, core), region: 4 (over z).
Axes of the slice: x: 2, y: 2, z: 4, core: 2. Of those that a mesh axis runs over, the one named last changes fastest.
Arguments:
- inputs: bfloat16 [8, 2, 1024, 256], P('dp', None, 'region'), may hold values from -6 to 6
- cotangent: bfloat16 [8, 2, 1024, 256], P('dp', None, 'region'), may hold values from -6 to 6
- w_filter: bfloat16 [2, 256, 256], replicated, may hold values from -0.25 to 0.25
- w_gate: bfloat16 [2, 256, 256], replicated, may hold values from -0.25 to 0.25
- w_mix: bfloat16 [2, 256, 256], replicated, may hold values from -0.25 to 0.25
- neighbours: int32 [8, 6], replicated, may hold values from 0 to 7, as said below
- adjacency: bfloat16 [8, 6, 128, 128], P('region'), may hold values from -0.21875 to 0.21875
Outputs:
- grad_inputs: bfloat16 [8, 2, 1024, 256], P('dp', None, 'region')
- grad_filter: float32 [2, 256, 256], replicated
- grad_gate: float32 [2, 256, 256], replicated
- grad_mix: float32 [2, 256, 256], replicated
Inputs may be any that keep to these rules, and one draw needn't show every extreme that they name: `neighbours`: for every region r (tiles r * 2 to (r + 1) * 2 - 1), exactly 3 of the 12 entries of its tiles' lists name tiles of other regions, each of a different region, so at most 1 name tiles of any one other region; all other entries name tiles of region r.
All inputs are finite; a program needn't handle non-finite values.
Results may differ from a plain program's by a relative error of at most 0.0053.
Values may be sent and summed in bfloat16 or wider, within the bound.
No kernel may reach another device: no remote copies, remote signals or barrier semaphores. Data moves between devices by JAX's collectives and lax.ppermute only.
A program may use at most 64 MiB of HBM per device.

v0:
```python
import math

import jax
import jax.numpy as jnp
from jax import lax
from jax.sharding import PartitionSpec as P

CAP = 1


def per_device(inputs, cotangent, w_filter, w_gate, w_mix, neighbours, adjacency):
    regions = lax.axis_size("region")
    region_id = lax.axis_index("region")
    windows, steps, site_count, chans = inputs.shape
    tiles_dev = site_count // 128
    per_tile = neighbours.shape[1]
    entries = tiles_dev * per_tile
    capacity = CAP
    table = neighbours.reshape(regions, entries)
    owners = table // tiles_dev
    local_tile = table % tiles_dev
    sources = jnp.arange(regions, dtype=jnp.int32)
    positions = jnp.arange(entries)
    earlier = positions[:, None] > positions[None, :]
    ranks = jnp.sum(
        ((owners[:, :, None] == owners[:, None, :]) & earlier[None]).astype(jnp.int32), axis=2
    )
    slot_ids = jnp.arange(capacity)
    remote_entry = owners != sources[:, None]
    hits = (
        (owners[:, None, :] == region_id)
        & (ranks[:, None, :] == slot_ids[None, :, None])
        & remote_entry[:, None, :]
    )
    send_tile = jnp.sum(jnp.where(hits, local_tile[:, None, :], 0), axis=2).reshape(-1)
    send_used = jnp.any(hits, axis=2).reshape(-1)
    own_owner = lax.dynamic_index_in_dim(owners, region_id, 0, keepdims=False)
    own_rank = lax.dynamic_index_in_dim(ranks, region_id, 0, keepdims=False)
    own_tiles = lax.dynamic_index_in_dim(table, region_id, 0, keepdims=False)
    own_local_tile = lax.dynamic_index_in_dim(local_tile, region_id, 0, keepdims=False)
    at_home = own_owner == region_id
    drop_index = jnp.where(at_home, regions * capacity, own_owner * capacity + own_rank)
    w_cat = jnp.concatenate(
        [
            jnp.concatenate([w_filter[0], w_gate[0]], axis=1),
            jnp.concatenate([w_filter[1], w_gate[1]], axis=1),
        ],
        axis=0,
    )
    w_mixed = w_mix.reshape(2 * chans, chans)
    previous = jnp.concatenate([jnp.zeros_like(inputs[:, :1]), inputs[:, :-1]], axis=1)
    joint = jnp.concatenate([inputs, previous], axis=3)
    act = jnp.einsum("btsi,io->btso", joint, w_cat, preferred_element_type=jnp.float32)
    filt = jnp.tanh(act[..., :chans])
    gate = jax.nn.sigmoid(act[..., chans:])
    hidden = (filt * gate).astype(jnp.bfloat16)
    tiled = hidden.reshape(windows, steps, tiles_dev, 128, chans)
    piece = lax.all_gather(tiled, "region", axis=2, tiled=True)
    count = piece.shape[2]
    select = (own_tiles[:, None] == jnp.arange(count)[None, :]).astype(jnp.bfloat16)
    chosen = jnp.einsum("en,btnqc->bteqc", select, piece, preferred_element_type=jnp.float32)
    chosen = chosen.astype(jnp.bfloat16).reshape(windows, steps, tiles_dev, per_tile, 128, chans)
    graph_sum = jnp.einsum(
        "jkpq,btjkqc->btjpc", adjacency, chosen, preferred_element_type=jnp.float32
    )
    graph = graph_sum.astype(jnp.bfloat16).reshape(windows, steps, site_count, chans)
    both = jnp.concatenate([hidden, graph], axis=3)
    mix_sum = jnp.einsum("btsi,btsc->ic", both, cotangent, preferred_element_type=jnp.float32)
    back = jnp.einsum("btsc,ic->btsi", cotangent, w_mixed, preferred_element_type=jnp.float32)
    direct = back[..., :chans]
    graph_cot = (
        back[..., chans:].astype(jnp.bfloat16).reshape(windows, steps, tiles_dev, 128, chans)
    )
    term = jnp.einsum(
        "jkpq,btjpc->btjkqc", adjacency, graph_cot, preferred_element_type=jnp.float32
    )
    term = term.astype(jnp.bfloat16).reshape(windows, steps, entries, 128, chans)
    outgoing_back = jnp.zeros((windows, steps, regions * capacity, 128, chans), jnp.bfloat16)
    outgoing_back = outgoing_back.at[:, :, drop_index].set(term, mode="drop")
    outgoing_back = outgoing_back.reshape(windows, steps, regions, capacity, 128, chans)
    returned = lax.all_to_all(outgoing_back, "region", split_axis=2, concat_axis=2, tiled=True)
    returned = returned.reshape(windows, steps, regions * capacity, 128, chans)
    owner_hot = (
        (send_tile[None, :] == jnp.arange(tiles_dev)[:, None]) & send_used[None, :]
    ).astype(jnp.bfloat16)
    graph_grad = jnp.einsum(
        "ln,btnqc->btlqc", owner_hot, returned, preferred_element_type=jnp.float32
    )
    home_hot = (
        (own_local_tile[None, :] == jnp.arange(tiles_dev)[:, None]) & at_home[None, :]
    ).astype(jnp.bfloat16)
    home_grad = jnp.einsum("le,bteqc->btlqc", home_hot, term, preferred_element_type=jnp.float32)
    grad_hidden = direct + (graph_grad + home_grad).reshape(windows, steps, site_count, chans)
    act_cot = jnp.concatenate(
        [grad_hidden * gate * (1.0 - filt * filt), grad_hidden * filt * gate * (1.0 - gate)], axis=3
    ).astype(jnp.bfloat16)
    conv_sum = jnp.einsum("btsi,btso->io", joint, act_cot, preferred_element_type=jnp.float32)
    back_in = jnp.einsum("btso,io->btsi", act_cot, w_cat, preferred_element_type=jnp.float32)
    later = jnp.concatenate(
        [back_in[:, 1:, :, chans:], jnp.zeros((windows, 1, site_count, chans), jnp.float32)], axis=1
    )
    grad_inputs = (cotangent.astype(jnp.float32) + back_in[..., :chans] + later).astype(
        jnp.bfloat16
    )
    conv_total, mix_total = lax.psum((conv_sum, mix_sum), ("dp", "region"))
    total_rows = windows * lax.axis_size("dp") * steps * site_count * regions
    factor = 1.0 / math.sqrt(total_rows)
    grad_filter = (conv_total[:, :chans] * factor).reshape(2, chans, chans)
    grad_gate = (conv_total[:, chans:] * factor).reshape(2, chans, chans)
    grad_mix = (mix_total * factor).reshape(2, chans, chans)
    return (grad_inputs, grad_filter, grad_gate, grad_mix)


def solution(mesh):
    return jax.shard_map(
        per_device,
        mesh=mesh,
        in_specs=(
            P("dp", None, "region", None),
            P("dp", None, "region", None),
            P(),
            P(),
            P(),
            P(),
            P("region", None, None, None),
        ),
        out_specs=(P("dp", None, "region", None), P(), P(), P()),
        check_vma=False,
    )
```

profile of v0, /device:TPU:0, one launch (start us, length us, event | category | flops | bytes accessed | tf_op | source)
XLA Modules:
  0.0 216.6 jit_solution(12049574940115928036)
XLA Ops:
  7.2 0.8 reshape.354
  8.6 1.4 convolution_bitcast_fusion
  10.0 0.9 copy-done.1
  11.6 0.7 copy.87
  12.8 1.3 copy.88
  14.2 3.2 %scatter_fusion = bf16[2,4,128,256]{3,2,1,0:T(8,128)(2,1)S(1)} fusion(bf16[2,4,128,256]{3,2,1,0:T(8,128)(2,1)S(1)} %broadcast.246, s32[12]{0:T(128)S(1)} %fusion.61, bf16[12,2,128,256]{3,2,1,0:T(8,128)(2,1)} %copy.88), kind=kCustom, calls=%fused_computation | custom fusion | bytes 4718640 | tf_op jit(solution)/shard_map/scatter | solution.py:79
  17.4 0.8 copy.89
  18.3 6.3 %all-to-all-start = ((bf16[1,2,4,1,128,256]{5,4,1,3,0,2:T(8,128)(2,1)}), bf16[1,2,4,1,128,256]{5,4,1,3,0,2:T(8,128)(2,1)S(1)}, u32[]{:S(2)}, u32[]{:S(2)}) async-start(bf16[1,2,4,1,128,256]{5,4,1,3,0,2:T(8,128)(2,1)} %copy.89), calls=%async_computation | async-start | bytes 1048576 | tf_op jit(solution)/shard_map/all_to_all | solution.py:81
  24.7 0.7 fusion.43
  25.4 1.6 slice.42
  27.2 1.6 convolution_bitcast_fusion.3
  28.8 0.7 fusion.59
  29.5 1.8 fusion
  31.3 7.7 %all-to-all-done = bf16[1,2,4,1,128,256]{5,4,1,3,0,2:T(8,128)(2,1)S(1)} async-done(((bf16[1,2,4,1,128,256]{5,4,1,3,0,2:T(8,128)(2,1)}), bf16[1,2,4,1,128,256]{5,4,1,3,0,2:T(8,128)(2,1)S(1)}, u32[]{:S(2)}, u32[]{:S(2)}) %all-to-all-start) | async-done | bytes 524320 | tf_op jit(solution)/shard_map/all_to_all | solution.py:81
  39.1 1.6 fusion.8
  41.0 0.7 copy.95
  41.9 2.4 %convolution_bitcast_fusion.1 = f32[512,512]{1,0:T(8,128)} fusion(bf16[2,256,256]{2,1,0:T(8,128)(2,1)S(1)} %get-tuple-element.9, bf16[2,256,256]{2,1,0:T(8,128)(2,1)S(1)} %get-tuple-element.8, bf16[1,1,256,256]{3,2,1,0:T(8,128)(2,1)S(1)} %copy-done.7, bf16[1,2,256,256]{3,2,1,0:T(8,128)(2,1)} %param.7), kind=kOutput, calls=%fused_computation.9 | convolution fusion | flops 271056896 | bytes 1966080 | tf_op jit(solution)/shard_map/btsi,btso->io/dot_general | solution.py:97
  44.3 24.7 %all-gather.2.cloned.1.call-done = bf16[1,2,8,128,256]{4,3,1,0,2:T(8,128)(2,1)} async-done(((bf16[1,2,2,128,256]{4,3,1,0,2:T(8,128)(2,1)}), bf16[1,2,8,128,256]{4,3,1,0,2:T(8,128)(2,1)}) %all-gather.2.cloned.1.call-update) | async-done | bytes 1048592 | tf_op jit(solution)/shard_map/all_gather | solution.py:58
  69.0 2.1 convert_bitcast_fusion
  72.6 1.1 convolution_bitcast_fusion.4
  74.3 0.8 fusion.21
  75.1 131.5 %all-reduce.5.cloned.1.call-done = (f32[512,512]{1,0:T(8,128)}, f32[512,256]{1,0:T(8,128)}) async-done(((f32[512,512]{1,0:T(8,128)}, f32[512,256]{1,0:T(8,128)}), (f32[512,512]{1,0:T(8,128)}, f32[512,256]{1,0:T(8,128)})) %all-reduce.5.cloned.1.call-update) | async-done | bytes 1572880 | tf_op jit(solution)/shard_map/psum | solution.py:105
  206.6 2.3 %slice_multiply_fusion = (f32[512,256]{1,0:T(8,128)}, f32[512,256]{1,0:T(8,128)}) fusion(f32[512,512]{1,0:T(8,128)} %get-tuple-element.4), kind=kLoop, calls=%fused_computation.24 | loop fusion | flops 262144 | bytes 2097152 | tf_op jit(solution)/shard_map/mul | solution.py:109
  208.9 0.8 broadcast_multiply_fusion
  (60 shorter events, 4.5 us)
Async XLA Ops:
  7.2 3.8 %copy-start = (bf16[2,6,128,128]{3,2,1,0:T(8,128)(2,1)S(1)}, bf16[2,6,128,128]{3,2,1,0:T(8,128)(2,1)}, u32[]{:S(2)}) copy-start(bf16[2,6,128,128]{3,2,1,0:T(8,128)(2,1)} %param.13) | copy-start | bytes 1179652
  10.0 1.0 copy-start.1
  17.4 7.2 %copy-start.16 = (s32[8,6]{1,0:T(8,128)S(1)}, s32[8,6]{1,0:T(8,128)}, u32[]{:S(2)}) copy-start(s32[8,6]{1,0:T(8,128)} %param.12) | copy-start | bytes 580
  17.4 9.7 %copy-start.5 = (bf16[2,256,256]{2,1,0:T(8,128)(2,1)S(1)}, bf16[2,256,256]{2,1,0:T(8,128)(2,1)}, u32[]{:S(2)}) copy-start(bf16[2,256,256]{2,1,0:T(8,128)(2,1)} %param.10) | copy-start | bytes 786436
  17.4 9.6 %copy-start.6 = (bf16[2,256,256]{2,1,0:T(8,128)(2,1)S(1)}, bf16[2,256,256]{2,1,0:T(8,128)(2,1)}, u32[]{:S(2)}) copy-start(bf16[2,256,256]{2,1,0:T(8,128)(2,1)} %param.9) | copy-start | bytes 786436
  18.3 20.8 %all-to-all-start = ((bf16[1,2,4,1,128,256]{5,4,1,3,0,2:T(8,128)(2,1)}), bf16[1,2,4,1,128,256]{5,4,1,3,0,2:T(8,128)(2,1)S(1)}, u32[]{:S(2)}, u32[]{:S(2)}) async-start(bf16[1,2,4,1,128,256]{5,4,1,3,0,2:T(8,128)(2,1)} %copy.89), calls=%async_computation | async-start | bytes 1048576 | tf_op jit(solution)/shard_map/all_to_all | solution.py:81
  24.6 44.4 %all-gather.2.cloned.1.call-start = ((), (), s32[]{:S(2)}) async-start(), calls=%async_computation.1 | async-start | bytes 1310720 | tf_op jit(solution)/shard_map/all_gather | solution.py:58
  27.1 1.7 copy-start.8
  27.1 1.7 copy-start.10
  27.1 1.7 copy-start.12
  27.1 1.7 copy-start.14
  29.5 9.5 %copy-start.17 = (s32[4]{0:T(128)S(1)}, s32[4]{0:T(128)}, u32[]{:S(2)}) copy-start(s32[4]{0:T(128)} %get-tuple-element.6) | copy-start | bytes 52
  31.3 9.4 %copy-start.2 = (f32[1,2,256,512]{3,2,1,0:T(8,128)S(1)}, f32[1,2,256,512]{3,2,1,0:T(8,128)}, u32[]{:S(2)}) copy-start(f32[1,2,256,512]{3,2,1,0:T(8,128)} %copy-done.1) | copy-start | bytes 3145732
  40.7 1.1 copy-start.7
  41.8 164.8 %all-reduce.5.cloned.1.call-start = ((), (), s32[]{:S(2)}) async-start(), calls=%async_computation.2 | async-start | bytes 3145728 | tf_op jit(solution)/shard_map/psum | solution.py:105
  71.6 1.0 copy-start.3
  72.6 1.2 copy-start.9
  72.6 1.2 copy-start.11
  72.6 1.2 copy-start.13
  72.6 1.2 copy-start.15
  206.6 2.3 %copy-start.4 = (f32[512,256]{1,0:T(8,128)S(1)}, f32[512,256]{1,0:T(8,128)}, u32[]{:S(2)}) copy-start(f32[512,256]{1,0:T(8,128)} %get-tuple-element.5) | copy-start | bytes 1572868
Sparse Core Ops, SparseCore 0:
  41.9 27.0 all-gather.1
  74.9 131.6 all-reduce.4
where the time goes:
time: 217 us
  waiting for transfers between devices  164 us (76%)
  between operations  14.4 us (7%)
  matrix products  13.5 us (6%)
  local copies, waits for them, and re-layouts  12.4 us (6%)
  starting transfers between devices  6.36 us (3%)
  other arithmetic  6.03 us (3%)
    psum x1, waiting for transfers between devices, per_device(): conv_total, mix_total = lax.psum((conv_sum, mix_sum), ('dp', 'region'))  132 us
    all_gather x1, waiting for transfers between devices, per_device(): piece = lax.all_gather(tiled, 'region', axis=2, tiled=True)  24.7 us
    all_to_all x1, waiting for transfers between devices, per_device(): lax.all_to_all(outgoing_back, 'region', split_axis=2, concat_axis=2, tile...  7.73 us
    all_to_all x1, starting transfers between devices, per_device(): lax.all_to_all(outgoing_back, 'region', split_axis=2, concat_axis=2, tile...  6.32 us
  transfers between devices with their start and end apart: 3, of which 3 were waited for; matrix products, arithmetic and copies ran while one was open for 5% of the time, Pallas kernels for 0%

commit v1 on v0

v1 whole, which is shorter than its diff:
```python
import functools
import math

import jax
import jax.numpy as jnp
from jax import lax
from jax.experimental import pallas as pl
from jax.experimental.pallas import tpu as pltpu
from jax.sharding import PartitionSpec as P

TILE = 128
F32 = jnp.float32
BF16 = jnp.bfloat16
VM = pl.BlockSpec(memory_space=pltpu.VMEM)
SM = pl.BlockSpec(memory_space=pltpu.SMEM)


def dot(a, b, ca, cb):
    return lax.dot_general(a, b, (((ca,), (cb,)), ((), ())), preferred_element_type=F32)


def call(body, outs, n_smem, n_vmem, scratch=(), flops=0, nbytes=0, name=None):
    return pl.pallas_call(
        body,
        out_shape=outs,
        in_specs=[SM] * n_smem + [VM] * n_vmem,
        out_specs=[VM] * len(outs),
        scratch_shapes=list(scratch),
        cost_estimate=pl.CostEstimate(flops=flops, bytes_accessed=nbytes, transcendentals=0),
        compiler_params=pltpu.CompilerParams(vmem_limit_bytes=40 * 1024 * 1024),
        name=name,
    )


def find_entry(nb_ref, source, target, tiles, per_tile):
    tile = jnp.int32(0)
    place = jnp.int32(0)
    named = jnp.int32(-1)
    for j in range(tiles):
        for k in range(per_tile):
            local = nb_ref[source * tiles + j, k] - target * tiles
            hit = jnp.logical_and(local >= 0, local < tiles)
            tile = jnp.where(hit, j, tile)
            place = jnp.where(hit, k, place)
            named = jnp.where(hit, local, named)
    return tile, place, named


def outgoing_body(regions, ids_ref, nb_ref, cot_ref, adj_ref, *out_refs):
    me = ids_ref[0]
    tiles, per_tile = adj_ref.shape[:2]
    for s in range(1, regions):
        other = lax.rem(me + s, regions)
        tile, place, named = find_entry(nb_ref, me, other, tiles, per_tile)
        out = out_refs[s - 1]

        @pl.when(named >= 0)
        def _():
            weights = adj_ref[tile, place]
            for t in range(cot_ref.shape[0]):
                rows = cot_ref[t, pl.ds(pl.multiple_of(tile * TILE, TILE), TILE), :]
                out[t] = dot(weights, rows, 0, 0).astype(BF16)

        @pl.when(named < 0)
        def _():
            out[...] = jnp.zeros_like(out)


def local_body(
    steps, ids_ref, nb_ref, x_ref, cot_ref, wf_ref, wg_ref, wm_ref, adj_ref,
    hidden_ref, df_ref, dg_ref, direct_ref, local_ref, mix_ref,
):
    me = ids_ref[0]
    tiles, per_tile = adj_ref.shape[:2]
    total = cot_ref.shape[0]
    mix = jnp.zeros(mix_ref.shape, F32)
    for t in range(total):
        x = x_ref[t]
        act_f = dot(x, wf_ref[0], 1, 0)
        act_g = dot(x, wg_ref[0], 1, 0)
        if t % steps:
            before = x_ref[t - 1]
            act_f += dot(before, wf_ref[1], 1, 0)
            act_g += dot(before, wg_ref[1], 1, 0)
        filt = jnp.tanh(act_f)
        gate = jax.nn.sigmoid(act_g)
        both = filt * gate
        hidden = both.astype(BF16)
        hidden_ref[t] = hidden
        df_ref[t] = gate * (1.0 - filt * filt)
        dg_ref[t] = both * (1.0 - gate)
        cot = cot_ref[t]
        direct_ref[t] = dot(cot, wm_ref[0], 1, 1)
        mix += dot(hidden, cot, 0, 0)
    mix_ref[...] = mix
    local_ref[...] = jnp.zeros_like(local_ref)
    for j in range(tiles):
        for k in range(per_tile):
            local = nb_ref[me * tiles + j, k] - me * tiles

            @pl.when(jnp.logical_and(local >= 0, local < tiles))
            def _():
                place = pl.ds(pl.multiple_of(local * TILE, TILE), TILE)
                for t in range(total):
                    local_ref[t, place, :] += dot(adj_ref[j, k], cot_ref[t, j * TILE : (j + 1) * TILE, :], 0, 0)


def gradient_body(
    regions, steps, per_tile, ids_ref, nb_ref, x_ref, hidden_ref, df_ref, dg_ref, direct_ref, local_ref, mix_ref, wm_ref, *refs
):
    arrived, (act_ref, keep_ref, send_ref), (sums, parts) = refs[: regions - 1], refs[regions - 1 : -2], refs[-2:]
    me, core = ids_ref[0], ids_ref[1]
    total, sites, chans = x_ref.shape
    tiles = sites // TILE
    sums[...] = local_ref[...]
    for s in range(1, regions):
        source = lax.rem(me - s + regions, regions)
        _, _, named = find_entry(nb_ref, source, me, tiles, per_tile)

        @pl.when(named >= 0)
        def _():
            place = pl.ds(pl.multiple_of(named * TILE, TILE), TILE)
            for t in range(total):
                sums[t, place, :] += arrived[s - 1][t].astype(F32)

    zero = jnp.zeros((chans, chans), F32)
    conv = [[zero, zero], [zero, zero]]
    mix = zero
    for t in range(total):
        summed = sums[t].astype(BF16)
        mix += dot(hidden_ref[t], summed, 0, 0)
        grad = direct_ref[t] + dot(summed, wm_ref[1], 1, 1)
        for part, factor in enumerate((df_ref, dg_ref)):
            act = (grad * factor[t]).astype(BF16)
            act_ref[part, t] = act
            conv[part][0] += dot(x_ref[t], act, 0, 0)
            if t % steps:
                conv[part][1] += dot(x_ref[t - 1], act, 0, 0)
    for tap in range(2):
        parts[tap, 0] = conv[0][tap]
        parts[tap, 1] = conv[1][tap]
    parts[0, 2] = mix_ref[...]
    parts[1, 2] = mix
    keep_ref[...] = parts[core]
    send_ref[...] = parts[1 - core].astype(BF16)


def inputs_body(steps, cot_ref, act_ref, wf_ref, wg_ref, out_ref):
    total = cot_ref.shape[0]
    for t in range(total):
        grad = cot_ref[t].astype(F32)
        grad += dot(act_ref[0, t], wf_ref[0], 1, 1) + dot(act_ref[1, t], wg_ref[0], 1, 1)
        if (t + 1) % steps:
            grad += dot(act_ref[0, t + 1], wf_ref[1], 1, 1) + dot(act_ref[1, t + 1], wg_ref[1], 1, 1)
        out_ref[t] = grad.astype(BF16)


def split_body(chips, ids_ref, keep_ref, got_ref, own_ref, *rest):
    sends, both = rest[:-1], rest[-1]
    chip = ids_ref[2]
    rows = own_ref.shape[1]
    both[...] = keep_ref[...] + got_ref[...].astype(F32)
    own_ref[...] = both[:, pl.ds(pl.multiple_of(chip * rows, rows), rows), :]
    for p in range(1, chips):
        other = partner(chip, p, chips)
        sends[p - 1][...] = both[:, pl.ds(pl.multiple_of(other * rows, rows), rows), :].astype(BF16)


def add_body(own_ref, *refs):
    total = own_ref[...]
    for got in refs[:-1]:
        total += got[...].astype(F32)
    refs[-1][...] = total.astype(BF16)


def region_sum_body(regions, ids_ref, own_ref, *refs):
    gots, out_ref, slots = refs[: regions - 1], refs[-2], refs[-1]
    me = ids_ref[0]
    slots[me] = own_ref[...]
    for s in range(1, regions):
        slots[lax.rem(me - s + regions, regions)] = gots[s - 1][...]
    total = slots[0].astype(F32)
    for r in range(1, regions):
        total += slots[r].astype(F32)
    out_ref[...] = total.astype(BF16)


def scale_body(chips, factor, ids_ref, *refs):
    chunks, outs = refs[: 2 * chips], refs[2 * chips :]
    core, chip = ids_ref[1], ids_ref[2]
    rows = chunks[0].shape[1]
    for c in range(2):
        tap = core if c == 0 else 1 - core
        for p in range(chips):
            other = partner(chip, p, chips)
            place = pl.ds(pl.multiple_of(other * rows, rows), rows)
            for a in range(3):
                outs[a][tap, place, :] = chunks[c * chips + p][a].astype(F32) * factor


def partner(chip, p, chips):
    return jnp.bitwise_xor(chip, p)


def chip_pairs(chips, p):
    return [(2 * c + b, 2 * (c ^ p) + b) for c in range(chips) for b in range(2)]


def per_device(inputs, cotangent, w_filter, w_gate, w_mix, neighbours, adjacency):
    regions = lax.axis_size("region")
    dp = lax.axis_size("dp")
    chips = dp // 2
    region = lax.axis_index("region").astype(jnp.int32)
    place = lax.axis_index("dp").astype(jnp.int32)
    ids = jnp.stack([region, place % 2, place // 2])
    windows, steps, sites, chans = inputs.shape
    total = windows * steps
    per_tile = neighbours.shape[1]
    x = inputs.reshape(total, sites, chans)
    cot = cotangent.reshape(total, sites, chans)
    shape = jax.ShapeDtypeStruct
    block = total * sites * chans

    outgoing = call(
        functools.partial(outgoing_body, regions),
        [shape((total, TILE, chans), BF16)] * (regions - 1), 2, 2, name="outgoing",
        flops=2 * (regions - 1) * total * TILE * TILE * chans, nbytes=4 * block,
    )(ids, neighbours, cot, adjacency)
    arrived = [
        lax.ppermute(part, "region", [(r, (r + s) % regions) for r in range(regions)])
        for s, part in enumerate(outgoing, 1)
    ]
    hidden, d_filter, d_gate, direct, local, mix = call(
        functools.partial(local_body, steps),
        [shape(x.shape, BF16)] + [shape(x.shape, F32)] * 4 + [shape((chans, chans), F32)], 2, 6, name="local",
        flops=14 * block * chans, nbytes=30 * block,
    )(ids, neighbours, x, cot, w_filter, w_gate, w_mix, adjacency)
    act_cot, keep, send = call(
        functools.partial(gradient_body, regions, steps, per_tile),
        [shape((2,) + x.shape, BF16), shape((3, chans, chans), F32), shape((3, chans, chans), BF16)],
        2, 8 + regions - 1, name="gradient",
        scratch=[pltpu.VMEM(x.shape, F32), pltpu.VMEM((2, 3, chans, chans), F32)],
        flops=10 * block * chans, nbytes=30 * block,
    )(ids, neighbours, x, hidden, d_filter, d_gate, direct, local, mix, w_mix, *arrived)
    (grad_inputs,) = call(
        functools.partial(inputs_body, steps), [shape(x.shape, BF16)], 0, 4, name="inputs",
        flops=8 * block * chans, nbytes=16 * block,
    )(cot, act_cot, w_filter, w_gate)

    rows = chans // chips
    chunk = (3, rows, chans)
    got = lax.ppermute(send, "dp", [(i, i ^ 1) for i in range(dp)])
    own, *sends = call(
        functools.partial(split_body, chips), [shape(chunk, F32)] + [shape(chunk, BF16)] * (chips - 1), 1, 2,
        scratch=[pltpu.VMEM((3, chans, chans), F32)], name="split",
    )(ids, keep, got)
    gots = [lax.ppermute(part, "dp", chip_pairs(chips, p)) for p, part in enumerate(sends, 1)]
    (mine,) = call(add_body, [shape(chunk, BF16)], 0, chips, name="add")(own, *gots)
    gots = [lax.ppermute(mine, "region", [(r, (r + s) % regions) for r in range(regions)]) for s in range(1, regions)]
    (done,) = call(
        functools.partial(region_sum_body, regions), [shape(chunk, BF16)], 1, regions,
        scratch=[pltpu.VMEM((regions,) + chunk, BF16)], name="region_sum",
    )(ids, mine, *gots)
    chunks = [done] + [lax.ppermute(done, "dp", chip_pairs(chips, p)) for p in range(1, chips)]
    chunks += [lax.ppermute(part, "dp", [(i, i ^ 1) for i in range(dp)]) for part in chunks]
    factor = 1.0 / math.sqrt(windows * dp * steps * sites * regions)
    grads = call(
        functools.partial(scale_body, chips, factor), [shape((2, chans, chans), F32)] * 3, 1, 2 * chips, name="scale"
    )(ids, *chunks)
    return (grad_inputs.reshape(inputs.shape), *grads)


def solution(mesh):
    return jax.shard_map(
        per_device,
        mesh=mesh,
        in_specs=(
            P("dp", None, "region", None),
            P("dp", None, "region", None),
            P(),
            P(),
            P(),
            P(),
            P("region", None, None, None),
        ),
        out_specs=(P("dp", None, "region", None), P(), P(), P()),
        check_vma=False,
    )
```

time: 217 us -> 55.9 us (0.26)
  waiting for transfers between devices: 164 us -> 18.7 us
  between operations: 14.4 us -> 0.75 us
  matrix products: 13.5 us -> 0 us
  starting transfers between devices: 6.36 us -> 19.3 us
  Pallas kernels: 0 us -> 10.4 us
  local copies, waits for them, and re-layouts: 12.4 us -> 6.36 us
  other arithmetic: 6.03 us -> 0.08 us
    psum x1 -> x0, waiting for transfers between devices: 132 us -> none  [per_device(): conv_total, mix_total = lax.psum((conv_sum, mix_sum), ('dp', 'region'))]
    all_gather x1 -> x0, waiting for transfers between devices: 24.7 us -> none  [per_device(): piece = lax.all_gather(tiled, 'region', axis=2, tiled=True)]
    ppermute x0 -> x17, starting transfers between devices: none -> 19.3 us  [the longest x3 7.02 us: per_device(): lax.ppermute(part, 'region', [(r, (r + s) % regions) for r in range(regio...]
    ppermute x0 -> x17, waiting for transfers between devices: none -> 18.7 us  [the longest x3 7.35 us: per_device(): lax.ppermute(mine, 'region', [(r, (r + s) % regions) for r in range(regio...]
    dot_general x10 -> x0, matrix products: 13.5 us -> none  [the longest x1 2.4 us: per_device(): jnp.einsum('btsi,btso->io', joint, act_cot, preferred_element_type=jnp.fl...]
    pallas_call x0 -> x8, Pallas kernels: none -> 10.4 us  [the longest x1 3.26 us: per_device(): call(functools.partial(local_body, steps), [shape(x.shape, BF16)] + [shap...]
    all_to_all x1 -> x0, waiting for transfers between devices: 7.73 us -> none  [per_device(): lax.all_to_all(outgoing_back, 'region', split_axis=2, concat_axis=2, tile...]
    all_to_all x1 -> x0, starting transfers between devices: 6.32 us -> none  [per_device(): lax.all_to_all(outgoing_back, 'region', split_axis=2, concat_axis=2, tile...]
  transfers between devices with their start and end apart: 3 -> 17, of which waited for: 3 -> 11; matrix products, arithmetic and copies ran while one was open for 5% -> 0% of each run, Pallas kernels for 0% -> 8%
where the time goes in v1:
time: 55.9 us; the launch traced here: 55.6 us
  starting transfers between devices  19.3 us (35%)
  waiting for transfers between devices  18.7 us (33%)
  Pallas kernels  10.4 us (19%)
  local copies, waits for them, and re-layouts  6.36 us (11%)
  between operations  0.75 us (1%)
    ppermute x3, waiting for transfers between devices, per_device(): lax.ppermute(mine, 'region', [(r, (r + s) % regions) for r in range(regio...  7.35 us
    ppermute x3, starting transfers between devices, per_device(): lax.ppermute(part, 'region', [(r, (r + s) % regions) for r in range(regio...  7.02 us
    unnamed x20, local copies, waits for them, and re-layouts  6.36 us
    ppermute x3, waiting for transfers between devices, per_device(): lax.ppermute(part, 'dp', chip_pairs(chips, p))  5.04 us
    ppermute x3, starting transfers between devices, per_device(): lax.ppermute(mine, 'region', [(r, (r + s) % regions) for r in range(regio...  5.03 us
    ppermute x3, waiting for transfers between devices, per_device(): lax.ppermute(done, 'dp', chip_pairs(chips, p))  4.18 us
    ppermute x3, starting transfers between devices, per_device(): lax.ppermute(done, 'dp', chip_pairs(chips, p))  3.55 us
    ppermute x3, starting transfers between devices, per_device(): lax.ppermute(part, 'dp', chip_pairs(chips, p))  3.55 us
  transfers between devices with their start and end apart: 17, of which 11 were waited for; matrix products, arithmetic and copies ran while one was open for 0% of the time, Pallas kernels for 8%

profile of v1, /device:TPU:0, one launch (start us, length us, event | category | flops | bytes accessed | tf_op | source)
XLA Modules:
  0.0 55.6 jit_solution(3270016951391625094)
XLA Ops:
  1.3 0.9 %copy-done = bf16[1,2,256,256]{3,2,1,0:T(8,128)(2,1)S(1)} copy-done((bf16[1,2,256,256]{3,2,1,0:T(8,128)(2,1)S(1)}, bf16[1,2,256,256]{3,2,1,0:T(8,128)(2,1)}, u32[]{:S(2)}) %copy-start) | copy-done | bytes 262168
  2.3 1.0 %copy-done.2 = bf16[2,6,128,128]{3,2,1,0:T(8,128)(2,1)S(1)} copy-done((bf16[2,6,128,128]{3,2,1,0:T(8,128)(2,1)S(1)}, bf16[2,6,128,128]{3,2,1,0:T(8,128)(2,1)}, u32[]{:S(2)}) %copy-start.2) | copy-done | bytes 393240
  3.3 1.3 %outgoing.1 = (bf16[2,128,256]{2,1,0:T(8,128)(2,1)S(1)}, bf16[2,128,256]{2,1,0:T(8,128)(2,1)S(1)}, bf16[2,128,256]{2,1,0:T(8,128)(2,1)S(1)}) custom-call(s32[3]{0:T(128)S(1)} %pad_add_fusion.ids_ref, s32[8,6]{1,0:T(8,128)S(1)} %copy-done.9, bf16[2,256,256]{2,1,0:T(8,128)(2,1)S(1)} %bitcast.6, bf16[2,6,128,128]{3,2,1,0:T(8,128)(2,1)S(1)} %copy-done.2), custom_call_target="tpu_custom_call" | custom-call | flops 50331648 | bytes 524288 | tf_op jit(solution)/shard_map/outgoing/pallas_call | solution.py:224
  4.6 3.1 %collective-permute-start = (bf16[2,128,256]{2,1,0:T(8,128)(2,1)S(1)}, bf16[2,128,256]{2,1,0:T(8,128)(2,1)S(1)}, u32[]{:S(2)}, u32[]{:S(2)}) collective-permute-start(bf16[2,128,256]{2,1,0:T(8,128)(2,1)S(1)} %get-tuple-element.29), channel_id=1, source_target_pairs={{0,1},{1,2},{2,3},{3,0},{4,5},{5,6},{6,7},{7,4},{8,9},{9,10},{10,1... | collective-permute-start | bytes 393224 | tf_op jit(solution)/shard_map/ppermute | solution.py:230
  7.7 2.6 %collective-permute-start.1 = (bf16[2,128,256]{2,1,0:T(8,128)(2,1)S(1)}, bf16[2,128,256]{2,1,0:T(8,128)(2,1)S(1)}, u32[]{:S(2)}, u32[]{:S(2)}) collective-permute-start(bf16[2,128,256]{2,1,0:T(8,128)(2,1)S(1)} %get-tuple-element.30), channel_id=1, source_target_pairs={{0,2},{1,3},{2,0},{3,1},{4,6},{5,7},{6,4},{7,5},{8,10},{9,11},{10,... | collective-permute-start | bytes 393224 | tf_op jit(solution)/shard_map/ppermute | solution.py:230
  10.3 1.4 %collective-permute-start.2 = (bf16[2,128,256]{2,1,0:T(8,128)(2,1)S(1)}, bf16[2,128,256]{2,1,0:T(8,128)(2,1)S(1)}, u32[]{:S(2)}, u32[]{:S(2)}) collective-permute-start(bf16[2,128,256]{2,1,0:T(8,128)(2,1)S(1)} %get-tuple-element.31), channel_id=1, source_target_pairs={{0,3},{1,0},{2,1},{3,2},{4,7},{5,4},{6,5},{7,6},{8,11},{9,8},{10,9... | collective-permute-start | bytes 393224 | tf_op jit(solution)/shard_map/ppermute | solution.py:230
  11.6 0.9 %copy-done.4 = bf16[1,2,256,256]{3,2,1,0:T(8,128)(2,1)S(1)} copy-done((bf16[1,2,256,256]{3,2,1,0:T(8,128)(2,1)S(1)}, bf16[1,2,256,256]{3,2,1,0:T(8,128)(2,1)}, u32[]{:S(2)}) %copy-start.4) | copy-done | bytes 262168
  12.6 0.9 %copy-done.5 = bf16[2,256,256]{2,1,0:T(8,128)(2,1)S(1)} copy-done((bf16[2,256,256]{2,1,0:T(8,128)(2,1)S(1)}, bf16[2,256,256]{2,1,0:T(8,128)(2,1)}, u32[]{:S(2)}) %copy-start.5) | copy-done | bytes 262168
  15.4 3.3 %local.1 = (bf16[2,256,256]{2,1,0:T(8,128)(2,1)S(1)}, f32[2,256,256]{2,1,0:T(8,128)S(1)}, f32[2,256,256]{2,1,0:T(8,128)S(1)}, f32[2,256,256]{2,1,0:T(8,128)S(1)}...) custom-call(s32[3]{0:T(128)S(1)} %pad_add_fusion.ids_ref, s32[8,6]{1,0:T(8,128)S(1)} %copy-done.9, ...), custom_call_target="tpu_custom_call" | custom-call | flops 469762048 | bytes 3932160 | tf_op jit(solution)/shard_map/local/pallas_call | solution.py:233
  18.9 1.6 %gradient.1 = (bf16[2,2,256,256]{3,2,1,0:T(8,128)(2,1)S(1)}, f32[3,256,256]{2,1,0:T(8,128)S(1)}, bf16[3,256,256]{2,1,0:T(8,128)(2,1)S(1)}) custom-call(s32[3]{0:T(128)S(1)} %pad_add_fusion.ids_ref, s32[8,6]{1,0:T(8,128)S(1)} %copy-done.9, bf16[2,256,256]{2,1,0:T(8,128)(2,1)S(1)} %bitcast.10, bf16[2,256,256]{2,1,0:T(8,128)(2,1)S(1)} %get-tuple-element.23.hidden_ref, ...), custom_call_target="tpu_custom_call" | custom-call | flops 335544320 | bytes 3932160 | tf_op jit(solution)/shard_map/gradient/pallas_call | solution.py:238
  20.6 1.7 %collective-permute-done.3.got_ref = bf16[3,256,256]{2,1,0:T(8,128)(2,1)S(1)} collective-permute-done((bf16[3,256,256]{2,1,0:T(8,128)(2,1)S(1)}, bf16[3,256,256]{2,1,0:T(8,128)(2,1)S(1)}, u32[]{:S(2)}, u32[]{:S(2)}) %collective-permute-start.3) | collective-permute-done | bytes 393248 | tf_op jit(solution)/shard_map/ppermute | solution.py:252
  23.0 1.6 %collective-permute-start.4 = (bf16[3,64,256]{2,1,0:T(8,128)(2,1)S(1)}, bf16[3,64,256]{2,1,0:T(8,128)(2,1)S(1)}, u32[]{:S(2)}, u32[]{:S(2)}) collective-permute-start(bf16[3,64,256]{2,1,0:T(8,128)(2,1)S(1)} %get-tuple-element.36), channel_id=1, source_target_pairs={{0,8},{4,12},{8,0},{12,4},{16,24},{20,28},{24,16},{28,20},{1,9},{5... | collective-permute-start | bytes 294920 | tf_op jit(solution)/shard_map/ppermute | solution.py:257
  24.5 1.5 %collective-permute-start.5 = (bf16[3,64,256]{2,1,0:T(8,128)(2,1)S(1)}, bf16[3,64,256]{2,1,0:T(8,128)(2,1)S(1)}, u32[]{:S(2)}, u32[]{:S(2)}) collective-permute-start(bf16[3,64,256]{2,1,0:T(8,128)(2,1)S(1)} %get-tuple-element.37), channel_id=1, source_target_pairs={{0,16},{4,20},{8,24},{12,28},{16,0},{20,4},{24,8},{28,12},{1,17},{... | collective-permute-start | bytes 294920 | tf_op jit(solution)/shard_map/ppermute | solution.py:257
  26.5 1.3 %collective-permute-done.4.refs_0_ = bf16[3,64,256]{2,1,0:T(8,128)(2,1)S(1)} collective-permute-done((bf16[3,64,256]{2,1,0:T(8,128)(2,1)S(1)}, bf16[3,64,256]{2,1,0:T(8,128)(2,1)S(1)}, u32[]{:S(2)}, u32[]{:S(2)}) %collective-permute-start.4) | collective-permute-done | bytes 98336 | tf_op jit(solution)/shard_map/ppermute | solution.py:257
  27.9 2.4 %collective-permute-done.5.refs_1_ = bf16[3,64,256]{2,1,0:T(8,128)(2,1)S(1)} collective-permute-done((bf16[3,64,256]{2,1,0:T(8,128)(2,1)S(1)}, bf16[3,64,256]{2,1,0:T(8,128)(2,1)S(1)}, u32[]{:S(2)}, u32[]{:S(2)}) %collective-permute-start.5) | collective-permute-done | bytes 98336 | tf_op jit(solution)/shard_map/ppermute | solution.py:257
  30.3 1.3 %collective-permute-done.6.refs_2_ = bf16[3,64,256]{2,1,0:T(8,128)(2,1)S(1)} collective-permute-done((bf16[3,64,256]{2,1,0:T(8,128)(2,1)S(1)}, bf16[3,64,256]{2,1,0:T(8,128)(2,1)S(1)}, u32[]{:S(2)}, u32[]{:S(2)}) %collective-permute-start.6) | collective-permute-done | bytes 98336 | tf_op jit(solution)/shard_map/ppermute | solution.py:257
  31.6 4.4 %collective-permute-start.9 = (bf16[3,64,256]{2,1,0:T(8,128)(2,1)S(1)}, bf16[3,64,256]{2,1,0:T(8,128)(2,1)S(1)}, u32[]{:S(2)}, u32[]{:S(2)}) collective-permute-start(bf16[3,64,256]{2,1,0:T(8,128)(2,1)S(1)} %add.11.own_ref), channel_id=1, source_target_pairs={{0,3},{1,0},{2,1},{3,2},{4,7},{5,4},{6,5},{7,6},{8,11},{9,8},{10,9... | collective-permute-start | bytes 294920 | tf_op jit(solution)/shard_map/ppermute | solution.py:259
  36.7 2.2 %collective-permute-done.9.refs_2_ = bf16[3,64,256]{2,1,0:T(8,128)(2,1)S(1)} collective-permute-done((bf16[3,64,256]{2,1,0:T(8,128)(2,1)S(1)}, bf16[3,64,256]{2,1,0:T(8,128)(2,1)S(1)}, u32[]{:S(2)}, u32[]{:S(2)}) %collective-permute-start.9) | collective-permute-done | bytes 98336 | tf_op jit(solution)/shard_map/ppermute | solution.py:259
  38.8 5.2 %collective-permute-done.8.refs_1_ = bf16[3,64,256]{2,1,0:T(8,128)(2,1)S(1)} collective-permute-done((bf16[3,64,256]{2,1,0:T(8,128)(2,1)S(1)}, bf16[3,64,256]{2,1,0:T(8,128)(2,1)S(1)}, u32[]{:S(2)}, u32[]{:S(2)}) %collective-permute-start.8) | collective-permute-done | bytes 98336 | tf_op jit(solution)/shard_map/ppermute | solution.py:259
  44.7 1.7 %collective-permute-start.12 = (bf16[3,64,256]{2,1,0:T(8,128)(2,1)S(1)}, bf16[3,64,256]{2,1,0:T(8,128)(2,1)S(1)}, u32[]{:S(2)}, u32[]{:S(2)}) collective-permute-start(bf16[3,64,256]{2,1,0:T(8,128)(2,1)S(1)} %region_sum.1.refs_0_), channel_id=1, source_target_pairs={{0,24},{4,28},{8,16},{12,20},{16,8},{20,12},{24,0},{28,4},{1,25},{... | collective-permute-start | bytes 294920 | tf_op jit(solution)/shard_map/ppermute | solution.py:264
  46.4 1.5 %collective-permute-start.11 = (bf16[3,64,256]{2,1,0:T(8,128)(2,1)S(1)}, bf16[3,64,256]{2,1,0:T(8,128)(2,1)S(1)}, u32[]{:S(2)}, u32[]{:S(2)}) collective-permute-start(bf16[3,64,256]{2,1,0:T(8,128)(2,1)S(1)} %region_sum.1.refs_0_), channel_id=1, source_target_pairs={{0,16},{4,20},{8,24},{12,28},{16,0},{20,4},{24,8},{28,12},{1,17},{... | collective-permute-start | bytes 294920 | tf_op jit(solution)/shard_map/ppermute | solution.py:264
  48.2 3.1 %collective-permute-done.12.refs_3_ = bf16[3,64,256]{2,1,0:T(8,128)(2,1)S(1)} collective-permute-done((bf16[3,64,256]{2,1,0:T(8,128)(2,1)S(1)}, bf16[3,64,256]{2,1,0:T(8,128)(2,1)S(1)}, u32[]{:S(2)}, u32[]{:S(2)}) %collective-permute-start.12) | collective-permute-done | bytes 98336 | tf_op jit(solution)/shard_map/ppermute | solution.py:264
  52.5 1.1 %inputs.1 = bf16[2,256,256]{2,1,0:T(8,128)(2,1)} custom-call(bf16[2,256,256]{2,1,0:T(8,128)(2,1)S(1)} %bitcast.8, bf16[2,2,256,256]{3,2,1,0:T(8,128)(2,1)S(1)} %get-tuple-element.32.act_ref, bf16[2,256,256]{2,1,0:T(8,128)(2,1)S(1)} %copy-done.7, bf16[2,256,256]{2,1,0:T(8,128)(2,1)S(1)} %copy-done.8), custom_call_target="tpu_custom_call" | custom-call | flops 268435456 | bytes 2097152 | tf_op jit(solution)/shard_map/inputs/pallas_call | solution.py:245
  53.8 1.8 %scale.1 = (f32[2,256,256]{2,1,0:T(8,128)}, f32[2,256,256]{2,1,0:T(8,128)}, f32[2,256,256]{2,1,0:T(8,128)}) custom-call(s32[3]{0:T(128)S(1)} %pad_add_fusion.ids_ref, bf16[3,64,256]{2,1,0:T(8,128)(2,1)S(1)} %region_sum.1.refs_0_, bf16[3,64,256]{2,1,0:T(8,128)(2,1)S(1)} %collective-permute-done.10.refs_1_, ...), custom_call_target="tpu_custom_call" | custom-call | tf_op jit(solution)/shard_map/scale/pallas_call | solution.py:267
  (39 shorter events, 7.1 us)
Async XLA Ops:
  1.3 0.9 %copy-start = (bf16[1,2,256,256]{3,2,1,0:T(8,128)(2,1)S(1)}, bf16[1,2,256,256]{3,2,1,0:T(8,128)(2,1)}, u32[]{:S(2)}) copy-start(bf16[1,2,256,256]{3,2,1,0:T(8,128)(2,1)} %param.8) | copy-start | bytes 786436
  2.3 1.0 %copy-start.2 = (bf16[2,6,128,128]{3,2,1,0:T(8,128)(2,1)S(1)}, bf16[2,6,128,128]{3,2,1,0:T(8,128)(2,1)}, u32[]{:S(2)}) copy-start(bf16[2,6,128,128]{3,2,1,0:T(8,128)(2,1)} %adj_ref.3) | copy-start | bytes 1179652
  3.3 8.4 %copy-start.1 = (bf16[1,2,256,256]{3,2,1,0:T(8,128)(2,1)S(1)}, bf16[1,2,256,256]{3,2,1,0:T(8,128)(2,1)}, u32[]{:S(2)}) copy-start(bf16[1,2,256,256]{3,2,1,0:T(8,128)(2,1)} %param.8) | copy-start | bytes 786436
  3.3 8.4 %copy-start.3 = (bf16[2,6,128,128]{3,2,1,0:T(8,128)(2,1)S(1)}, bf16[2,6,128,128]{3,2,1,0:T(8,128)(2,1)}, u32[]{:S(2)}) copy-start(bf16[2,6,128,128]{3,2,1,0:T(8,128)(2,1)} %adj_ref.3) | copy-start | bytes 1179652
  4.6 14.1 %collective-permute-start = (bf16[2,128,256]{2,1,0:T(8,128)(2,1)S(1)}, bf16[2,128,256]{2,1,0:T(8,128)(2,1)S(1)}, u32[]{:S(2)}, u32[]{:S(2)}) collective-permute-start(bf16[2,128,256]{2,1,0:T(8,128)(2,1)S(1)} %get-tuple-element.29), channel_id=1, source_target_pairs={{0,1},{1,2},{2,3},{3,0},{4,5},{5,6},{6,7},{7,4},{8,9},{9,10},{10,1... | collective-permute-start | bytes 393224 | tf_op jit(solution)/shard_map/ppermute | solution.py:230
  7.7 11.2 %collective-permute-start.1 = (bf16[2,128,256]{2,1,0:T(8,128)(2,1)S(1)}, bf16[2,128,256]{2,1,0:T(8,128)(2,1)S(1)}, u32[]{:S(2)}, u32[]{:S(2)}) collective-permute-start(bf16[2,128,256]{2,1,0:T(8,128)(2,1)S(1)} %get-tuple-element.30), channel_id=1, source_target_pairs={{0,2},{1,3},{2,0},{3,1},{4,6},{5,7},{6,4},{7,5},{8,10},{9,11},{10,... | collective-permute-start | bytes 393224 | tf_op jit(solution)/shard_map/ppermute | solution.py:230
  10.3 8.6 %collective-permute-start.2 = (bf16[2,128,256]{2,1,0:T(8,128)(2,1)S(1)}, bf16[2,128,256]{2,1,0:T(8,128)(2,1)S(1)}, u32[]{:S(2)}, u32[]{:S(2)}) collective-permute-start(bf16[2,128,256]{2,1,0:T(8,128)(2,1)S(1)} %get-tuple-element.31), channel_id=1, source_target_pairs={{0,3},{1,0},{2,1},{3,2},{4,7},{5,4},{6,5},{7,6},{8,11},{9,8},{10,9... | collective-permute-start | bytes 393224 | tf_op jit(solution)/shard_map/ppermute | solution.py:230
  11.6 1.0 %copy-start.4 = (bf16[1,2,256,256]{3,2,1,0:T(8,128)(2,1)S(1)}, bf16[1,2,256,256]{3,2,1,0:T(8,128)(2,1)}, u32[]{:S(2)}) copy-start(bf16[1,2,256,256]{3,2,1,0:T(8,128)(2,1)} %param.7) | copy-start | bytes 786436
  12.6 0.9 %copy-start.5 = (bf16[2,256,256]{2,1,0:T(8,128)(2,1)S(1)}, bf16[2,256,256]{2,1,0:T(8,128)(2,1)}, u32[]{:S(2)}) copy-start(bf16[2,256,256]{2,1,0:T(8,128)(2,1)} %wm_ref.3) | copy-start | bytes 786436
  20.5 1.8 %collective-permute-start.3 = (bf16[3,256,256]{2,1,0:T(8,128)(2,1)S(1)}, bf16[3,256,256]{2,1,0:T(8,128)(2,1)S(1)}, u32[]{:S(2)}, u32[]{:S(2)}) collective-permute-start(bf16[3,256,256]{2,1,0:T(8,128)(2,1)S(1)} %get-tuple-element.34), channel_id=1, source_target_pairs={{0,4},{4,0},{8,12},{12,8},{16,20},{20,16},{24,28},{28,24},{1,5},{5... | collective-permute-start | bytes 1179656 | tf_op jit(solution)/shard_map/ppermute | solution.py:252
  23.0 4.9 %collective-permute-start.4 = (bf16[3,64,256]{2,1,0:T(8,128)(2,1)S(1)}, bf16[3,64,256]{2,1,0:T(8,128)(2,1)S(1)}, u32[]{:S(2)}, u32[]{:S(2)}) collective-permute-start(bf16[3,64,256]{2,1,0:T(8,128)(2,1)S(1)} %get-tuple-element.36), channel_id=1, source_target_pairs={{0,8},{4,12},{8,0},{12,4},{16,24},{20,28},{24,16},{28,20},{1,9},{5... | collective-permute-start | bytes 294920 | tf_op jit(solution)/shard_map/ppermute | solution.py:257
  24.5 5.8 %collective-permute-start.5 = (bf16[3,64,256]{2,1,0:T(8,128)(2,1)S(1)}, bf16[3,64,256]{2,1,0:T(8,128)(2,1)S(1)}, u32[]{:S(2)}, u32[]{:S(2)}) collective-permute-start(bf16[3,64,256]{2,1,0:T(8,128)(2,1)S(1)} %get-tuple-element.37), channel_id=1, source_target_pairs={{0,16},{4,20},{8,24},{12,28},{16,0},{20,4},{24,8},{28,12},{1,17},{... | collective-permute-start | bytes 294920 | tf_op jit(solution)/shard_map/ppermute | solution.py:257
  26.1 5.5 %collective-permute-start.6 = (bf16[3,64,256]{2,1,0:T(8,128)(2,1)S(1)}, bf16[3,64,256]{2,1,0:T(8,128)(2,1)S(1)}, u32[]{:S(2)}, u32[]{:S(2)}) collective-permute-start(bf16[3,64,256]{2,1,0:T(8,128)(2,1)S(1)} %get-tuple-element.38), channel_id=1, source_target_pairs={{0,24},{4,28},{8,16},{12,20},{16,8},{20,12},{24,0},{28,4},{1,25},{... | collective-permute-start | bytes 294920 | tf_op jit(solution)/shard_map/ppermute | solution.py:257
  31.6 20.9 %copy-start.7 = (bf16[2,256,256]{2,1,0:T(8,128)(2,1)S(1)}, bf16[2,256,256]{2,1,0:T(8,128)(2,1)}, u32[]{:S(2)}) copy-start(bf16[2,256,256]{2,1,0:T(8,128)(2,1)} %wf_ref.3) | copy-start | bytes 786436
  31.6 7.2 %collective-permute-start.9 = (bf16[3,64,256]{2,1,0:T(8,128)(2,1)S(1)}, bf16[3,64,256]{2,1,0:T(8,128)(2,1)S(1)}, u32[]{:S(2)}, u32[]{:S(2)}) collective-permute-start(bf16[3,64,256]{2,1,0:T(8,128)(2,1)S(1)} %add.11.own_ref), channel_id=1, source_target_pairs={{0,3},{1,0},{2,1},{3,2},{4,7},{5,4},{6,5},{7,6},{8,11},{9,8},{10,9... | collective-permute-start | bytes 294920 | tf_op jit(solution)/shard_map/ppermute | solution.py:259
  36.0 8.0 %collective-permute-start.8 = (bf16[3,64,256]{2,1,0:T(8,128)(2,1)S(1)}, bf16[3,64,256]{2,1,0:T(8,128)(2,1)S(1)}, u32[]{:S(2)}, u32[]{:S(2)}) collective-permute-start(bf16[3,64,256]{2,1,0:T(8,128)(2,1)S(1)} %add.11.own_ref), channel_id=1, source_target_pairs={{0,2},{1,3},{2,0},{3,1},{4,6},{5,7},{6,4},{7,5},{8,10},{9,11},{10,... | collective-permute-start | bytes 294920 | tf_op jit(solution)/shard_map/ppermute | solution.py:259
  36.4 7.6 %collective-permute-start.7 = (bf16[3,64,256]{2,1,0:T(8,128)(2,1)S(1)}, bf16[3,64,256]{2,1,0:T(8,128)(2,1)S(1)}, u32[]{:S(2)}, u32[]{:S(2)}) collective-permute-start(bf16[3,64,256]{2,1,0:T(8,128)(2,1)S(1)} %add.11.own_ref), channel_id=1, source_target_pairs={{0,1},{1,2},{2,3},{3,0},{4,5},{5,6},{6,7},{7,4},{8,9},{9,10},{10,1... | collective-permute-start | bytes 294920 | tf_op jit(solution)/shard_map/ppermute | solution.py:259
  44.7 6.6 %collective-permute-start.12 = (bf16[3,64,256]{2,1,0:T(8,128)(2,1)S(1)}, bf16[3,64,256]{2,1,0:T(8,128)(2,1)S(1)}, u32[]{:S(2)}, u32[]{:S(2)}) collective-permute-start(bf16[3,64,256]{2,1,0:T(8,128)(2,1)S(1)} %region_sum.1.refs_0_), channel_id=1, source_target_pairs={{0,24},{4,28},{8,16},{12,20},{16,8},{20,12},{24,0},{28,4},{1,25},{... | collective-permute-start | bytes 294920 | tf_op jit(solution)/shard_map/ppermute | solution.py:264
  46.4 5.3 %collective-permute-start.11 = (bf16[3,64,256]{2,1,0:T(8,128)(2,1)S(1)}, bf16[3,64,256]{2,1,0:T(8,128)(2,1)S(1)}, u32[]{:S(2)}, u32[]{:S(2)}) collective-permute-start(bf16[3,64,256]{2,1,0:T(8,128)(2,1)S(1)} %region_sum.1.refs_0_), channel_id=1, source_target_pairs={{0,16},{4,20},{8,24},{12,28},{16,0},{20,4},{24,8},{28,12},{1,17},{... | collective-permute-start | bytes 294920 | tf_op jit(solution)/shard_map/ppermute | solution.py:264
  47.9 4.6 %collective-permute-start.10 = (bf16[3,64,256]{2,1,0:T(8,128)(2,1)S(1)}, bf16[3,64,256]{2,1,0:T(8,128)(2,1)S(1)}, u32[]{:S(2)}, u32[]{:S(2)}) collective-permute-start(bf16[3,64,256]{2,1,0:T(8,128)(2,1)S(1)} %region_sum.1.refs_0_), channel_id=1, source_target_pairs={{0,8},{4,12},{8,0},{12,4},{16,24},{20,28},{24,16},{28,20},{1,9},{5... | collective-permute-start | bytes 294920 | tf_op jit(solution)/shard_map/ppermute | solution.py:264
  48.2 5.4 %collective-permute-start.13 = (bf16[3,64,256]{2,1,0:T(8,128)(2,1)S(1)}, bf16[3,64,256]{2,1,0:T(8,128)(2,1)S(1)}, u32[]{:S(2)}, u32[]{:S(2)}) collective-permute-start(bf16[3,64,256]{2,1,0:T(8,128)(2,1)S(1)} %region_sum.1.refs_0_), channel_id=1, source_target_pairs={{0,4},{4,0},{8,12},{12,8},{16,20},{20,16},{24,28},{28,24},{1,5},{5... | collective-permute-start | bytes 294920 | tf_op jit(solution)/shard_map/ppermute | solution.py:265
  51.3 2.4 %collective-permute-start.16 = (bf16[3,64,256]{2,1,0:T(8,128)(2,1)S(1)}, bf16[3,64,256]{2,1,0:T(8,128)(2,1)S(1)}, u32[]{:S(2)}, u32[]{:S(2)}) collective-permute-start(bf16[3,64,256]{2,1,0:T(8,128)(2,1)S(1)} %collective-permute-done.12.refs_3_), channel_id=1, source_target_pairs={{0,4},{4,0},{8,12},{12,8},{16,20},{20,16},{24,28},{28,24},{1,5},{5... | collective-permute-start | bytes 294920 | tf_op jit(solution)/shard_map/ppermute | solution.py:265
  51.7 2.0 %collective-permute-start.15 = (bf16[3,64,256]{2,1,0:T(8,128)(2,1)S(1)}, bf16[3,64,256]{2,1,0:T(8,128)(2,1)S(1)}, u32[]{:S(2)}, u32[]{:S(2)}) collective-permute-start(bf16[3,64,256]{2,1,0:T(8,128)(2,1)S(1)} %collective-permute-done.11.refs_2_), channel_id=1, source_target_pairs={{0,4},{4,0},{8,12},{12,8},{16,20},{20,16},{24,28},{28,24},{1,5},{5... | collective-permute-start | bytes 294920 | tf_op jit(solution)/shard_map/ppermute | solution.py:265
  52.5 1.3 %collective-permute-start.14 = (bf16[3,64,256]{2,1,0:T(8,128)(2,1)S(1)}, bf16[3,64,256]{2,1,0:T(8,128)(2,1)S(1)}, u32[]{:S(2)}, u32[]{:S(2)}) collective-permute-start(bf16[3,64,256]{2,1,0:T(8,128)(2,1)S(1)} %collective-permute-done.10.refs_1_), channel_id=1, source_target_pairs={{0,4},{4,0},{8,12},{12,8},{16,20},{20,16},{24,28},{28,24},{1,5},{5... | collective-permute-start | bytes 294920 | tf_op jit(solution)/shard_map/ppermute | solution.py:265
  (3 other events, 2.6 us)

commit v2 on v1

v2 whole, which is shorter than its diff:
```python
import functools
import math

import jax
import jax.numpy as jnp
from jax import lax
from jax.experimental import pallas as pl
from jax.experimental.pallas import tpu as pltpu
from jax.sharding import PartitionSpec as P

TILE = 128
F32 = jnp.float32
BF16 = jnp.bfloat16
VM = pl.BlockSpec(memory_space=pltpu.VMEM)
HB = pl.BlockSpec(memory_space=pltpu.HBM)
BOTH = ("dp", "region")


def dot(a, b, ca=1, cb=0):
    return lax.dot_general(a, b, (((ca,), (cb,)), ((), ())), preferred_element_type=F32)


def call(body, outs, ins, name, out_specs=None, scratch=(), flops=0, nbytes=0, aliases=None):
    return pl.pallas_call(
        body,
        out_shape=outs,
        in_specs=ins,
        out_specs=out_specs or [VM] * len(outs),
        scratch_shapes=list(scratch),
        cost_estimate=pl.CostEstimate(flops=flops, bytes_accessed=nbytes, transcendentals=0),
        compiler_params=pltpu.CompilerParams(vmem_limit_bytes=40 * 1024 * 1024),
        input_output_aliases=aliases or {},
        name=name,
    )


def fetch(pairs, sems):
    copies = [pltpu.make_async_copy(src, dst, sems.at[i]) for i, (src, dst) in enumerate(pairs)]
    for copy in copies:
        copy.start()
    return copies


def find_entry(nb_ref, source, target, tiles, per_tile):
    tile = jnp.int32(0)
    place = jnp.int32(0)
    named = jnp.int32(-1)
    for j in range(tiles):
        for k in range(per_tile):
            local = nb_ref[source * tiles + j, k] - target * tiles
            hit = jnp.logical_and(local >= 0, local < tiles)
            tile = jnp.where(hit, j, tile)
            place = jnp.where(hit, k, place)
            named = jnp.where(hit, local, named)
    return tile, place, named


def region_of():
    return lax.axis_index("region").astype(jnp.int32)


def lane_of():
    place = lax.axis_index("dp").astype(jnp.int32)
    lane, chip, region = jnp.bitwise_and(place, 1), lax.shift_right_logical(place, 1), region_of()
    return lane, jnp.where(lane == 0, chip, region), jnp.where(lane == 0, region, chip)


def outgoing_body(regions, order, nb_hbm, cot_hbm, adj_hbm, *refs):
    out_refs, (nb_ref, cot_ref, adj_ref, sems) = refs[: regions - 1], refs[regions - 1 :]
    me = region_of()
    tiles, per_tile = adj_ref.shape[:2]
    total = cot_ref.shape[0]
    first, *copies = fetch(
        [(nb_hbm, nb_ref)]
        + [(cot_hbm.at[t], cot_ref.at[t]) for t in range(total)]
        + [(adj_hbm.at[j], adj_ref.at[j]) for j in range(tiles)],
        sems,
    )
    first.wait()
    found = [find_entry(nb_ref, me, jnp.bitwise_xor(me, p), tiles, per_tile) for p in order]
    for copy in copies:
        copy.wait()
    for out, (tile, place, named) in zip(out_refs, found):

        @pl.when(named >= 0)
        def _():
            weights = adj_ref[tile, place]
            for t in range(total):
                rows = cot_ref[t, pl.ds(pl.multiple_of(tile * TILE, TILE), TILE), :]
                out[t] = dot(weights, rows, 0, 0).astype(BF16)

        @pl.when(named < 0)
        def _():
            out[...] = jnp.zeros_like(out)


def local_body(
    steps, order, nb_hbm, x_hbm, cot_hbm, wf_hbm, wg_hbm, wm_hbm, adj_hbm,
    df_ref, dg_ref, direct_ref, local_ref, mix_ref, xt_ref, ht_ref, wt_ref, mask_ref,
    nb_ref, x_ref, cot_ref, wf_ref, wg_ref, wm_ref, adj_ref, sems,
):
    me = region_of()
    tiles, per_tile = adj_ref.shape[:2]
    total = cot_ref.shape[0]
    c_nb, c_x, c_wf, c_wg, c_cot, c_wm, c_adj = fetch(
        [(nb_hbm, nb_ref), (x_hbm, x_ref), (wf_hbm, wf_ref), (wg_hbm, wg_ref), (cot_hbm, cot_ref), (wm_hbm, wm_ref), (adj_hbm, adj_ref)],
        sems,
    )
    c_x.wait()
    c_wf.wait()
    c_wg.wait()
    for t in range(total):
        x = x_ref[t]
        act_f = dot(x, wf_ref[0])
        act_g = dot(x, wg_ref[0])
        if t % steps:
            before = x_ref[t - 1]
            act_f += dot(before, wf_ref[1])
            act_g += dot(before, wg_ref[1])
        filt = jnp.tanh(act_f)
        gate = jax.nn.sigmoid(act_g)
        both = filt * gate
        ht_ref[t] = both.astype(BF16).T
        xt_ref[t] = x.T
        df_ref[t] = gate * (1.0 - filt * filt)
        dg_ref[t] = both * (1.0 - gate)
    c_cot.wait()
    c_wm.wait()
    wt_ref[...] = wm_ref[1].T
    mix = jnp.zeros(mix_ref.shape, F32)
    for t in range(total):
        cot = cot_ref[t]
        direct_ref[t] = dot(cot, wm_ref[0], 1, 1)
        mix += dot(ht_ref[t], cot)
    mix_ref[...] = mix
    local_ref[...] = jnp.zeros_like(local_ref)
    c_nb.wait()
    c_adj.wait()
    for j in range(tiles):
        for k in range(per_tile):
            local = nb_ref[me * tiles + j, k] - me * tiles

            @pl.when(jnp.logical_and(local >= 0, local < tiles))
            def _():
                place = pl.ds(pl.multiple_of(local * TILE, TILE), TILE)
                for t in range(total):
                    local_ref[t, place, :] += dot(adj_ref[j, k], cot_ref[t, j * TILE : (j + 1) * TILE, :], 0, 0)

    for s, p in enumerate(order):
        _, _, named = find_entry(nb_ref, jnp.bitwise_xor(me, p), me, tiles, per_tile)
        for j in range(tiles):
            mask_ref[s, j] = jnp.full(mask_ref.shape[2:], jnp.where(named == j, 1.0, 0.0), F32)


def tap_rows(tap, part, steps, xt_ref, act_ref):
    total = xt_ref.shape[0]
    if tap == 0:
        terms = [dot(xt_ref[t], act_ref[part, t]) for t in range(total)]
    else:
        terms = [dot(xt_ref[t - 1], act_ref[part, t]) for t in range(total) if t % steps]
    return functools.reduce(jnp.add, terms)


def half_of(tap, steps, xt_ref, ht_ref, mix_ref, act_ref, sums_ref):
    if tap == 0:
        mix = mix_ref[...]
    else:
        mix = functools.reduce(jnp.add, [dot(ht_ref[t], sums_ref[t]) for t in range(ht_ref.shape[0])])
    return [tap_rows(tap, 0, steps, xt_ref, act_ref), tap_rows(tap, 1, steps, xt_ref, act_ref), mix]


def send_body(regions, steps, df_ref, dg_ref, direct_ref, local_ref, mix_ref, xt_ref, ht_ref, wt_ref, mask_ref, *refs):
    arrived, (act_ref, sums_ref, send_ref) = refs[: regions - 1], refs[regions - 1 :]
    lane, _, _ = lane_of()
    total, sites, _ = local_ref.shape
    tiles = sites // TILE
    for t in range(total):
        summed = []
        for j in range(tiles):
            part = local_ref[t, j * TILE : (j + 1) * TILE, :]
            for s in range(regions - 1):
                part += mask_ref[s, j, :1] * arrived[s][t].astype(F32)
            summed.append(part.astype(BF16))
        summed = jnp.concatenate(summed, axis=0)
        sums_ref[t] = summed
        grad = direct_ref[t] + dot(summed, wt_ref[...])
        act_ref[0, t] = (grad * df_ref[t]).astype(BF16)
        act_ref[1, t] = (grad * dg_ref[t]).astype(BF16)
    for tap in range(2):

        @pl.when(lane == 1 - tap)
        def _():
            for i, part in enumerate(half_of(tap, steps, xt_ref, ht_ref, mix_ref, act_ref, sums_ref)):
                send_ref[i] = part.astype(BF16)


def keep_body(steps, mix_ref, xt_ref, ht_ref, act_ref, sums_ref, cot_ref, wf_ref, wg_ref, keep_ref, out_ref):
    lane, _, _ = lane_of()
    for tap in range(2):

        @pl.when(lane == tap)
        def _():
            for i, part in enumerate(half_of(tap, steps, xt_ref, ht_ref, mix_ref, act_ref, sums_ref)):
                keep_ref[i] = part

    total = cot_ref.shape[0]
    for t in range(total):
        grad = cot_ref[t].astype(F32)
        grad += dot(act_ref[0, t], wf_ref[0], 1, 1) + dot(act_ref[1, t], wg_ref[0], 1, 1)
        if (t + 1) % steps:
            grad += dot(act_ref[0, t + 1], wf_ref[1], 1, 1) + dot(act_ref[1, t + 1], wg_ref[1], 1, 1)
        out_ref[t] = grad.astype(BF16)


def split_body(ways, keep_ref, got_ref, own_ref, *sends):
    _, mine, _ = lane_of()
    rows = own_ref.shape[1]

    def chunk(p):
        place = pl.ds(pl.multiple_of(jnp.bitwise_xor(mine, p) * rows, rows), rows)
        return keep_ref[:, place, :] + got_ref[:, place, :].astype(F32)

    own_ref[...] = chunk(0)
    for p, send in enumerate(sends, 1):
        send[...] = chunk(p).astype(BF16)


def tree(parts):
    while len(parts) > 1:
        parts = [parts[i] + parts[i + 1] for i in range(0, len(parts), 2)]
    return parts[0]


def add_body(*refs):
    refs[-1][...] = tree([ref[...].astype(F32) for ref in refs[:-1]]).astype(BF16)


def scale_body(ways, factor, other, *refs):
    chunks, refs = refs[:ways], refs[ways:]
    outs, (held, sems) = refs[-5:-2], refs[-2:]
    lane, first, second = lane_of()
    tap, mine = (1 - lane, second) if other else (lane, first)
    rows = chunks[0].shape[1]
    copies = []
    for p in range(ways):
        place = pl.ds(pl.multiple_of(jnp.bitwise_xor(mine, p) * rows, rows), rows)
        for a in range(3):
            held[p, a] = chunks[p][a].astype(F32) * factor
            copy = pltpu.make_async_copy(held.at[p, a], outs[a].at[tap, place], sems.at[p, a])
            copy.start()
            copies.append(copy)
    for copy in copies:
        copy.wait()


def per_device(inputs, cotangent, w_filter, w_gate, w_mix, neighbours, adjacency):
    regions = lax.axis_size("region")
    dp = lax.axis_size("dp")
    ways = dp // 2
    assert ways == regions
    windows, steps, sites, chans = inputs.shape
    total = windows * steps
    tiles, per_tile = adjacency.shape[:2]
    x = inputs.reshape(total, sites, chans)
    cot = cotangent.reshape(total, sites, chans)
    shape = jax.ShapeDtypeStruct
    block = total * sites * chans
    order = sorted(range(1, regions), key=lambda p: p < regions // 2)
    dma = pltpu.SemaphoreType.DMA

    outgoing = call(
        functools.partial(outgoing_body, regions, order),
        [shape((total, TILE, chans), BF16)] * (regions - 1), [HB] * 3, "outgoing",
        scratch=[
            pltpu.SMEM(neighbours.shape, jnp.int32), pltpu.VMEM(cot.shape, BF16), pltpu.VMEM(adjacency.shape, BF16),
            dma((1 + total + tiles,)),
        ],
        flops=2 * (regions - 1) * total * TILE * TILE * chans, nbytes=4 * block,
    )(neighbours, cot, adjacency)
    arrived = [
        lax.ppermute(part, "region", [(r, r ^ p) for r in range(regions)]) for p, part in zip(order, outgoing)
    ]
    square = shape((chans, chans), F32)
    turned = shape((total, chans, sites), BF16)
    d_filter, d_gate, direct, local, mix, xt, ht, wt, mask = call(
        functools.partial(local_body, steps, order),
        [shape(x.shape, F32)] * 4
        + [square, turned, turned, shape((chans, chans), BF16), shape((regions - 1, tiles, 8, chans), F32)],
        [HB] * 7, "local",
        scratch=[
            pltpu.SMEM(neighbours.shape, jnp.int32), pltpu.VMEM(x.shape, BF16), pltpu.VMEM(x.shape, BF16),
            pltpu.VMEM(w_filter.shape, BF16), pltpu.VMEM(w_gate.shape, BF16), pltpu.VMEM(w_mix.shape, BF16),
            pltpu.VMEM(adjacency.shape, BF16), dma((7,)),
        ],
        flops=14 * block * chans, nbytes=30 * block,
    )(neighbours, x, cot, w_filter, w_gate, w_mix, adjacency)
    act_cot, sums, send = call(
        functools.partial(send_body, regions, steps),
        [shape((2,) + x.shape, BF16), shape(x.shape, BF16), shape((3, chans, chans), BF16)],
        [VM] * (9 + regions - 1), "send",
        flops=6 * block * chans, nbytes=30 * block,
    )(d_filter, d_gate, direct, local, mix, xt, ht, wt, mask, *arrived)
    swap = [(i, i ^ 1) for i in range(dp)]
    got = lax.ppermute(send, "dp", swap)
    keep, grad_inputs = call(
        functools.partial(keep_body, steps),
        [shape((3, chans, chans), F32), shape(x.shape, BF16)], [VM] * 8, "keep",
        flops=12 * block * chans, nbytes=30 * block,
    )(mix, xt, ht, act_cot, sums, cot, w_filter, w_gate)

    rows = chans // ways
    chunk = (3, rows, chans)

    def pairs(p, turn):
        result = []
        for d in range(dp):
            for r in range(regions):
                e, q = (d ^ (2 * p), r) if (d % 2 == 0) == turn else (d, r ^ p)
                result.append((d * regions + r, e * regions + q))
        return result

    own, *sends = call(
        functools.partial(split_body, ways),
        [shape(chunk, F32)] + [shape(chunk, BF16)] * (ways - 1), [VM] * 2, "split",
    )(keep, got)
    gots = [lax.ppermute(part, BOTH, pairs(p, True)) for p, part in enumerate(sends, 1)]
    (mine,) = call(add_body, [shape(chunk, BF16)], [VM] * ways, "add_first")(own, *gots)
    gots = [lax.ppermute(mine, BOTH, pairs(p, False)) for p in range(1, ways)]
    (done,) = call(add_body, [shape(chunk, BF16)], [VM] * ways, "add_second")(mine, *gots)
    chunks = [done] + [lax.ppermute(done, BOTH, pairs(p, True)) for p in range(1, ways)]
    others = [lax.ppermute(part, "dp", swap) for part in chunks]
    factor = 1.0 / math.sqrt(windows * dp * steps * sites * regions)
    results = [shape((2, chans, chans), F32)] * 3
    extra = dict(out_specs=[HB] * 3, scratch=[pltpu.VMEM((ways,) + chunk, F32), dma((ways, 3))])
    grads = call(functools.partial(scale_body, ways, factor, False), results, [VM] * ways, "scale_own", **extra)(*chunks)
    grads = call(
        functools.partial(scale_body, ways, factor, True), results, [VM] * ways + [HB] * 3, "scale_other",
        aliases={ways + a: a for a in range(3)}, **extra,
    )(*others, *grads)
    return (grad_inputs.reshape(inputs.shape), *grads)


def solution(mesh):
    return jax.shard_map(
        per_device,
        mesh=mesh,
        in_specs=(
            P("dp", None, "region", None),
            P("dp", None, "region", None),
            P(),
            P(),
            P(),
            P(),
            P("region", None, None, None),
        ),
        out_specs=(P("dp", None, "region", None), P(), P(), P()),
        check_vma=False,
    )
```

time: 55.9 us -> 50.2 us (0.90)
  waiting for transfers between devices: 18.7 us -> 15.7 us
  starting transfers between devices: 19.3 us -> 17.6 us
  Pallas kernels: 10.4 us -> 9.06 us
    ppermute x17, waiting for transfers between devices: 18.7 us -> 15.7 us  [the longest x3 5.41 us: per_device(): gots = [lax.ppermute(mine, BOTH, pairs(p, False)) for p in range(1, ways)]]
    ppermute x17, starting transfers between devices: 19.3 us -> 17.6 us  [the longest x3 5.68 us: per_device(): lax.ppermute(part, 'region', [(r, r ^ p) for r in range(regions)])]
    pallas_call x8 -> x9, Pallas kernels: 10.4 us -> 9.06 us  [the longest x1 3.28 us: per_device(): call(functools.partial(local_body, steps, order), [shape(x.shape, F32)] *...]
  transfers between devices with their start and end apart: 17 -> 17, of which waited for: 11 -> 12; matrix products, arithmetic and copies ran while one was open for 0% -> 0% of each run, Pallas kernels for 8% -> 11%
where the time goes in v2:
time: 50.2 us; the launch traced here: 49.8 us
  starting transfers between devices  17.6 us (35%)
  waiting for transfers between devices  15.7 us (31%)
  Pallas kernels  9.06 us (18%)
  local copies, waits for them, and re-layouts  6.66 us (13%)
  between operations  0.74 us (1%)
    unnamed x20, local copies, waits for them, and re-layouts  6.66 us
    ppermute x3, starting transfers between devices, per_device(): lax.ppermute(part, 'region', [(r, r ^ p) for r in range(regions)])  5.68 us
    ppermute x3, waiting for transfers between devices, per_device(): gots = [lax.ppermute(mine, BOTH, pairs(p, False)) for p in range(1, ways)]  5.41 us
    ppermute x3, waiting for transfers between devices, per_device(): lax.ppermute(part, BOTH, pairs(p, True))  5.09 us
    ppermute x3, starting transfers between devices, per_device(): gots = [lax.ppermute(mine, BOTH, pairs(p, False)) for p in range(1, ways)]  4.69 us
    ppermute x3, starting transfers between devices, per_device(): lax.ppermute(done, BOTH, pairs(p, True))  3.55 us
    ppermute x3, starting transfers between devices, per_device(): lax.ppermute(part, BOTH, pairs(p, True))  3.55 us
    pallas_call x1, Pallas kernels, per_device(): call(functools.partial(local_body, steps, order), [shape(x.shape, F32)] *...  3.28 us
  transfers between devices with their start and end apart: 17, of which 12 were waited for; matrix products, arithmetic and copies ran while one was open for 0% of the time, Pallas kernels for 11%

profile of v2, /device:TPU:0, one launch (start us, length us, event | category | flops | bytes accessed | tf_op | source)
XLA Modules:
  0.0 49.8 jit_solution(6916496926945149487)
XLA Ops:
  1.6 1.0 %copy-done.2 = bf16[2,6,128,128]{3,2,1,0:T(8,128)(2,1)S(1)} copy-done((bf16[2,6,128,128]{3,2,1,0:T(8,128)(2,1)S(1)}, bf16[2,6,128,128]{3,2,1,0:T(8,128)(2,1)}, u32[]{:S(2)}) %copy-start.2) | copy-done | bytes 393240
  3.3 1.6 %outgoing.1 = (bf16[2,128,256]{2,1,0:T(8,128)(2,1)S(1)}, bf16[2,128,256]{2,1,0:T(8,128)(2,1)S(1)}, bf16[2,128,256]{2,1,0:T(8,128)(2,1)S(1)}) custom-call(s32[8,6]{1,0:T(8,128)S(1)} %copy-done.7, bf16[2,256,256]{2,1,0:T(8,128)(2,1)S(1)} %bitcast.3, bf16[2,6,128,128]{3,2,1,0:T(8,128)(2,1)S(1)} %copy-done.2), custom_call_target="tpu_custom_call" | custom-call | flops 50331648 | bytes 524288 | tf_op jit(solution)/shard_map/outgoing/pallas_call | solution.py:271
  4.9 4.1 %collective-permute-start = (bf16[2,128,256]{2,1,0:T(8,128)(2,1)S(1)}, bf16[2,128,256]{2,1,0:T(8,128)(2,1)S(1)}, u32[]{:S(2)}, u32[]{:S(2)}) collective-permute-start(bf16[2,128,256]{2,1,0:T(8,128)(2,1)S(1)} %get-tuple-element.40), channel_id=1, source_target_pairs={{0,2},{1,3},{2,0},{3,1},{4,6},{5,7},{6,4},{7,5},{8,10},{9,11},{10,... | collective-permute-start | bytes 393224 | tf_op jit(solution)/shard_map/ppermute | solution.py:281
  9.0 1.3 %collective-permute-start.1 = (bf16[2,128,256]{2,1,0:T(8,128)(2,1)S(1)}, bf16[2,128,256]{2,1,0:T(8,128)(2,1)S(1)}, u32[]{:S(2)}, u32[]{:S(2)}) collective-permute-start(bf16[2,128,256]{2,1,0:T(8,128)(2,1)S(1)} %get-tuple-element.41), channel_id=1, source_target_pairs={{0,3},{1,2},{2,1},{3,0},{4,7},{5,6},{6,5},{7,4},{8,11},{9,10},{10,... | collective-permute-start | bytes 393224 | tf_op jit(solution)/shard_map/ppermute | solution.py:281
  10.6 0.9 %copy-done.4 = bf16[2,256,256]{2,1,0:T(8,128)(2,1)S(1)} copy-done((bf16[2,256,256]{2,1,0:T(8,128)(2,1)S(1)}, bf16[2,256,256]{2,1,0:T(8,128)(2,1)}, u32[]{:S(2)}) %copy-start.4) | copy-done | bytes 262168
  11.5 0.9 %copy-done.6 = bf16[2,256,256]{2,1,0:T(8,128)(2,1)S(1)} copy-done((bf16[2,256,256]{2,1,0:T(8,128)(2,1)S(1)}, bf16[2,256,256]{2,1,0:T(8,128)(2,1)}, u32[]{:S(2)}) %copy-start.6) | copy-done | bytes 262168
  12.5 0.9 %copy-done.8 = bf16[1,2,256,256]{3,2,1,0:T(8,128)(2,1)S(1)} copy-done((bf16[1,2,256,256]{3,2,1,0:T(8,128)(2,1)S(1)}, bf16[1,2,256,256]{3,2,1,0:T(8,128)(2,1)}, u32[]{:S(2)}) %copy-start.8) | copy-done | bytes 262168
  13.4 0.9 %copy-done.9 = bf16[2,256,256]{2,1,0:T(8,128)(2,1)S(1)} copy-done((bf16[2,256,256]{2,1,0:T(8,128)(2,1)S(1)}, bf16[2,256,256]{2,1,0:T(8,128)(2,1)}, u32[]{:S(2)}) %copy-start.9) | copy-done | bytes 262168
  14.4 3.3 %local.1 = (f32[2,256,256]{2,1,0:T(8,128)S(1)}, f32[2,256,256]{2,1,0:T(8,128)S(1)}, f32[2,256,256]{2,1,0:T(8,128)S(1)}, f32[2,256,256]{2,1,0:T(8,128)S(1)}, f32[...) custom-call(s32[8,6]{1,0:T(8,128)S(1)} %copy-done.7, ...), custom_call_target="tpu_custom_call" | custom-call | flops 469762048 | bytes 3932160 | tf_op jit(solution)/shard_map/local/pallas_call | solution.py:285
  17.7 1.3 %collective-permute-done.refs_0_ = bf16[2,128,256]{2,1,0:T(8,128)(2,1)S(1)} collective-permute-done((bf16[2,128,256]{2,1,0:T(8,128)(2,1)S(1)}, bf16[2,128,256]{2,1,0:T(8,128)(2,1)S(1)}, u32[]{:S(2)}, u32[]{:S(2)}) %collective-permute-start) | collective-permute-done | bytes 131104 | tf_op jit(solution)/shard_map/ppermute | solution.py:281
  20.4 1.4 %keep.1 = (f32[3,256,256]{2,1,0:T(8,128)S(1)}, bf16[2,256,256]{2,1,0:T(8,128)(2,1)}) custom-call(f32[256,256]{1,0:T(8,128)S(1)} %get-tuple-element.31.mix_ref, bf16[2,256,256]{2,1,0:T(8,128)(2,1)S(1)} %get-tuple-element.32.xt_ref, bf16[2,256,256]{2,1,0:T(8,128)(2,1)S(1)} %get-tuple-element.33.ht_ref, bf16[2,2,256,256]{3,2,1,0:T(8,128)(2,1)S(1)} %get-tuple-element.43.act_ref, ...), custom_call_target="tpu_custom_call" | custom-call | flops 402653184 | bytes 3932160 | tf_op jit(solution)/shard_map/keep/pallas_call | solution.py:305
  22.0 1.6 %collective-permute-start.4 = (bf16[3,64,256]{2,1,0:T(8,128)(2,1)S(1)}, bf16[3,64,256]{2,1,0:T(8,128)(2,1)S(1)}, u32[]{:S(2)}, u32[]{:S(2)}) collective-permute-start(bf16[3,64,256]{2,1,0:T(8,128)(2,1)S(1)} %get-tuple-element.49), channel_id=1, source_target_pairs={{0,8},{1,9},{2,10},{3,11},{4,5},{5,4},{6,7},{7,6},{8,0},{9,1},{10,... | collective-permute-start | bytes 294920 | tf_op jit(solution)/shard_map/ppermute | solution.py:326
  23.6 1.5 %collective-permute-start.5 = (bf16[3,64,256]{2,1,0:T(8,128)(2,1)S(1)}, bf16[3,64,256]{2,1,0:T(8,128)(2,1)S(1)}, u32[]{:S(2)}, u32[]{:S(2)}) collective-permute-start(bf16[3,64,256]{2,1,0:T(8,128)(2,1)S(1)} %get-tuple-element.50), channel_id=1, source_target_pairs={{0,16},{1,17},{2,18},{3,19},{4,6},{5,7},{6,4},{7,5},{8,24},{9,25},... | collective-permute-start | bytes 294920 | tf_op jit(solution)/shard_map/ppermute | solution.py:326
  25.5 1.1 %collective-permute-done.4.refs_1_ = bf16[3,64,256]{2,1,0:T(8,128)(2,1)S(1)} collective-permute-done((bf16[3,64,256]{2,1,0:T(8,128)(2,1)S(1)}, bf16[3,64,256]{2,1,0:T(8,128)(2,1)S(1)}, u32[]{:S(2)}, u32[]{:S(2)}) %collective-permute-start.4) | collective-permute-done | bytes 98336 | tf_op jit(solution)/shard_map/ppermute | solution.py:326
  26.7 1.5 %collective-permute-done.5.refs_2_ = bf16[3,64,256]{2,1,0:T(8,128)(2,1)S(1)} collective-permute-done((bf16[3,64,256]{2,1,0:T(8,128)(2,1)S(1)}, bf16[3,64,256]{2,1,0:T(8,128)(2,1)S(1)}, u32[]{:S(2)}, u32[]{:S(2)}) %collective-permute-start.5) | collective-permute-done | bytes 98336 | tf_op jit(solution)/shard_map/ppermute | solution.py:326
  28.2 2.4 %collective-permute-done.6.refs_3_ = bf16[3,64,256]{2,1,0:T(8,128)(2,1)S(1)} collective-permute-done((bf16[3,64,256]{2,1,0:T(8,128)(2,1)S(1)}, bf16[3,64,256]{2,1,0:T(8,128)(2,1)S(1)}, u32[]{:S(2)}, u32[]{:S(2)}) %collective-permute-start.6) | collective-permute-done | bytes 98336 | tf_op jit(solution)/shard_map/ppermute | solution.py:326
  30.7 3.5 %collective-permute-start.9 = (bf16[3,64,256]{2,1,0:T(8,128)(2,1)S(1)}, bf16[3,64,256]{2,1,0:T(8,128)(2,1)S(1)}, u32[]{:S(2)}, u32[]{:S(2)}) collective-permute-start(bf16[3,64,256]{2,1,0:T(8,128)(2,1)S(1)} %add_first.1.refs_0_), channel_id=1, source_target_pairs={{0,3},{1,2},{2,1},{3,0},{4,28},{5,29},{6,30},{7,31},{8,11},{9,10},... | collective-permute-start | bytes 294920 | tf_op jit(solution)/shard_map/ppermute | solution.py:328
  35.4 1.9 %collective-permute-done.9.refs_3_ = bf16[3,64,256]{2,1,0:T(8,128)(2,1)S(1)} collective-permute-done((bf16[3,64,256]{2,1,0:T(8,128)(2,1)S(1)}, bf16[3,64,256]{2,1,0:T(8,128)(2,1)S(1)}, u32[]{:S(2)}, u32[]{:S(2)}) %collective-permute-start.9) | collective-permute-done | bytes 98336 | tf_op jit(solution)/shard_map/ppermute | solution.py:328
  37.2 3.5 %collective-permute-done.8.refs_2_ = bf16[3,64,256]{2,1,0:T(8,128)(2,1)S(1)} collective-permute-done((bf16[3,64,256]{2,1,0:T(8,128)(2,1)S(1)}, bf16[3,64,256]{2,1,0:T(8,128)(2,1)S(1)}, u32[]{:S(2)}, u32[]{:S(2)}) %collective-permute-start.8) | collective-permute-done | bytes 98336 | tf_op jit(solution)/shard_map/ppermute | solution.py:328
  41.4 1.5 %collective-permute-start.13 = (bf16[3,64,256]{2,1,0:T(8,128)(2,1)S(1)}, bf16[3,64,256]{2,1,0:T(8,128)(2,1)S(1)}, u32[]{:S(2)}, u32[]{:S(2)}) collective-permute-start(bf16[3,64,256]{2,1,0:T(8,128)(2,1)S(1)} %add_second.1.refs_0_), channel_id=1, source_target_pairs={{0,16},{1,17},{2,18},{3,19},{4,6},{5,7},{6,4},{7,5},{8,24},{9,25},... | collective-permute-start | bytes 294920 | tf_op jit(solution)/shard_map/ppermute | solution.py:330
  42.9 1.5 %collective-permute-start.11 = (bf16[3,64,256]{2,1,0:T(8,128)(2,1)S(1)}, bf16[3,64,256]{2,1,0:T(8,128)(2,1)S(1)}, u32[]{:S(2)}, u32[]{:S(2)}) collective-permute-start(bf16[3,64,256]{2,1,0:T(8,128)(2,1)S(1)} %add_second.1.refs_0_), channel_id=1, source_target_pairs={{0,8},{1,9},{2,10},{3,11},{4,5},{5,4},{6,7},{7,6},{8,0},{9,1},{10,... | collective-permute-start | bytes 294920 | tf_op jit(solution)/shard_map/ppermute | solution.py:330
  44.4 2.1 %collective-permute-done.15.refs_3_ = bf16[3,64,256]{2,1,0:T(8,128)(2,1)S(1)} collective-permute-done((bf16[3,64,256]{2,1,0:T(8,128)(2,1)S(1)}, bf16[3,64,256]{2,1,0:T(8,128)(2,1)S(1)}, u32[]{:S(2)}, u32[]{:S(2)}) %collective-permute-start.15) | collective-permute-done | bytes 98336 | tf_op jit(solution)/shard_map/ppermute | solution.py:330
  47.6 1.0 %scale_own.1 = (f32[2,256,256]{2,1,0:T(8,128)}, f32[2,256,256]{2,1,0:T(8,128)}, f32[2,256,256]{2,1,0:T(8,128)}) custom-call(bf16[3,64,256]{2,1,0:T(8,128)(2,1)S(1)} %add_second.1.refs_0_, bf16[3,64,256]{2,1,0:T(8,128)(2,1)S(1)} %collective-permute-done.11.refs_1_, bf16[3,64,256]{2,1,0:T(8,128)(2,1)S(1)} %collective-permute-done.13.refs_2_, ...), custom_call_target="tpu_custom_call" | custom-call | tf_op jit(solution)/shard_map/scale_own/pallas_call | solution.py:335
  48.8 1.0 %scale_other.1 = (f32[2,256,256]{2,1,0:T(8,128)}, f32[2,256,256]{2,1,0:T(8,128)}, f32[2,256,256]{2,1,0:T(8,128)}) custom-call(bf16[3,64,256]{2,1,0:T(8,128)(2,1)S(1)} %collective-permute-done.10.refs_0_, bf16[3,64,256]{2,1,0:T(8,128)(2,1)S(1)} %collective-permute-done.12.refs_1_, ...), custom_call_target="tpu_custom_call", output_to_operand_aliasing={{0}: (4, {}), {1}: (5, {}), {2}: (6, {})} | custom-call | tf_op jit(solution)/shard_map/scale_other/pallas_call | solution.py:336
  (39 shorter events, 6.9 us)
Async XLA Ops:
  0.6 1.0 %copy-start = (bf16[1,2,256,256]{3,2,1,0:T(8,128)(2,1)S(1)}, bf16[1,2,256,256]{3,2,1,0:T(8,128)(2,1)}, u32[]{:S(2)}) copy-start(bf16[1,2,256,256]{3,2,1,0:T(8,128)(2,1)} %param.8) | copy-start | bytes 786436
  1.6 1.0 %copy-start.2 = (bf16[2,6,128,128]{3,2,1,0:T(8,128)(2,1)S(1)}, bf16[2,6,128,128]{3,2,1,0:T(8,128)(2,1)}, u32[]{:S(2)}) copy-start(bf16[2,6,128,128]{3,2,1,0:T(8,128)(2,1)} %adj_hbm.3) | copy-start | bytes 1179652
  3.3 7.3 %copy-start.1 = (bf16[1,2,256,256]{3,2,1,0:T(8,128)(2,1)S(1)}, bf16[1,2,256,256]{3,2,1,0:T(8,128)(2,1)}, u32[]{:S(2)}) copy-start(bf16[1,2,256,256]{3,2,1,0:T(8,128)(2,1)} %param.8) | copy-start | bytes 786436
  3.3 7.3 %copy-start.3 = (bf16[2,6,128,128]{3,2,1,0:T(8,128)(2,1)S(1)}, bf16[2,6,128,128]{3,2,1,0:T(8,128)(2,1)}, u32[]{:S(2)}) copy-start(bf16[2,6,128,128]{3,2,1,0:T(8,128)(2,1)} %adj_hbm.3) | copy-start | bytes 1179652
  4.9 14.1 %collective-permute-start = (bf16[2,128,256]{2,1,0:T(8,128)(2,1)S(1)}, bf16[2,128,256]{2,1,0:T(8,128)(2,1)S(1)}, u32[]{:S(2)}, u32[]{:S(2)}) collective-permute-start(bf16[2,128,256]{2,1,0:T(8,128)(2,1)S(1)} %get-tuple-element.40), channel_id=1, source_target_pairs={{0,2},{1,3},{2,0},{3,1},{4,6},{5,7},{6,4},{7,5},{8,10},{9,11},{10,... | collective-permute-start | bytes 393224 | tf_op jit(solution)/shard_map/ppermute | solution.py:281
  9.0 10.0 %collective-permute-start.1 = (bf16[2,128,256]{2,1,0:T(8,128)(2,1)S(1)}, bf16[2,128,256]{2,1,0:T(8,128)(2,1)S(1)}, u32[]{:S(2)}, u32[]{:S(2)}) collective-permute-start(bf16[2,128,256]{2,1,0:T(8,128)(2,1)S(1)} %get-tuple-element.41), channel_id=1, source_target_pairs={{0,3},{1,2},{2,1},{3,0},{4,7},{5,6},{6,5},{7,4},{8,11},{9,10},{10,... | collective-permute-start | bytes 393224 | tf_op jit(solution)/shard_map/ppermute | solution.py:281
  10.3 9.1 %collective-permute-start.2 = (bf16[2,128,256]{2,1,0:T(8,128)(2,1)S(1)}, bf16[2,128,256]{2,1,0:T(8,128)(2,1)S(1)}, u32[]{:S(2)}, u32[]{:S(2)}) collective-permute-start(bf16[2,128,256]{2,1,0:T(8,128)(2,1)S(1)} %get-tuple-element.42), channel_id=1, source_target_pairs={{0,1},{1,0},{2,3},{3,2},{4,5},{5,4},{6,7},{7,6},{8,9},{9,8},{10,11... | collective-permute-start | bytes 393224 | tf_op jit(solution)/shard_map/ppermute | solution.py:281
  10.6 1.0 %copy-start.4 = (bf16[2,256,256]{2,1,0:T(8,128)(2,1)S(1)}, bf16[2,256,256]{2,1,0:T(8,128)(2,1)}, u32[]{:S(2)}) copy-start(bf16[2,256,256]{2,1,0:T(8,128)(2,1)} %wf_ref.1) | copy-start | bytes 786436
  11.5 0.9 %copy-start.6 = (bf16[2,256,256]{2,1,0:T(8,128)(2,1)S(1)}, bf16[2,256,256]{2,1,0:T(8,128)(2,1)}, u32[]{:S(2)}) copy-start(bf16[2,256,256]{2,1,0:T(8,128)(2,1)} %wg_ref.1) | copy-start | bytes 786436
  19.5 1.0 %copy-start.5 = (bf16[2,256,256]{2,1,0:T(8,128)(2,1)S(1)}, bf16[2,256,256]{2,1,0:T(8,128)(2,1)}, u32[]{:S(2)}) copy-start(bf16[2,256,256]{2,1,0:T(8,128)(2,1)} %wf_ref.1) | copy-start | bytes 786436
  20.1 1.8 %collective-permute-start.3 = (bf16[3,256,256]{2,1,0:T(8,128)(2,1)S(1)}, bf16[3,256,256]{2,1,0:T(8,128)(2,1)S(1)}, u32[]{:S(2)}, u32[]{:S(2)}) collective-permute-start(bf16[3,256,256]{2,1,0:T(8,128)(2,1)S(1)} %get-tuple-element.47), channel_id=1, source_target_pairs={{0,4},{4,0},{8,12},{12,8},{16,20},{20,16},{24,28},{28,24},{1,5},{5... | collective-permute-start | bytes 1179656 | tf_op jit(solution)/shard_map/ppermute | solution.py:304
  22.0 4.7 %collective-permute-start.4 = (bf16[3,64,256]{2,1,0:T(8,128)(2,1)S(1)}, bf16[3,64,256]{2,1,0:T(8,128)(2,1)S(1)}, u32[]{:S(2)}, u32[]{:S(2)}) collective-permute-start(bf16[3,64,256]{2,1,0:T(8,128)(2,1)S(1)} %get-tuple-element.49), channel_id=1, source_target_pairs={{0,8},{1,9},{2,10},{3,11},{4,5},{5,4},{6,7},{7,6},{8,0},{9,1},{10,... | collective-permute-start | bytes 294920 | tf_op jit(solution)/shard_map/ppermute | solution.py:326
  23.6 4.6 %collective-permute-start.5 = (bf16[3,64,256]{2,1,0:T(8,128)(2,1)S(1)}, bf16[3,64,256]{2,1,0:T(8,128)(2,1)S(1)}, u32[]{:S(2)}, u32[]{:S(2)}) collective-permute-start(bf16[3,64,256]{2,1,0:T(8,128)(2,1)S(1)} %get-tuple-element.50), channel_id=1, source_target_pairs={{0,16},{1,17},{2,18},{3,19},{4,6},{5,7},{6,4},{7,5},{8,24},{9,25},... | collective-permute-start | bytes 294920 | tf_op jit(solution)/shard_map/ppermute | solution.py:326
  25.1 5.5 %collective-permute-start.6 = (bf16[3,64,256]{2,1,0:T(8,128)(2,1)S(1)}, bf16[3,64,256]{2,1,0:T(8,128)(2,1)S(1)}, u32[]{:S(2)}, u32[]{:S(2)}) collective-permute-start(bf16[3,64,256]{2,1,0:T(8,128)(2,1)S(1)} %get-tuple-element.51), channel_id=1, source_target_pairs={{0,24},{1,25},{2,26},{3,27},{4,7},{5,6},{6,5},{7,4},{8,16},{9,17},... | collective-permute-start | bytes 294920 | tf_op jit(solution)/shard_map/ppermute | solution.py:326
  30.7 6.6 %collective-permute-start.9 = (bf16[3,64,256]{2,1,0:T(8,128)(2,1)S(1)}, bf16[3,64,256]{2,1,0:T(8,128)(2,1)S(1)}, u32[]{:S(2)}, u32[]{:S(2)}) collective-permute-start(bf16[3,64,256]{2,1,0:T(8,128)(2,1)S(1)} %add_first.1.refs_0_), channel_id=1, source_target_pairs={{0,3},{1,2},{2,1},{3,0},{4,28},{5,29},{6,30},{7,31},{8,11},{9,10},... | collective-permute-start | bytes 294920 | tf_op jit(solution)/shard_map/ppermute | solution.py:328
  34.2 6.6 %collective-permute-start.8 = (bf16[3,64,256]{2,1,0:T(8,128)(2,1)S(1)}, bf16[3,64,256]{2,1,0:T(8,128)(2,1)S(1)}, u32[]{:S(2)}, u32[]{:S(2)}) collective-permute-start(bf16[3,64,256]{2,1,0:T(8,128)(2,1)S(1)} %add_first.1.refs_0_), channel_id=1, source_target_pairs={{0,2},{1,3},{2,0},{3,1},{4,20},{5,21},{6,22},{7,23},{8,10},{9,11},... | collective-permute-start | bytes 294920 | tf_op jit(solution)/shard_map/ppermute | solution.py:328
  34.9 5.9 %collective-permute-start.7 = (bf16[3,64,256]{2,1,0:T(8,128)(2,1)S(1)}, bf16[3,64,256]{2,1,0:T(8,128)(2,1)S(1)}, u32[]{:S(2)}, u32[]{:S(2)}) collective-permute-start(bf16[3,64,256]{2,1,0:T(8,128)(2,1)S(1)} %add_first.1.refs_0_), channel_id=1, source_target_pairs={{0,1},{1,0},{2,3},{3,2},{4,12},{5,13},{6,14},{7,15},{8,9},{9,8},{1... | collective-permute-start | bytes 294920 | tf_op jit(solution)/shard_map/ppermute | solution.py:328
  40.8 5.7 %collective-permute-start.15 = (bf16[3,64,256]{2,1,0:T(8,128)(2,1)S(1)}, bf16[3,64,256]{2,1,0:T(8,128)(2,1)S(1)}, u32[]{:S(2)}, u32[]{:S(2)}) collective-permute-start(bf16[3,64,256]{2,1,0:T(8,128)(2,1)S(1)} %add_second.1.refs_0_), channel_id=1, source_target_pairs={{0,24},{1,25},{2,26},{3,27},{4,7},{5,6},{6,5},{7,4},{8,16},{9,17},... | collective-permute-start | bytes 294920 | tf_op jit(solution)/shard_map/ppermute | solution.py:330
  41.4 5.7 %collective-permute-start.13 = (bf16[3,64,256]{2,1,0:T(8,128)(2,1)S(1)}, bf16[3,64,256]{2,1,0:T(8,128)(2,1)S(1)}, u32[]{:S(2)}, u32[]{:S(2)}) collective-permute-start(bf16[3,64,256]{2,1,0:T(8,128)(2,1)S(1)} %add_second.1.refs_0_), channel_id=1, source_target_pairs={{0,16},{1,17},{2,18},{3,19},{4,6},{5,7},{6,4},{7,5},{8,24},{9,25},... | collective-permute-start | bytes 294920 | tf_op jit(solution)/shard_map/ppermute | solution.py:330
  42.9 4.6 %collective-permute-start.11 = (bf16[3,64,256]{2,1,0:T(8,128)(2,1)S(1)}, bf16[3,64,256]{2,1,0:T(8,128)(2,1)S(1)}, u32[]{:S(2)}, u32[]{:S(2)}) collective-permute-start(bf16[3,64,256]{2,1,0:T(8,128)(2,1)S(1)} %add_second.1.refs_0_), channel_id=1, source_target_pairs={{0,8},{1,9},{2,10},{3,11},{4,5},{5,4},{6,7},{7,6},{8,0},{9,1},{10,... | collective-permute-start | bytes 294920 | tf_op jit(solution)/shard_map/ppermute | solution.py:330
  44.4 4.2 %collective-permute-start.10 = (bf16[3,64,256]{2,1,0:T(8,128)(2,1)S(1)}, bf16[3,64,256]{2,1,0:T(8,128)(2,1)S(1)}, u32[]{:S(2)}, u32[]{:S(2)}) collective-permute-start(bf16[3,64,256]{2,1,0:T(8,128)(2,1)S(1)} %add_second.1.refs_0_), channel_id=1, source_target_pairs={{0,4},{4,0},{8,12},{12,8},{16,20},{20,16},{24,28},{28,24},{1,5},{5... | collective-permute-start | bytes 294920 | tf_op jit(solution)/shard_map/ppermute | solution.py:331
  46.5 2.0 %collective-permute-start.16 = (bf16[3,64,256]{2,1,0:T(8,128)(2,1)S(1)}, bf16[3,64,256]{2,1,0:T(8,128)(2,1)S(1)}, u32[]{:S(2)}, u32[]{:S(2)}) collective-permute-start(bf16[3,64,256]{2,1,0:T(8,128)(2,1)S(1)} %collective-permute-done.15.refs_3_), channel_id=1, source_target_pairs={{0,4},{4,0},{8,12},{12,8},{16,20},{20,16},{24,28},{28,24},{1,5},{5... | collective-permute-start | bytes 294920 | tf_op jit(solution)/shard_map/ppermute | solution.py:331
  47.1 1.5 %collective-permute-start.14 = (bf16[3,64,256]{2,1,0:T(8,128)(2,1)S(1)}, bf16[3,64,256]{2,1,0:T(8,128)(2,1)S(1)}, u32[]{:S(2)}, u32[]{:S(2)}) collective-permute-start(bf16[3,64,256]{2,1,0:T(8,128)(2,1)S(1)} %collective-permute-done.13.refs_2_), channel_id=1, source_target_pairs={{0,4},{4,0},{8,12},{12,8},{16,20},{20,16},{24,28},{28,24},{1,5},{5... | collective-permute-start | bytes 294920 | tf_op jit(solution)/shard_map/ppermute | solution.py:331
  47.5 1.3 %collective-permute-start.12 = (bf16[3,64,256]{2,1,0:T(8,128)(2,1)S(1)}, bf16[3,64,256]{2,1,0:T(8,128)(2,1)S(1)}, u32[]{:S(2)}, u32[]{:S(2)}) collective-permute-start(bf16[3,64,256]{2,1,0:T(8,128)(2,1)S(1)} %collective-permute-done.11.refs_1_), channel_id=1, source_target_pairs={{0,4},{4,0},{8,12},{12,8},{16,20},{20,16},{24,28},{28,24},{1,5},{5... | collective-permute-start | bytes 294920 | tf_op jit(solution)/shard_map/ppermute | solution.py:331
  (3 other events, 2.6 us)

commit v3 on v2

--- a/solution.py
+++ b/solution.py
@@ -34,6 +34,10 @@
     )
 
 
+def in_hbm(*arrays):
+    return [pltpu.with_memory_space_constraint(array, pltpu.HBM) for array in arrays]
+
+
 def fetch(pairs, sems):
     copies = [pltpu.make_async_copy(src, dst, sems.at[i]) for i, (src, dst) in enumerate(pairs)]
     for copy in copies:
@@ -70,28 +74,21 @@
     me = region_of()
     tiles, per_tile = adj_ref.shape[:2]
     total = cot_ref.shape[0]
-    first, *copies = fetch(
-        [(nb_hbm, nb_ref)]
-        + [(cot_hbm.at[t], cot_ref.at[t]) for t in range(total)]
-        + [(adj_hbm.at[j], adj_ref.at[j]) for j in range(tiles)],
-        sems,
-    )
+    parts = [(nb_hbm, nb_ref)]
+    for j in range(tiles):
+        rows = pl.ds(j * TILE, TILE)
+        parts += [(cot_hbm.at[t, rows], cot_ref.at[t, rows]) for t in range(total)]
+        parts += [(adj_hbm.at[j, pl.ds(k, 2)], adj_ref.at[j, pl.ds(k, 2)]) for k in range(0, per_tile, 2)]
+    first, *copies = fetch(parts, sems)
     first.wait()
     found = [find_entry(nb_ref, me, jnp.bitwise_xor(me, p), tiles, per_tile) for p in order]
     for copy in copies:
         copy.wait()
-    for out, (tile, place, named) in zip(out_refs, found):
-
-        @pl.when(named >= 0)
-        def _():
-            weights = adj_ref[tile, place]
-            for t in range(total):
-                rows = cot_ref[t, pl.ds(pl.multiple_of(tile * TILE, TILE), TILE), :]
-                out[t] = dot(weights, rows, 0, 0).astype(BF16)
-
-        @pl.when(named < 0)
-        def _():
-            out[...] = jnp.zeros_like(out)
+    for out, (tile, place, _) in zip(out_refs, found):
+        weights = adj_ref[tile, place]
+        for t in range(total):
+            rows = cot_ref[t, pl.ds(pl.multiple_of(tile * TILE, TILE), TILE), :]
+            out[t] = dot(weights, rows, 0, 0).astype(BF16)
 
 
 def local_body(
@@ -265,7 +262,7 @@
     cot = cotangent.reshape(total, sites, chans)
     shape = jax.ShapeDtypeStruct
     block = total * sites * chans
-    order = sorted(range(1, regions), key=lambda p: p < regions // 2)
+    order = sorted(range(1, regions), reverse=True)
     dma = pltpu.SemaphoreType.DMA
 
     outgoing = call(
@@ -273,10 +270,10 @@
         [shape((total, TILE, chans), BF16)] * (regions - 1), [HB] * 3, "outgoing",
         scratch=[
             pltpu.SMEM(neighbours.shape, jnp.int32), pltpu.VMEM(cot.shape, BF16), pltpu.VMEM(adjacency.shape, BF16),
-            dma((1 + total + tiles,)),
+            dma((1 + tiles * (total + per_tile // 2),)),
         ],
         flops=2 * (regions - 1) * total * TILE * TILE * chans, nbytes=4 * block,
-    )(neighbours, cot, adjacency)
+    )(*in_hbm(neighbours, cot, adjacency))
     arrived = [
         lax.ppermute(part, "region", [(r, r ^ p) for r in range(regions)]) for p, part in zip(order, outgoing)
     ]
@@ -293,7 +290,7 @@
             pltpu.VMEM(adjacency.shape, BF16), dma((7,)),
         ],
         flops=14 * block * chans, nbytes=30 * block,
-    )(neighbours, x, cot, w_filter, w_gate, w_mix, adjacency)
+    )(*in_hbm(neighbours, x, cot, w_filter, w_gate, w_mix, adjacency))
     act_cot, sums, send = call(
         functools.partial(send_body, regions, steps),
         [shape((2,) + x.shape, BF16), shape(x.shape, BF16), shape((3, chans, chans), BF16)],

time: 50.2 us -> 48.1 us (0.958)
  local copies, waits for them, and re-layouts: 6.66 us -> 0.39 us
  waiting for transfers between devices: 15.7 us -> 18.8 us
  Pallas kernels: 9.06 us -> 9.78 us
    unnamed x20 -> x6, local copies, waits for them, and re-layouts: 6.66 us -> 0.39 us
    ppermute x3, waiting for transfers between devices: 1.82 us -> 6.31 us  [per_device(): lax.ppermute(part, 'region', [(r, r ^ p) for r in range(regions)])]
    ppermute x3, waiting for transfers between devices: 3.12 us -> 2.25 us  [per_device(): lax.ppermute(done, BOTH, pairs(p, True))]
    pallas_call x1, Pallas kernels: 3.28 us -> 4.11 us  [per_device(): call(functools.partial(local_body, steps, order), [shape(x.shape, F32)] *...]
  transfers between devices with their start and end apart: 17 -> 17, of which waited for: 12 -> 9; matrix products, arithmetic and copies ran while one was open for 0% -> 0% of each run, Pallas kernels for 11% -> 14%
where the time goes in v3:
time: 48.1 us; the launch traced here: 47.6 us
  waiting for transfers between devices  18.8 us (39%)
  starting transfers between devices  17.9 us (37%)
  Pallas kernels  9.78 us (20%)
  between operations  0.74 us (2%)
    ppermute x3, waiting for transfers between devices, per_device(): lax.ppermute(part, 'region', [(r, r ^ p) for r in range(regions)])  6.31 us
    ppermute x3, starting transfers between devices, per_device(): lax.ppermute(part, 'region', [(r, r ^ p) for r in range(regions)])  5.76 us
    ppermute x3, waiting for transfers between devices, per_device(): lax.ppermute(part, BOTH, pairs(p, True))  5.04 us
    ppermute x3, waiting for transfers between devices, per_device(): gots = [lax.ppermute(mine, BOTH, pairs(p, False)) for p in range(1, ways)]  5.03 us
    ppermute x3, starting transfers between devices, per_device(): gots = [lax.ppermute(mine, BOTH, pairs(p, False)) for p in range(1, ways)]  4.45 us
    pallas_call x1, Pallas kernels, per_device(): call(functools.partial(local_body, steps, order), [shape(x.shape, F32)] *...  4.11 us
    ppermute x3, starting transfers between devices, per_device(): lax.ppermute(part, BOTH, pairs(p, True))  3.55 us
    ppermute x3, starting transfers between devices, per_device(): lax.ppermute(done, BOTH, pairs(p, True))  3.55 us
  transfers between devices with their start and end apart: 17, of which 9 were waited for; matrix products, arithmetic and copies ran while one was open for 0% of the time, Pallas kernels for 14%

profile of v3, /device:TPU:0, one launch (start us, length us, event | category | flops | bytes accessed | tf_op | source)
XLA Modules:
  0.0 47.6 jit_solution(6017686208338102892)
XLA Ops:
  0.6 1.5 %outgoing.1 = (bf16[2,128,256]{2,1,0:T(8,128)(2,1)S(1)}, bf16[2,128,256]{2,1,0:T(8,128)(2,1)S(1)}, bf16[2,128,256]{2,1,0:T(8,128)(2,1)S(1)}) custom-call(s32[8,6]{1,0:T(8,128)} %nb_hbm.3, bf16[2,256,256]{2,1,0:T(8,128)(2,1)} %bitcast.3, bf16[2,6,128,128]{3,2,1,0:T(8,128)(2,1)} %adj_hbm.3), custom_call_target="tpu_custom_call" | custom-call | flops 50331648 | bytes 524288 | tf_op jit(solution)/shard_map/outgoing/pallas_call | solution.py:268
  2.1 5.1 %collective-permute-start = (bf16[2,128,256]{2,1,0:T(8,128)(2,1)S(1)}, bf16[2,128,256]{2,1,0:T(8,128)(2,1)S(1)}, u32[]{:S(2)}, u32[]{:S(2)}) collective-permute-start(bf16[2,128,256]{2,1,0:T(8,128)(2,1)S(1)} %get-tuple-element.40), channel_id=1, source_target_pairs={{0,3},{1,2},{2,1},{3,0},{4,7},{5,6},{6,5},{7,4},{8,11},{9,10},{10,... | collective-permute-start | bytes 393224 | tf_op jit(solution)/shard_map/ppermute | solution.py:278
  7.3 0.6 %collective-permute-start.2 = (bf16[2,128,256]{2,1,0:T(8,128)(2,1)S(1)}, bf16[2,128,256]{2,1,0:T(8,128)(2,1)S(1)}, u32[]{:S(2)}, u32[]{:S(2)}) collective-permute-start(bf16[2,128,256]{2,1,0:T(8,128)(2,1)S(1)} %get-tuple-element.42), channel_id=1, source_target_pairs={{0,1},{1,0},{2,3},{3,2},{4,5},{5,4},{6,7},{7,6},{8,9},{9,8},{10,11... | collective-permute-start | bytes 393224 | tf_op jit(solution)/shard_map/ppermute | solution.py:278
  7.9 4.1 %local.1 = (f32[2,256,256]{2,1,0:T(8,128)S(1)}, f32[2,256,256]{2,1,0:T(8,128)S(1)}, f32[2,256,256]{2,1,0:T(8,128)S(1)}, f32[2,256,256]{2,1,0:T(8,128)S(1)}, f32[...) custom-call(s32[8,6]{1,0:T(8,128)} %nb_hbm.3, ...), custom_call_target="tpu_custom_call" | custom-call | flops 469762048 | bytes 3932160 | tf_op jit(solution)/shard_map/local/pallas_call | solution.py:282
  12.0 6.3 %collective-permute-done.1.refs_1_ = bf16[2,128,256]{2,1,0:T(8,128)(2,1)S(1)} collective-permute-done((bf16[2,128,256]{2,1,0:T(8,128)(2,1)S(1)}, bf16[2,128,256]{2,1,0:T(8,128)(2,1)S(1)}, u32[]{:S(2)}, u32[]{:S(2)}) %collective-permute-start.1) | collective-permute-done | bytes 131104 | tf_op jit(solution)/shard_map/ppermute | solution.py:278
  18.3 0.6 %send.1 = (bf16[2,2,256,256]{3,2,1,0:T(8,128)(2,1)S(1)}, bf16[2,256,256]{2,1,0:T(8,128)(2,1)S(1)}, bf16[3,256,256]{2,1,0:T(8,128)(2,1)S(1)}) custom-call(f32[2,256,256]{2,1,0:T(8,128)S(1)} %get-tuple-element.34.df_ref, f32[2,256,256]{2,1,0:T(8,128)S(1)} %get-tuple-element.35.dg_ref, f32[2,256,256]{2,1,0:T(8,128)S(1)} %get-tuple-element.36.direct_ref, ...), custom_call_target="tpu_custom_call" | custom-call | flops 201326592 | bytes 3932160 | tf_op jit(solution)/shard_map/send/pallas_call | solution.py:294
  19.1 0.2 copy-done
  19.4 1.4 %keep.1 = (f32[3,256,256]{2,1,0:T(8,128)S(1)}, bf16[2,256,256]{2,1,0:T(8,128)(2,1)}) custom-call(f32[256,256]{1,0:T(8,128)S(1)} %get-tuple-element.31.mix_ref, bf16[2,256,256]{2,1,0:T(8,128)(2,1)S(1)} %get-tuple-element.32.xt_ref, bf16[2,256,256]{2,1,0:T(8,128)(2,1)S(1)} %get-tuple-element.33.ht_ref, bf16[2,2,256,256]{3,2,1,0:T(8,128)(2,1)S(1)} %get-tuple-element.43.act_ref, ...), custom_call_target="tpu_custom_call" | custom-call | flops 402653184 | bytes 3932160 | tf_op jit(solution)/shard_map/keep/pallas_call | solution.py:302
  20.9 1.6 %collective-permute-start.4 = (bf16[3,64,256]{2,1,0:T(8,128)(2,1)S(1)}, bf16[3,64,256]{2,1,0:T(8,128)(2,1)S(1)}, u32[]{:S(2)}, u32[]{:S(2)}) collective-permute-start(bf16[3,64,256]{2,1,0:T(8,128)(2,1)S(1)} %get-tuple-element.49), channel_id=1, source_target_pairs={{0,8},{1,9},{2,10},{3,11},{4,5},{5,4},{6,7},{7,6},{8,0},{9,1},{10,... | collective-permute-start | bytes 294920 | tf_op jit(solution)/shard_map/ppermute | solution.py:323
  22.5 1.5 %collective-permute-start.5 = (bf16[3,64,256]{2,1,0:T(8,128)(2,1)S(1)}, bf16[3,64,256]{2,1,0:T(8,128)(2,1)S(1)}, u32[]{:S(2)}, u32[]{:S(2)}) collective-permute-start(bf16[3,64,256]{2,1,0:T(8,128)(2,1)S(1)} %get-tuple-element.50), channel_id=1, source_target_pairs={{0,16},{1,17},{2,18},{3,19},{4,6},{5,7},{6,4},{7,5},{8,24},{9,25},... | collective-permute-start | bytes 294920 | tf_op jit(solution)/shard_map/ppermute | solution.py:323
  24.0 0.5 collective-permute-start.6
  24.5 1.1 %collective-permute-done.4.refs_1_ = bf16[3,64,256]{2,1,0:T(8,128)(2,1)S(1)} collective-permute-done((bf16[3,64,256]{2,1,0:T(8,128)(2,1)S(1)}, bf16[3,64,256]{2,1,0:T(8,128)(2,1)S(1)}, u32[]{:S(2)}, u32[]{:S(2)}) %collective-permute-start.4) | collective-permute-done | bytes 98336 | tf_op jit(solution)/shard_map/ppermute | solution.py:323
  25.6 1.5 %collective-permute-done.5.refs_2_ = bf16[3,64,256]{2,1,0:T(8,128)(2,1)S(1)} collective-permute-done((bf16[3,64,256]{2,1,0:T(8,128)(2,1)S(1)}, bf16[3,64,256]{2,1,0:T(8,128)(2,1)S(1)}, u32[]{:S(2)}, u32[]{:S(2)}) %collective-permute-start.5) | collective-permute-done | bytes 98336 | tf_op jit(solution)/shard_map/ppermute | solution.py:323
  27.1 2.4 %collective-permute-done.6.refs_3_ = bf16[3,64,256]{2,1,0:T(8,128)(2,1)S(1)} collective-permute-done((bf16[3,64,256]{2,1,0:T(8,128)(2,1)S(1)}, bf16[3,64,256]{2,1,0:T(8,128)(2,1)S(1)}, u32[]{:S(2)}, u32[]{:S(2)}) %collective-permute-start.6) | collective-permute-done | bytes 98336 | tf_op jit(solution)/shard_map/ppermute | solution.py:323
  29.6 2.5 %collective-permute-start.9 = (bf16[3,64,256]{2,1,0:T(8,128)(2,1)S(1)}, bf16[3,64,256]{2,1,0:T(8,128)(2,1)S(1)}, u32[]{:S(2)}, u32[]{:S(2)}) collective-permute-start(bf16[3,64,256]{2,1,0:T(8,128)(2,1)S(1)} %add_first.1.refs_0_), channel_id=1, source_target_pairs={{0,3},{1,2},{2,1},{3,0},{4,28},{5,29},{6,30},{7,31},{8,11},{9,10},... | collective-permute-start | bytes 294920 | tf_op jit(solution)/shard_map/ppermute | solution.py:325
  32.1 1.9 %collective-permute-start.7 = (bf16[3,64,256]{2,1,0:T(8,128)(2,1)S(1)}, bf16[3,64,256]{2,1,0:T(8,128)(2,1)S(1)}, u32[]{:S(2)}, u32[]{:S(2)}) collective-permute-start(bf16[3,64,256]{2,1,0:T(8,128)(2,1)S(1)} %add_first.1.refs_0_), channel_id=1, source_target_pairs={{0,1},{1,0},{2,3},{3,2},{4,12},{5,13},{6,14},{7,15},{8,9},{9,8},{1... | collective-permute-start | bytes 294920 | tf_op jit(solution)/shard_map/ppermute | solution.py:325
  34.0 2.1 %collective-permute-done.9.refs_3_ = bf16[3,64,256]{2,1,0:T(8,128)(2,1)S(1)} collective-permute-done((bf16[3,64,256]{2,1,0:T(8,128)(2,1)S(1)}, bf16[3,64,256]{2,1,0:T(8,128)(2,1)S(1)}, u32[]{:S(2)}, u32[]{:S(2)}) %collective-permute-start.9) | collective-permute-done | bytes 98336 | tf_op jit(solution)/shard_map/ppermute | solution.py:325
  36.1 3.0 %collective-permute-done.8.refs_2_ = bf16[3,64,256]{2,1,0:T(8,128)(2,1)S(1)} collective-permute-done((bf16[3,64,256]{2,1,0:T(8,128)(2,1)S(1)}, bf16[3,64,256]{2,1,0:T(8,128)(2,1)S(1)}, u32[]{:S(2)}, u32[]{:S(2)}) %collective-permute-start.8) | collective-permute-done | bytes 98336 | tf_op jit(solution)/shard_map/ppermute | solution.py:325
  39.2 1.3 %collective-permute-start.13 = (bf16[3,64,256]{2,1,0:T(8,128)(2,1)S(1)}, bf16[3,64,256]{2,1,0:T(8,128)(2,1)S(1)}, u32[]{:S(2)}, u32[]{:S(2)}) collective-permute-start(bf16[3,64,256]{2,1,0:T(8,128)(2,1)S(1)} %add_second.1.refs_0_), channel_id=1, source_target_pairs={{0,16},{1,17},{2,18},{3,19},{4,6},{5,7},{6,4},{7,5},{8,24},{9,25},... | collective-permute-start | bytes 294920 | tf_op jit(solution)/shard_map/ppermute | solution.py:327
  40.5 2.1 %collective-permute-start.11 = (bf16[3,64,256]{2,1,0:T(8,128)(2,1)S(1)}, bf16[3,64,256]{2,1,0:T(8,128)(2,1)S(1)}, u32[]{:S(2)}, u32[]{:S(2)}) collective-permute-start(bf16[3,64,256]{2,1,0:T(8,128)(2,1)S(1)} %add_second.1.refs_0_), channel_id=1, source_target_pairs={{0,8},{1,9},{2,10},{3,11},{4,5},{5,4},{6,7},{7,6},{8,0},{9,1},{10,... | collective-permute-start | bytes 294920 | tf_op jit(solution)/shard_map/ppermute | solution.py:327
  42.7 2.1 %collective-permute-done.15.refs_3_ = bf16[3,64,256]{2,1,0:T(8,128)(2,1)S(1)} collective-permute-done((bf16[3,64,256]{2,1,0:T(8,128)(2,1)S(1)}, bf16[3,64,256]{2,1,0:T(8,128)(2,1)S(1)}, u32[]{:S(2)}, u32[]{:S(2)}) %collective-permute-start.15) | collective-permute-done | bytes 98336 | tf_op jit(solution)/shard_map/ppermute | solution.py:327
  44.9 0.4 collective-permute-start.14
  45.5 1.0 %scale_own.1 = (f32[2,256,256]{2,1,0:T(8,128)}, f32[2,256,256]{2,1,0:T(8,128)}, f32[2,256,256]{2,1,0:T(8,128)}) custom-call(bf16[3,64,256]{2,1,0:T(8,128)(2,1)S(1)} %add_second.1.refs_0_, bf16[3,64,256]{2,1,0:T(8,128)(2,1)S(1)} %collective-permute-done.11.refs_1_, bf16[3,64,256]{2,1,0:T(8,128)(2,1)S(1)} %collective-permute-done.13.refs_2_, ...), custom_call_target="tpu_custom_call" | custom-call | tf_op jit(solution)/shard_map/scale_own/pallas_call | solution.py:332
  46.6 1.0 %scale_other.1 = (f32[2,256,256]{2,1,0:T(8,128)}, f32[2,256,256]{2,1,0:T(8,128)}, f32[2,256,256]{2,1,0:T(8,128)}) custom-call(bf16[3,64,256]{2,1,0:T(8,128)(2,1)S(1)} %collective-permute-done.10.refs_0_, bf16[3,64,256]{2,1,0:T(8,128)(2,1)S(1)} %collective-permute-done.12.refs_1_, ...), custom_call_target="tpu_custom_call", output_to_operand_aliasing={{0}: (4, {}), {1}: (5, {}), {2}: (6, {})} | custom-call | tf_op jit(solution)/shard_map/scale_other/pallas_call | solution.py:333
  (25 shorter events, 0.9 us)
Async XLA Ops:
  2.1 9.9 %collective-permute-start = (bf16[2,128,256]{2,1,0:T(8,128)(2,1)S(1)}, bf16[2,128,256]{2,1,0:T(8,128)(2,1)S(1)}, u32[]{:S(2)}, u32[]{:S(2)}) collective-permute-start(bf16[2,128,256]{2,1,0:T(8,128)(2,1)S(1)} %get-tuple-element.40), channel_id=1, source_target_pairs={{0,3},{1,2},{2,1},{3,0},{4,7},{5,6},{6,5},{7,4},{8,11},{9,10},{10,... | collective-permute-start | bytes 393224 | tf_op jit(solution)/shard_map/ppermute | solution.py:278
  7.3 11.1 %collective-permute-start.1 = (bf16[2,128,256]{2,1,0:T(8,128)(2,1)S(1)}, bf16[2,128,256]{2,1,0:T(8,128)(2,1)S(1)}, u32[]{:S(2)}, u32[]{:S(2)}) collective-permute-start(bf16[2,128,256]{2,1,0:T(8,128)(2,1)S(1)} %get-tuple-element.41), channel_id=1, source_target_pairs={{0,2},{1,3},{2,0},{3,1},{4,6},{5,7},{6,4},{7,5},{8,10},{9,11},{10,... | collective-permute-start | bytes 393224 | tf_op jit(solution)/shard_map/ppermute | solution.py:278
  7.3 11.1 %collective-permute-start.2 = (bf16[2,128,256]{2,1,0:T(8,128)(2,1)S(1)}, bf16[2,128,256]{2,1,0:T(8,128)(2,1)S(1)}, u32[]{:S(2)}, u32[]{:S(2)}) collective-permute-start(bf16[2,128,256]{2,1,0:T(8,128)(2,1)S(1)} %get-tuple-element.42), channel_id=1, source_target_pairs={{0,1},{1,0},{2,3},{3,2},{4,5},{5,4},{6,7},{7,6},{8,9},{9,8},{10,11... | collective-permute-start | bytes 393224 | tf_op jit(solution)/shard_map/ppermute | solution.py:278
  18.3 1.0 %copy-start = (bf16[1,2,256,256]{3,2,1,0:T(8,128)(2,1)S(1)}, bf16[1,2,256,256]{3,2,1,0:T(8,128)(2,1)}, u32[]{:S(2)}) copy-start(bf16[1,2,256,256]{3,2,1,0:T(8,128)(2,1)} %param.8) | copy-start | bytes 786436
  18.3 1.0 %copy-start.1 = (bf16[2,256,256]{2,1,0:T(8,128)(2,1)S(1)}, bf16[2,256,256]{2,1,0:T(8,128)(2,1)}, u32[]{:S(2)}) copy-start(bf16[2,256,256]{2,1,0:T(8,128)(2,1)} %wf_ref.1) | copy-start | bytes 786436
  18.3 1.1 %copy-start.2 = (bf16[2,256,256]{2,1,0:T(8,128)(2,1)S(1)}, bf16[2,256,256]{2,1,0:T(8,128)(2,1)}, u32[]{:S(2)}) copy-start(bf16[2,256,256]{2,1,0:T(8,128)(2,1)} %wg_ref.1) | copy-start | bytes 786436
  19.0 1.9 %collective-permute-start.3 = (bf16[3,256,256]{2,1,0:T(8,128)(2,1)S(1)}, bf16[3,256,256]{2,1,0:T(8,128)(2,1)S(1)}, u32[]{:S(2)}, u32[]{:S(2)}) collective-permute-start(bf16[3,256,256]{2,1,0:T(8,128)(2,1)S(1)} %get-tuple-element.47), channel_id=1, source_target_pairs={{0,4},{4,0},{8,12},{12,8},{16,20},{20,16},{24,28},{28,24},{1,5},{5... | collective-permute-start | bytes 1179656 | tf_op jit(solution)/shard_map/ppermute | solution.py:301
  20.9 4.7 %collective-permute-start.4 = (bf16[3,64,256]{2,1,0:T(8,128)(2,1)S(1)}, bf16[3,64,256]{2,1,0:T(8,128)(2,1)S(1)}, u32[]{:S(2)}, u32[]{:S(2)}) collective-permute-start(bf16[3,64,256]{2,1,0:T(8,128)(2,1)S(1)} %get-tuple-element.49), channel_id=1, source_target_pairs={{0,8},{1,9},{2,10},{3,11},{4,5},{5,4},{6,7},{7,6},{8,0},{9,1},{10,... | collective-permute-start | bytes 294920 | tf_op jit(solution)/shard_map/ppermute | solution.py:323
  22.5 4.6 %collective-permute-start.5 = (bf16[3,64,256]{2,1,0:T(8,128)(2,1)S(1)}, bf16[3,64,256]{2,1,0:T(8,128)(2,1)S(1)}, u32[]{:S(2)}, u32[]{:S(2)}) collective-permute-start(bf16[3,64,256]{2,1,0:T(8,128)(2,1)S(1)} %get-tuple-element.50), channel_id=1, source_target_pairs={{0,16},{1,17},{2,18},{3,19},{4,6},{5,7},{6,4},{7,5},{8,24},{9,25},... | collective-permute-start | bytes 294920 | tf_op jit(solution)/shard_map/ppermute | solution.py:323
  24.0 5.5 %collective-permute-start.6 = (bf16[3,64,256]{2,1,0:T(8,128)(2,1)S(1)}, bf16[3,64,256]{2,1,0:T(8,128)(2,1)S(1)}, u32[]{:S(2)}, u32[]{:S(2)}) collective-permute-start(bf16[3,64,256]{2,1,0:T(8,128)(2,1)S(1)} %get-tuple-element.51), channel_id=1, source_target_pairs={{0,24},{1,25},{2,26},{3,27},{4,7},{5,6},{6,5},{7,4},{8,16},{9,17},... | collective-permute-start | bytes 294920 | tf_op jit(solution)/shard_map/ppermute | solution.py:323
  29.6 6.5 %collective-permute-start.9 = (bf16[3,64,256]{2,1,0:T(8,128)(2,1)S(1)}, bf16[3,64,256]{2,1,0:T(8,128)(2,1)S(1)}, u32[]{:S(2)}, u32[]{:S(2)}) collective-permute-start(bf16[3,64,256]{2,1,0:T(8,128)(2,1)S(1)} %add_first.1.refs_0_), channel_id=1, source_target_pairs={{0,3},{1,2},{2,1},{3,0},{4,28},{5,29},{6,30},{7,31},{8,11},{9,10},... | collective-permute-start | bytes 294920 | tf_op jit(solution)/shard_map/ppermute | solution.py:325
  32.1 6.9 %collective-permute-start.8 = (bf16[3,64,256]{2,1,0:T(8,128)(2,1)S(1)}, bf16[3,64,256]{2,1,0:T(8,128)(2,1)S(1)}, u32[]{:S(2)}, u32[]{:S(2)}) collective-permute-start(bf16[3,64,256]{2,1,0:T(8,128)(2,1)S(1)} %add_first.1.refs_0_), channel_id=1, source_target_pairs={{0,2},{1,3},{2,0},{3,1},{4,20},{5,21},{6,22},{7,23},{8,10},{9,11},... | collective-permute-start | bytes 294920 | tf_op jit(solution)/shard_map/ppermute | solution.py:325
  32.1 6.9 %collective-permute-start.7 = (bf16[3,64,256]{2,1,0:T(8,128)(2,1)S(1)}, bf16[3,64,256]{2,1,0:T(8,128)(2,1)S(1)}, u32[]{:S(2)}, u32[]{:S(2)}) collective-permute-start(bf16[3,64,256]{2,1,0:T(8,128)(2,1)S(1)} %add_first.1.refs_0_), channel_id=1, source_target_pairs={{0,1},{1,0},{2,3},{3,2},{4,12},{5,13},{6,14},{7,15},{8,9},{9,8},{1... | collective-permute-start | bytes 294920 | tf_op jit(solution)/shard_map/ppermute | solution.py:325
  39.1 5.7 %collective-permute-start.15 = (bf16[3,64,256]{2,1,0:T(8,128)(2,1)S(1)}, bf16[3,64,256]{2,1,0:T(8,128)(2,1)S(1)}, u32[]{:S(2)}, u32[]{:S(2)}) collective-permute-start(bf16[3,64,256]{2,1,0:T(8,128)(2,1)S(1)} %add_second.1.refs_0_), channel_id=1, source_target_pairs={{0,24},{1,25},{2,26},{3,27},{4,7},{5,6},{6,5},{7,4},{8,16},{9,17},... | collective-permute-start | bytes 294920 | tf_op jit(solution)/shard_map/ppermute | solution.py:327
  39.2 5.7 %collective-permute-start.13 = (bf16[3,64,256]{2,1,0:T(8,128)(2,1)S(1)}, bf16[3,64,256]{2,1,0:T(8,128)(2,1)S(1)}, u32[]{:S(2)}, u32[]{:S(2)}) collective-permute-start(bf16[3,64,256]{2,1,0:T(8,128)(2,1)S(1)} %add_second.1.refs_0_), channel_id=1, source_target_pairs={{0,16},{1,17},{2,18},{3,19},{4,6},{5,7},{6,4},{7,5},{8,24},{9,25},... | collective-permute-start | bytes 294920 | tf_op jit(solution)/shard_map/ppermute | solution.py:327
  40.5 4.8 %collective-permute-start.11 = (bf16[3,64,256]{2,1,0:T(8,128)(2,1)S(1)}, bf16[3,64,256]{2,1,0:T(8,128)(2,1)S(1)}, u32[]{:S(2)}, u32[]{:S(2)}) collective-permute-start(bf16[3,64,256]{2,1,0:T(8,128)(2,1)S(1)} %add_second.1.refs_0_), channel_id=1, source_target_pairs={{0,8},{1,9},{2,10},{3,11},{4,5},{5,4},{6,7},{7,6},{8,0},{9,1},{10,... | collective-permute-start | bytes 294920 | tf_op jit(solution)/shard_map/ppermute | solution.py:327
  42.7 3.8 %collective-permute-start.10 = (bf16[3,64,256]{2,1,0:T(8,128)(2,1)S(1)}, bf16[3,64,256]{2,1,0:T(8,128)(2,1)S(1)}, u32[]{:S(2)}, u32[]{:S(2)}) collective-permute-start(bf16[3,64,256]{2,1,0:T(8,128)(2,1)S(1)} %add_second.1.refs_0_), channel_id=1, source_target_pairs={{0,4},{4,0},{8,12},{12,8},{16,20},{20,16},{24,28},{28,24},{1,5},{5... | collective-permute-start | bytes 294920 | tf_op jit(solution)/shard_map/ppermute | solution.py:328
  44.8 1.6 %collective-permute-start.16 = (bf16[3,64,256]{2,1,0:T(8,128)(2,1)S(1)}, bf16[3,64,256]{2,1,0:T(8,128)(2,1)S(1)}, u32[]{:S(2)}, u32[]{:S(2)}) collective-permute-start(bf16[3,64,256]{2,1,0:T(8,128)(2,1)S(1)} %collective-permute-done.15.refs_3_), channel_id=1, source_target_pairs={{0,4},{4,0},{8,12},{12,8},{16,20},{20,16},{24,28},{28,24},{1,5},{5... | collective-permute-start | bytes 294920 | tf_op jit(solution)/shard_map/ppermute | solution.py:328
  44.9 1.5 %collective-permute-start.14 = (bf16[3,64,256]{2,1,0:T(8,128)(2,1)S(1)}, bf16[3,64,256]{2,1,0:T(8,128)(2,1)S(1)}, u32[]{:S(2)}, u32[]{:S(2)}) collective-permute-start(bf16[3,64,256]{2,1,0:T(8,128)(2,1)S(1)} %collective-permute-done.13.refs_2_), channel_id=1, source_target_pairs={{0,4},{4,0},{8,12},{12,8},{16,20},{20,16},{24,28},{28,24},{1,5},{5... | collective-permute-start | bytes 294920 | tf_op jit(solution)/shard_map/ppermute | solution.py:328
  45.3 1.3 %collective-permute-start.12 = (bf16[3,64,256]{2,1,0:T(8,128)(2,1)S(1)}, bf16[3,64,256]{2,1,0:T(8,128)(2,1)S(1)}, u32[]{:S(2)}, u32[]{:S(2)}) collective-permute-start(bf16[3,64,256]{2,1,0:T(8,128)(2,1)S(1)} %collective-permute-done.11.refs_1_), channel_id=1, source_target_pairs={{0,4},{4,0},{8,12},{12,8},{16,20},{20,16},{24,28},{28,24},{1,5},{5... | collective-permute-start | bytes 294920 | tf_op jit(solution)/shard_map/ppermute | solution.py:328

commit v4 on v3

--- a/solution.py
+++ b/solution.py
@@ -13,6 +13,7 @@
 BF16 = jnp.bfloat16
 VM = pl.BlockSpec(memory_space=pltpu.VMEM)
 HB = pl.BlockSpec(memory_space=pltpu.HBM)
+AN = pl.BlockSpec(memory_space=pl.ANY)
 BOTH = ("dp", "region")
 
 
@@ -191,7 +192,7 @@
                 send_ref[i] = part.astype(BF16)
 
 
-def keep_body(steps, mix_ref, xt_ref, ht_ref, act_ref, sums_ref, cot_ref, wf_ref, wg_ref, keep_ref, out_ref):
+def keep_body(steps, mix_ref, xt_ref, ht_ref, act_ref, sums_ref, keep_ref):
     lane, _, _ = lane_of()
     for tap in range(2):
 
@@ -200,6 +201,9 @@
             for i, part in enumerate(half_of(tap, steps, xt_ref, ht_ref, mix_ref, act_ref, sums_ref)):
                 keep_ref[i] = part
 
+
+def inputs_body(steps, act_ref, cot_ref, wf_ref, wg_ref, _, out_ref, token_ref):
+    token_ref[...] = jnp.zeros_like(token_ref)
     total = cot_ref.shape[0]
     for t in range(total):
         grad = cot_ref[t].astype(F32)
@@ -228,8 +232,8 @@
     return parts[0]
 
 
-def add_body(*refs):
-    refs[-1][...] = tree([ref[...].astype(F32) for ref in refs[:-1]]).astype(BF16)
+def add_body(ways, *refs):
+    refs[-1][...] = tree([ref[...].astype(F32) for ref in refs[:ways]]).astype(BF16)
 
 
 def scale_body(ways, factor, other, *refs):
@@ -262,7 +266,7 @@
     cot = cotangent.reshape(total, sites, chans)
     shape = jax.ShapeDtypeStruct
     block = total * sites * chans
-    order = sorted(range(1, regions), reverse=True)
+    order = sorted(range(1, regions), key=lambda p: p != regions // 2)
     dma = pltpu.SemaphoreType.DMA
 
     outgoing = call(
@@ -299,11 +303,10 @@
     )(d_filter, d_gate, direct, local, mix, xt, ht, wt, mask, *arrived)
     swap = [(i, i ^ 1) for i in range(dp)]
     got = lax.ppermute(send, "dp", swap)
-    keep, grad_inputs = call(
-        functools.partial(keep_body, steps),
-        [shape((3, chans, chans), F32), shape(x.shape, BF16)], [VM] * 8, "keep",
-        flops=12 * block * chans, nbytes=30 * block,
-    )(mix, xt, ht, act_cot, sums, cot, w_filter, w_gate)
+    (keep,) = call(
+        functools.partial(keep_body, steps), [shape((3, chans, chans), F32)], [VM] * 5, "keep",
+        flops=6 * block * chans, nbytes=20 * block,
+    )(mix, xt, ht, act_cot, sums)
 
     rows = chans // ways
     chunk = (3, rows, chans)
@@ -321,9 +324,15 @@
         [shape(chunk, F32)] + [shape(chunk, BF16)] * (ways - 1), [VM] * 2, "split",
     )(keep, got)
     gots = [lax.ppermute(part, BOTH, pairs(p, True)) for p, part in enumerate(sends, 1)]
-    (mine,) = call(add_body, [shape(chunk, BF16)], [VM] * ways, "add_first")(own, *gots)
+    (mine,) = call(functools.partial(add_body, ways), [shape(chunk, BF16)], [VM] * ways, "add_first")(own, *gots)
     gots = [lax.ppermute(mine, BOTH, pairs(p, False)) for p in range(1, ways)]
-    (done,) = call(add_body, [shape(chunk, BF16)], [VM] * ways, "add_second")(mine, *gots)
+    grad_inputs, token = call(
+        functools.partial(inputs_body, steps), [shape(x.shape, BF16), shape((8, 128), F32)], [VM] * 4 + [AN], "inputs",
+        flops=8 * block * chans, nbytes=16 * block,
+    )(act_cot, cot, w_filter, w_gate, mine)
+    (done,) = call(
+        functools.partial(add_body, ways), [shape(chunk, BF16)], [VM] * ways + [AN], "add_second"
+    )(mine, *gots, token)
     chunks = [done] + [lax.ppermute(done, BOTH, pairs(p, True)) for p in range(1, ways)]
     others = [lax.ppermute(part, "dp", swap) for part in chunks]
     factor = 1.0 / math.sqrt(windows * dp * steps * sites * regions)

time: 48.1 us -> 46.6 us (0.969)
  waiting for transfers between devices: 18.8 us -> 18.1 us
    ppermute x3, waiting for transfers between devices: 6.31 us -> 4.63 us  [per_device(): lax.ppermute(part, 'region', [(r, r ^ p) for r in range(regions)])]
    ppermute x3, waiting for transfers between devices: 5.03 us -> 3.65 us  [per_device(): gots = [lax.ppermute(mine, BOTH, pairs(p, False)) for p in range(1, ways)]]
    ppermute x1, waiting for transfers between devices: 0.01 us -> 1.37 us  [per_device(): got = lax.ppermute(send, 'dp', swap)]
    ppermute x3, waiting for transfers between devices: 2.25 us -> 3.12 us  [per_device(): lax.ppermute(done, BOTH, pairs(p, True))]
    pallas_call x3 -> x4, Pallas kernels: 1.52 us -> 1.54 us  [the longest x1 1.11 us: per_device(): call(functools.partial(inputs_body, steps), [shape(x.shape, BF16), shape(...]
  transfers between devices with their start and end apart: 17 -> 17, of which waited for: 9 -> 13; matrix products, arithmetic and copies ran while one was open for 0% -> 0% of each run, Pallas kernels for 14% -> 14%
where the time goes in v4:
time: 46.6 us; the launch traced here: 46.4 us
  waiting for transfers between devices  18.1 us (39%)
  starting transfers between devices  17.8 us (38%)
  Pallas kernels  9.8 us (21%)
  between operations  0.73 us (2%)
    ppermute x3, starting transfers between devices, per_device(): lax.ppermute(part, 'region', [(r, r ^ p) for r in range(regions)])  5.68 us
    ppermute x3, waiting for transfers between devices, per_device(): lax.ppermute(part, BOTH, pairs(p, True))  5.04 us
    ppermute x3, starting transfers between devices, per_device(): gots = [lax.ppermute(mine, BOTH, pairs(p, False)) for p in range(1, ways)]  4.87 us
    ppermute x3, waiting for transfers between devices, per_device(): lax.ppermute(part, 'region', [(r, r ^ p) for r in range(regions)])  4.63 us
    pallas_call x1, Pallas kernels, per_device(): call(functools.partial(local_body, steps, order), [shape(x.shape, F32)] *...  4.11 us
    ppermute x3, waiting for transfers between devices, per_device(): gots = [lax.ppermute(mine, BOTH, pairs(p, False)) for p in range(1, ways)]  3.65 us
    ppermute x3, starting transfers between devices, per_device(): lax.ppermute(done, BOTH, pairs(p, True))  3.55 us
    ppermute x3, starting transfers between devices, per_device(): lax.ppermute(part, BOTH, pairs(p, True))  3.55 us
  transfers between devices with their start and end apart: 17, of which 13 were waited for; matrix products, arithmetic and copies ran while one was open for 0% of the time, Pallas kernels for 14%

profile of v4, /device:TPU:0, one launch (start us, length us, event | category | flops | bytes accessed | tf_op | source)
XLA Modules:
  0.0 46.4 jit_solution(12254915898033162372)
XLA Ops:
  0.6 1.5 %outgoing.1 = (bf16[2,128,256]{2,1,0:T(8,128)(2,1)S(1)}, bf16[2,128,256]{2,1,0:T(8,128)(2,1)S(1)}, bf16[2,128,256]{2,1,0:T(8,128)(2,1)S(1)}) custom-call(s32[8,6]{1,0:T(8,128)} %nb_hbm.3, bf16[2,256,256]{2,1,0:T(8,128)(2,1)} %bitcast.3, bf16[2,6,128,128]{3,2,1,0:T(8,128)(2,1)} %adj_hbm.3), custom_call_target="tpu_custom_call" | custom-call | flops 50331648 | bytes 524288 | tf_op jit(solution)/shard_map/outgoing/pallas_call | solution.py:272
  2.1 4.1 %collective-permute-start = (bf16[2,128,256]{2,1,0:T(8,128)(2,1)S(1)}, bf16[2,128,256]{2,1,0:T(8,128)(2,1)S(1)}, u32[]{:S(2)}, u32[]{:S(2)}) collective-permute-start(bf16[2,128,256]{2,1,0:T(8,128)(2,1)S(1)} %get-tuple-element.40), channel_id=1, source_target_pairs={{0,2},{1,3},{2,0},{3,1},{4,6},{5,7},{6,4},{7,5},{8,10},{9,11},{10,... | collective-permute-start | bytes 393224 | tf_op jit(solution)/shard_map/ppermute | solution.py:282
  6.2 1.6 %collective-permute-start.1 = (bf16[2,128,256]{2,1,0:T(8,128)(2,1)S(1)}, bf16[2,128,256]{2,1,0:T(8,128)(2,1)S(1)}, u32[]{:S(2)}, u32[]{:S(2)}) collective-permute-start(bf16[2,128,256]{2,1,0:T(8,128)(2,1)S(1)} %get-tuple-element.41), channel_id=1, source_target_pairs={{0,1},{1,0},{2,3},{3,2},{4,5},{5,4},{6,7},{7,6},{8,9},{9,8},{10,11... | collective-permute-start | bytes 393224 | tf_op jit(solution)/shard_map/ppermute | solution.py:282
  7.8 4.1 %local.1 = (f32[2,256,256]{2,1,0:T(8,128)S(1)}, f32[2,256,256]{2,1,0:T(8,128)S(1)}, f32[2,256,256]{2,1,0:T(8,128)S(1)}, f32[2,256,256]{2,1,0:T(8,128)S(1)}, f32[...) custom-call(s32[8,6]{1,0:T(8,128)} %nb_hbm.3, ...), custom_call_target="tpu_custom_call" | custom-call | flops 469762048 | bytes 3932160 | tf_op jit(solution)/shard_map/local/pallas_call | solution.py:286
  11.9 2.3 %collective-permute-done.refs_0_ = bf16[2,128,256]{2,1,0:T(8,128)(2,1)S(1)} collective-permute-done((bf16[2,128,256]{2,1,0:T(8,128)(2,1)S(1)}, bf16[2,128,256]{2,1,0:T(8,128)(2,1)S(1)}, u32[]{:S(2)}, u32[]{:S(2)}) %collective-permute-start) | collective-permute-done | bytes 131104 | tf_op jit(solution)/shard_map/ppermute | solution.py:282
  14.2 2.4 %collective-permute-done.2.refs_2_ = bf16[2,128,256]{2,1,0:T(8,128)(2,1)S(1)} collective-permute-done((bf16[2,128,256]{2,1,0:T(8,128)(2,1)S(1)}, bf16[2,128,256]{2,1,0:T(8,128)(2,1)S(1)}, u32[]{:S(2)}, u32[]{:S(2)}) %collective-permute-start.2) | collective-permute-done | bytes 131104 | tf_op jit(solution)/shard_map/ppermute | solution.py:282
  16.6 0.6 %send.1 = (bf16[2,2,256,256]{3,2,1,0:T(8,128)(2,1)S(1)}, bf16[2,256,256]{2,1,0:T(8,128)(2,1)S(1)}, bf16[3,256,256]{2,1,0:T(8,128)(2,1)S(1)}) custom-call(f32[2,256,256]{2,1,0:T(8,128)S(1)} %get-tuple-element.31.df_ref, f32[2,256,256]{2,1,0:T(8,128)S(1)} %get-tuple-element.32.dg_ref, f32[2,256,256]{2,1,0:T(8,128)S(1)} %get-tuple-element.33.direct_ref, ...), custom_call_target="tpu_custom_call" | custom-call | flops 201326592 | bytes 3932160 | tf_op jit(solution)/shard_map/send/pallas_call | solution.py:298
  17.6 1.4 %collective-permute-done.3.got_ref = bf16[3,256,256]{2,1,0:T(8,128)(2,1)S(1)} collective-permute-done((bf16[3,256,256]{2,1,0:T(8,128)(2,1)S(1)}, bf16[3,256,256]{2,1,0:T(8,128)(2,1)S(1)}, u32[]{:S(2)}, u32[]{:S(2)}) %collective-permute-start.3) | collective-permute-done | bytes 393248 | tf_op jit(solution)/shard_map/ppermute | solution.py:305
  19.1 1.6 %collective-permute-start.4 = (bf16[3,64,256]{2,1,0:T(8,128)(2,1)S(1)}, bf16[3,64,256]{2,1,0:T(8,128)(2,1)S(1)}, u32[]{:S(2)}, u32[]{:S(2)}) collective-permute-start(bf16[3,64,256]{2,1,0:T(8,128)(2,1)S(1)} %get-tuple-element.47), channel_id=1, source_target_pairs={{0,8},{1,9},{2,10},{3,11},{4,5},{5,4},{6,7},{7,6},{8,0},{9,1},{10,... | collective-permute-start | bytes 294920 | tf_op jit(solution)/shard_map/ppermute | solution.py:326
  20.6 1.5 %collective-permute-start.5 = (bf16[3,64,256]{2,1,0:T(8,128)(2,1)S(1)}, bf16[3,64,256]{2,1,0:T(8,128)(2,1)S(1)}, u32[]{:S(2)}, u32[]{:S(2)}) collective-permute-start(bf16[3,64,256]{2,1,0:T(8,128)(2,1)S(1)} %get-tuple-element.48), channel_id=1, source_target_pairs={{0,16},{1,17},{2,18},{3,19},{4,6},{5,7},{6,4},{7,5},{8,24},{9,25},... | collective-permute-start | bytes 294920 | tf_op jit(solution)/shard_map/ppermute | solution.py:326
  22.6 1.1 %collective-permute-done.4.refs_1_ = bf16[3,64,256]{2,1,0:T(8,128)(2,1)S(1)} collective-permute-done((bf16[3,64,256]{2,1,0:T(8,128)(2,1)S(1)}, bf16[3,64,256]{2,1,0:T(8,128)(2,1)S(1)}, u32[]{:S(2)}, u32[]{:S(2)}) %collective-permute-start.4) | collective-permute-done | bytes 98336 | tf_op jit(solution)/shard_map/ppermute | solution.py:326
  23.7 1.5 %collective-permute-done.5.refs_2_ = bf16[3,64,256]{2,1,0:T(8,128)(2,1)S(1)} collective-permute-done((bf16[3,64,256]{2,1,0:T(8,128)(2,1)S(1)}, bf16[3,64,256]{2,1,0:T(8,128)(2,1)S(1)}, u32[]{:S(2)}, u32[]{:S(2)}) %collective-permute-start.5) | collective-permute-done | bytes 98336 | tf_op jit(solution)/shard_map/ppermute | solution.py:326
  25.2 2.4 %collective-permute-done.6.refs_3_ = bf16[3,64,256]{2,1,0:T(8,128)(2,1)S(1)} collective-permute-done((bf16[3,64,256]{2,1,0:T(8,128)(2,1)S(1)}, bf16[3,64,256]{2,1,0:T(8,128)(2,1)S(1)}, u32[]{:S(2)}, u32[]{:S(2)}) %collective-permute-start.6) | collective-permute-done | bytes 98336 | tf_op jit(solution)/shard_map/ppermute | solution.py:326
  27.7 2.5 %collective-permute-start.9 = (bf16[3,64,256]{2,1,0:T(8,128)(2,1)S(1)}, bf16[3,64,256]{2,1,0:T(8,128)(2,1)S(1)}, u32[]{:S(2)}, u32[]{:S(2)}) collective-permute-start(bf16[3,64,256]{2,1,0:T(8,128)(2,1)S(1)} %add_first.1._.refs_0_), channel_id=1, source_target_pairs={{0,3},{1,2},{2,1},{3,0},{4,28},{5,29},{6,30},{7,31},{8,11},{9,10},... | collective-permute-start | bytes 294920 | tf_op jit(solution)/shard_map/ppermute | solution.py:328
  30.2 1.9 %collective-permute-start.8 = (bf16[3,64,256]{2,1,0:T(8,128)(2,1)S(1)}, bf16[3,64,256]{2,1,0:T(8,128)(2,1)S(1)}, u32[]{:S(2)}, u32[]{:S(2)}) collective-permute-start(bf16[3,64,256]{2,1,0:T(8,128)(2,1)S(1)} %add_first.1._.refs_0_), channel_id=1, source_target_pairs={{0,2},{1,3},{2,0},{3,1},{4,20},{5,21},{6,22},{7,23},{8,10},{9,11},... | collective-permute-start | bytes 294920 | tf_op jit(solution)/shard_map/ppermute | solution.py:328
  32.6 1.1 %inputs.1 = (bf16[2,256,256]{2,1,0:T(8,128)(2,1)}, f32[8,128]{1,0:T(8,128)S(1)}) custom-call(bf16[2,2,256,256]{3,2,1,0:T(8,128)(2,1)S(1)} %get-tuple-element.43.act_ref, bf16[2,256,256]{2,1,0:T(8,128)(2,1)S(1)} %bitcast.5, bf16[2,256,256]{2,1,0:T(8,128)(2,1)S(1)} %copy-done.1, bf16[2,256,256]{2,1,0:T(8,128)(2,1)S(1)} %copy-done.2, ...), custom_call_target="tpu_custom_call" | custom-call | flops 268435456 | bytes 2097152 | tf_op jit(solution)/shard_map/inputs/pallas_call | solution.py:329
  33.7 0.6 %collective-permute-done.9.refs_3_ = bf16[3,64,256]{2,1,0:T(8,128)(2,1)S(1)} collective-permute-done((bf16[3,64,256]{2,1,0:T(8,128)(2,1)S(1)}, bf16[3,64,256]{2,1,0:T(8,128)(2,1)S(1)}, u32[]{:S(2)}, u32[]{:S(2)}) %collective-permute-start.9) | collective-permute-done | bytes 98336 | tf_op jit(solution)/shard_map/ppermute | solution.py:328
  34.3 2.1 %collective-permute-done.8.refs_2_ = bf16[3,64,256]{2,1,0:T(8,128)(2,1)S(1)} collective-permute-done((bf16[3,64,256]{2,1,0:T(8,128)(2,1)S(1)}, bf16[3,64,256]{2,1,0:T(8,128)(2,1)S(1)}, u32[]{:S(2)}, u32[]{:S(2)}) %collective-permute-start.8) | collective-permute-done | bytes 98336 | tf_op jit(solution)/shard_map/ppermute | solution.py:328
  36.4 1.0 %collective-permute-done.7.refs_1_ = bf16[3,64,256]{2,1,0:T(8,128)(2,1)S(1)} collective-permute-done((bf16[3,64,256]{2,1,0:T(8,128)(2,1)S(1)}, bf16[3,64,256]{2,1,0:T(8,128)(2,1)S(1)}, u32[]{:S(2)}, u32[]{:S(2)}) %collective-permute-start.7) | collective-permute-done | bytes 98336 | tf_op jit(solution)/shard_map/ppermute | solution.py:328
  37.9 1.5 %collective-permute-start.13 = (bf16[3,64,256]{2,1,0:T(8,128)(2,1)S(1)}, bf16[3,64,256]{2,1,0:T(8,128)(2,1)S(1)}, u32[]{:S(2)}, u32[]{:S(2)}) collective-permute-start(bf16[3,64,256]{2,1,0:T(8,128)(2,1)S(1)} %add_second.1.refs_0_), channel_id=1, source_target_pairs={{0,16},{1,17},{2,18},{3,19},{4,6},{5,7},{6,4},{7,5},{8,24},{9,25},... | collective-permute-start | bytes 294920 | tf_op jit(solution)/shard_map/ppermute | solution.py:336
  39.5 1.5 %collective-permute-start.11 = (bf16[3,64,256]{2,1,0:T(8,128)(2,1)S(1)}, bf16[3,64,256]{2,1,0:T(8,128)(2,1)S(1)}, u32[]{:S(2)}, u32[]{:S(2)}) collective-permute-start(bf16[3,64,256]{2,1,0:T(8,128)(2,1)S(1)} %add_second.1.refs_0_), channel_id=1, source_target_pairs={{0,8},{1,9},{2,10},{3,11},{4,5},{5,4},{6,7},{7,6},{8,0},{9,1},{10,... | collective-permute-start | bytes 294920 | tf_op jit(solution)/shard_map/ppermute | solution.py:336
  41.0 2.1 %collective-permute-done.15.refs_3_ = bf16[3,64,256]{2,1,0:T(8,128)(2,1)S(1)} collective-permute-done((bf16[3,64,256]{2,1,0:T(8,128)(2,1)S(1)}, bf16[3,64,256]{2,1,0:T(8,128)(2,1)S(1)}, u32[]{:S(2)}, u32[]{:S(2)}) %collective-permute-start.15) | collective-permute-done | bytes 98336 | tf_op jit(solution)/shard_map/ppermute | solution.py:336
  44.1 1.0 %scale_own.1 = (f32[2,256,256]{2,1,0:T(8,128)}, f32[2,256,256]{2,1,0:T(8,128)}, f32[2,256,256]{2,1,0:T(8,128)}) custom-call(bf16[3,64,256]{2,1,0:T(8,128)(2,1)S(1)} %add_second.1.refs_0_, bf16[3,64,256]{2,1,0:T(8,128)(2,1)S(1)} %collective-permute-done.11.refs_1_, bf16[3,64,256]{2,1,0:T(8,128)(2,1)S(1)} %collective-permute-done.13.refs_2_, ...), custom_call_target="tpu_custom_call" | custom-call | tf_op jit(solution)/shard_map/scale_own/pallas_call | solution.py:341
  45.4 1.0 %scale_other.1 = (f32[2,256,256]{2,1,0:T(8,128)}, f32[2,256,256]{2,1,0:T(8,128)}, f32[2,256,256]{2,1,0:T(8,128)}) custom-call(bf16[3,64,256]{2,1,0:T(8,128)(2,1)S(1)} %collective-permute-done.10.refs_0_, bf16[3,64,256]{2,1,0:T(8,128)(2,1)S(1)} %collective-permute-done.12.refs_1_, ...), custom_call_target="tpu_custom_call", output_to_operand_aliasing={{0}: (4, {}), {1}: (5, {}), {2}: (6, {})} | custom-call | tf_op jit(solution)/shard_map/scale_other/pallas_call | solution.py:342
  (26 shorter events, 3.4 us)
Async XLA Ops:
  2.1 12.1 %collective-permute-start = (bf16[2,128,256]{2,1,0:T(8,128)(2,1)S(1)}, bf16[2,128,256]{2,1,0:T(8,128)(2,1)S(1)}, u32[]{:S(2)}, u32[]{:S(2)}) collective-permute-start(bf16[2,128,256]{2,1,0:T(8,128)(2,1)S(1)} %get-tuple-element.40), channel_id=1, source_target_pairs={{0,2},{1,3},{2,0},{3,1},{4,6},{5,7},{6,4},{7,5},{8,10},{9,11},{10,... | collective-permute-start | bytes 393224 | tf_op jit(solution)/shard_map/ppermute | solution.py:282
  6.2 8.0 %collective-permute-start.1 = (bf16[2,128,256]{2,1,0:T(8,128)(2,1)S(1)}, bf16[2,128,256]{2,1,0:T(8,128)(2,1)S(1)}, u32[]{:S(2)}, u32[]{:S(2)}) collective-permute-start(bf16[2,128,256]{2,1,0:T(8,128)(2,1)S(1)} %get-tuple-element.41), channel_id=1, source_target_pairs={{0,1},{1,0},{2,3},{3,2},{4,5},{5,4},{6,7},{7,6},{8,9},{9,8},{10,11... | collective-permute-start | bytes 393224 | tf_op jit(solution)/shard_map/ppermute | solution.py:282
  7.8 8.8 %collective-permute-start.2 = (bf16[2,128,256]{2,1,0:T(8,128)(2,1)S(1)}, bf16[2,128,256]{2,1,0:T(8,128)(2,1)S(1)}, u32[]{:S(2)}, u32[]{:S(2)}) collective-permute-start(bf16[2,128,256]{2,1,0:T(8,128)(2,1)S(1)} %get-tuple-element.42), channel_id=1, source_target_pairs={{0,3},{1,2},{2,1},{3,0},{4,7},{5,6},{6,5},{7,4},{8,11},{9,10},{10,... | collective-permute-start | bytes 393224 | tf_op jit(solution)/shard_map/ppermute | solution.py:282
  17.2 1.8 %collective-permute-start.3 = (bf16[3,256,256]{2,1,0:T(8,128)(2,1)S(1)}, bf16[3,256,256]{2,1,0:T(8,128)(2,1)S(1)}, u32[]{:S(2)}, u32[]{:S(2)}) collective-permute-start(bf16[3,256,256]{2,1,0:T(8,128)(2,1)S(1)} %get-tuple-element.45), channel_id=1, source_target_pairs={{0,4},{4,0},{8,12},{12,8},{16,20},{20,16},{24,28},{28,24},{1,5},{5... | collective-permute-start | bytes 1179656 | tf_op jit(solution)/shard_map/ppermute | solution.py:305
  19.0 13.6 %copy-start.2 = (bf16[2,256,256]{2,1,0:T(8,128)(2,1)S(1)}, bf16[2,256,256]{2,1,0:T(8,128)(2,1)}, u32[]{:S(2)}) copy-start(bf16[2,256,256]{2,1,0:T(8,128)(2,1)} %wg_ref.1) | copy-start | bytes 786436
  19.1 4.7 %collective-permute-start.4 = (bf16[3,64,256]{2,1,0:T(8,128)(2,1)S(1)}, bf16[3,64,256]{2,1,0:T(8,128)(2,1)S(1)}, u32[]{:S(2)}, u32[]{:S(2)}) collective-permute-start(bf16[3,64,256]{2,1,0:T(8,128)(2,1)S(1)} %get-tuple-element.47), channel_id=1, source_target_pairs={{0,8},{1,9},{2,10},{3,11},{4,5},{5,4},{6,7},{7,6},{8,0},{9,1},{10,... | collective-permute-start | bytes 294920 | tf_op jit(solution)/shard_map/ppermute | solution.py:326
  20.6 4.6 %collective-permute-start.5 = (bf16[3,64,256]{2,1,0:T(8,128)(2,1)S(1)}, bf16[3,64,256]{2,1,0:T(8,128)(2,1)S(1)}, u32[]{:S(2)}, u32[]{:S(2)}) collective-permute-start(bf16[3,64,256]{2,1,0:T(8,128)(2,1)S(1)} %get-tuple-element.48), channel_id=1, source_target_pairs={{0,16},{1,17},{2,18},{3,19},{4,6},{5,7},{6,4},{7,5},{8,24},{9,25},... | collective-permute-start | bytes 294920 | tf_op jit(solution)/shard_map/ppermute | solution.py:326
  22.1 5.5 %collective-permute-start.6 = (bf16[3,64,256]{2,1,0:T(8,128)(2,1)S(1)}, bf16[3,64,256]{2,1,0:T(8,128)(2,1)S(1)}, u32[]{:S(2)}, u32[]{:S(2)}) collective-permute-start(bf16[3,64,256]{2,1,0:T(8,128)(2,1)S(1)} %get-tuple-element.49), channel_id=1, source_target_pairs={{0,24},{1,25},{2,26},{3,27},{4,7},{5,6},{6,5},{7,4},{8,16},{9,17},... | collective-permute-start | bytes 294920 | tf_op jit(solution)/shard_map/ppermute | solution.py:326
  27.7 4.9 %copy-start = (bf16[1,2,256,256]{3,2,1,0:T(8,128)(2,1)S(1)}, bf16[1,2,256,256]{3,2,1,0:T(8,128)(2,1)}, u32[]{:S(2)}) copy-start(bf16[1,2,256,256]{3,2,1,0:T(8,128)(2,1)} %param.8) | copy-start | bytes 786436
  27.7 4.9 %copy-start.1 = (bf16[2,256,256]{2,1,0:T(8,128)(2,1)S(1)}, bf16[2,256,256]{2,1,0:T(8,128)(2,1)}, u32[]{:S(2)}) copy-start(bf16[2,256,256]{2,1,0:T(8,128)(2,1)} %wf_ref.1) | copy-start | bytes 786436
  27.7 6.5 %collective-permute-start.9 = (bf16[3,64,256]{2,1,0:T(8,128)(2,1)S(1)}, bf16[3,64,256]{2,1,0:T(8,128)(2,1)S(1)}, u32[]{:S(2)}, u32[]{:S(2)}) collective-permute-start(bf16[3,64,256]{2,1,0:T(8,128)(2,1)S(1)} %add_first.1._.refs_0_), channel_id=1, source_target_pairs={{0,3},{1,2},{2,1},{3,0},{4,28},{5,29},{6,30},{7,31},{8,11},{9,10},... | collective-permute-start | bytes 294920 | tf_op jit(solution)/shard_map/ppermute | solution.py:328
  30.2 6.2 %collective-permute-start.8 = (bf16[3,64,256]{2,1,0:T(8,128)(2,1)S(1)}, bf16[3,64,256]{2,1,0:T(8,128)(2,1)S(1)}, u32[]{:S(2)}, u32[]{:S(2)}) collective-permute-start(bf16[3,64,256]{2,1,0:T(8,128)(2,1)S(1)} %add_first.1._.refs_0_), channel_id=1, source_target_pairs={{0,2},{1,3},{2,0},{3,1},{4,20},{5,21},{6,22},{7,23},{8,10},{9,11},... | collective-permute-start | bytes 294920 | tf_op jit(solution)/shard_map/ppermute | solution.py:328
  32.1 5.3 %collective-permute-start.7 = (bf16[3,64,256]{2,1,0:T(8,128)(2,1)S(1)}, bf16[3,64,256]{2,1,0:T(8,128)(2,1)S(1)}, u32[]{:S(2)}, u32[]{:S(2)}) collective-permute-start(bf16[3,64,256]{2,1,0:T(8,128)(2,1)S(1)} %add_first.1._.refs_0_), channel_id=1, source_target_pairs={{0,1},{1,0},{2,3},{3,2},{4,12},{5,13},{6,14},{7,15},{8,9},{9,8},{1... | collective-permute-start | bytes 294920 | tf_op jit(solution)/shard_map/ppermute | solution.py:328
  37.4 5.7 %collective-permute-start.15 = (bf16[3,64,256]{2,1,0:T(8,128)(2,1)S(1)}, bf16[3,64,256]{2,1,0:T(8,128)(2,1)S(1)}, u32[]{:S(2)}, u32[]{:S(2)}) collective-permute-start(bf16[3,64,256]{2,1,0:T(8,128)(2,1)S(1)} %add_second.1.refs_0_), channel_id=1, source_target_pairs={{0,24},{1,25},{2,26},{3,27},{4,7},{5,6},{6,5},{7,4},{8,16},{9,17},... | collective-permute-start | bytes 294920 | tf_op jit(solution)/shard_map/ppermute | solution.py:336
  37.9 5.7 %collective-permute-start.13 = (bf16[3,64,256]{2,1,0:T(8,128)(2,1)S(1)}, bf16[3,64,256]{2,1,0:T(8,128)(2,1)S(1)}, u32[]{:S(2)}, u32[]{:S(2)}) collective-permute-start(bf16[3,64,256]{2,1,0:T(8,128)(2,1)S(1)} %add_second.1.refs_0_), channel_id=1, source_target_pairs={{0,16},{1,17},{2,18},{3,19},{4,6},{5,7},{6,4},{7,5},{8,24},{9,25},... | collective-permute-start | bytes 294920 | tf_op jit(solution)/shard_map/ppermute | solution.py:336
  39.5 4.6 %collective-permute-start.11 = (bf16[3,64,256]{2,1,0:T(8,128)(2,1)S(1)}, bf16[3,64,256]{2,1,0:T(8,128)(2,1)S(1)}, u32[]{:S(2)}, u32[]{:S(2)}) collective-permute-start(bf16[3,64,256]{2,1,0:T(8,128)(2,1)S(1)} %add_second.1.refs_0_), channel_id=1, source_target_pairs={{0,8},{1,9},{2,10},{3,11},{4,5},{5,4},{6,7},{7,6},{8,0},{9,1},{10,... | collective-permute-start | bytes 294920 | tf_op jit(solution)/shard_map/ppermute | solution.py:336
  41.0 4.2 %collective-permute-start.10 = (bf16[3,64,256]{2,1,0:T(8,128)(2,1)S(1)}, bf16[3,64,256]{2,1,0:T(8,128)(2,1)S(1)}, u32[]{:S(2)}, u32[]{:S(2)}) collective-permute-start(bf16[3,64,256]{2,1,0:T(8,128)(2,1)S(1)} %add_second.1.refs_0_), channel_id=1, source_target_pairs={{0,4},{4,0},{8,12},{12,8},{16,20},{20,16},{24,28},{28,24},{1,5},{5... | collective-permute-start | bytes 294920 | tf_op jit(solution)/shard_map/ppermute | solution.py:337
  43.1 2.0 %collective-permute-start.16 = (bf16[3,64,256]{2,1,0:T(8,128)(2,1)S(1)}, bf16[3,64,256]{2,1,0:T(8,128)(2,1)S(1)}, u32[]{:S(2)}, u32[]{:S(2)}) collective-permute-start(bf16[3,64,256]{2,1,0:T(8,128)(2,1)S(1)} %collective-permute-done.15.refs_3_), channel_id=1, source_target_pairs={{0,4},{4,0},{8,12},{12,8},{16,20},{20,16},{24,28},{28,24},{1,5},{5... | collective-permute-start | bytes 294920 | tf_op jit(solution)/shard_map/ppermute | solution.py:337
  43.6 1.5 %collective-permute-start.14 = (bf16[3,64,256]{2,1,0:T(8,128)(2,1)S(1)}, bf16[3,64,256]{2,1,0:T(8,128)(2,1)S(1)}, u32[]{:S(2)}, u32[]{:S(2)}) collective-permute-start(bf16[3,64,256]{2,1,0:T(8,128)(2,1)S(1)} %collective-permute-done.13.refs_2_), channel_id=1, source_target_pairs={{0,4},{4,0},{8,12},{12,8},{16,20},{20,16},{24,28},{28,24},{1,5},{5... | collective-permute-start | bytes 294920 | tf_op jit(solution)/shard_map/ppermute | solution.py:337
  44.1 1.3 %collective-permute-start.12 = (bf16[3,64,256]{2,1,0:T(8,128)(2,1)S(1)}, bf16[3,64,256]{2,1,0:T(8,128)(2,1)S(1)}, u32[]{:S(2)}, u32[]{:S(2)}) collective-permute-start(bf16[3,64,256]{2,1,0:T(8,128)(2,1)S(1)} %collective-permute-done.11.refs_1_), channel_id=1, source_target_pairs={{0,4},{4,0},{8,12},{12,8},{16,20},{20,16},{24,28},{28,24},{1,5},{5... | collective-permute-start | bytes 294920 | tf_op jit(solution)/shard_map/ppermute | solution.py:337

commit v5 on v4

--- a/solution.py
+++ b/solution.py
@@ -75,11 +75,7 @@
     me = region_of()
     tiles, per_tile = adj_ref.shape[:2]
     total = cot_ref.shape[0]
-    parts = [(nb_hbm, nb_ref)]
-    for j in range(tiles):
-        rows = pl.ds(j * TILE, TILE)
-        parts += [(cot_hbm.at[t, rows], cot_ref.at[t, rows]) for t in range(total)]
-        parts += [(adj_hbm.at[j, pl.ds(k, 2)], adj_ref.at[j, pl.ds(k, 2)]) for k in range(0, per_tile, 2)]
+    parts = [(nb_hbm, nb_ref), (cot_hbm, cot_ref), (adj_hbm, adj_ref)]
     first, *copies = fetch(parts, sems)
     first.wait()
     found = [find_entry(nb_ref, me, jnp.bitwise_xor(me, p), tiles, per_tile) for p in order]
@@ -274,7 +270,7 @@
         [shape((total, TILE, chans), BF16)] * (regions - 1), [HB] * 3, "outgoing",
         scratch=[
             pltpu.SMEM(neighbours.shape, jnp.int32), pltpu.VMEM(cot.shape, BF16), pltpu.VMEM(adjacency.shape, BF16),
-            dma((1 + tiles * (total + per_tile // 2),)),
+            dma((3,)),
         ],
         flops=2 * (regions - 1) * total * TILE * TILE * chans, nbytes=4 * block,
     )(*in_hbm(neighbours, cot, adjacency))

time: 46.6 us -> 46.4 us (level)
  no operation moved by 1% of the time
where the time goes in v5:
time: 46.4 us; the launch traced here: 46.3 us
  waiting for transfers between devices  18.1 us (39%)
  starting transfers between devices  17.8 us (38%)
  Pallas kernels  9.69 us (21%)
  between operations  0.73 us (2%)
    ppermute x3, starting transfers between devices, per_device(): lax.ppermute(part, 'region', [(r, r ^ p) for r in range(regions)])  5.68 us
    ppermute x3, waiting for transfers between devices, per_device(): lax.ppermute(part, BOTH, pairs(p, True))  5.04 us
    ppermute x3, starting transfers between devices, per_device(): gots = [lax.ppermute(mine, BOTH, pairs(p, False)) for p in range(1, ways)]  4.86 us
    ppermute x3, waiting for transfers between devices, per_device(): lax.ppermute(part, 'region', [(r, r ^ p) for r in range(regions)])  4.63 us
    pallas_call x1, Pallas kernels, per_device(): call(functools.partial(local_body, steps, order), [shape(x.shape, F32)] *...  4.11 us
    ppermute x3, waiting for transfers between devices, per_device(): gots = [lax.ppermute(mine, BOTH, pairs(p, False)) for p in range(1, ways)]  3.66 us
    ppermute x3, starting transfers between devices, per_device(): lax.ppermute(done, BOTH, pairs(p, True))  3.55 us
    ppermute x3, starting transfers between devices, per_device(): lax.ppermute(part, BOTH, pairs(p, True))  3.55 us
  transfers between devices with their start and end apart: 17, of which 13 were waited for; matrix products, arithmetic and copies ran while one was open for 0% of the time, Pallas kernels for 14%

profile of v5, /device:TPU:0, one launch (start us, length us, event | category | flops | bytes accessed | tf_op | source)
XLA Modules:
  0.0 46.3 jit_solution(14747771304990131912)
XLA Ops:
  0.6 1.4 %outgoing.1 = (bf16[2,128,256]{2,1,0:T(8,128)(2,1)S(1)}, bf16[2,128,256]{2,1,0:T(8,128)(2,1)S(1)}, bf16[2,128,256]{2,1,0:T(8,128)(2,1)S(1)}) custom-call(s32[8,6]{1,0:T(8,128)} %nb_hbm.3, bf16[2,256,256]{2,1,0:T(8,128)(2,1)} %bitcast.3, bf16[2,6,128,128]{3,2,1,0:T(8,128)(2,1)} %adj_hbm.3), custom_call_target="tpu_custom_call" | custom-call | flops 50331648 | bytes 524288 | tf_op jit(solution)/shard_map/outgoing/pallas_call | solution.py:268
  2.0 4.1 %collective-permute-start = (bf16[2,128,256]{2,1,0:T(8,128)(2,1)S(1)}, bf16[2,128,256]{2,1,0:T(8,128)(2,1)S(1)}, u32[]{:S(2)}, u32[]{:S(2)}) collective-permute-start(bf16[2,128,256]{2,1,0:T(8,128)(2,1)S(1)} %get-tuple-element.40), channel_id=1, source_target_pairs={{0,2},{1,3},{2,0},{3,1},{4,6},{5,7},{6,4},{7,5},{8,10},{9,11},{10,... | collective-permute-start | bytes 393224 | tf_op jit(solution)/shard_map/ppermute | solution.py:278
  6.1 1.6 %collective-permute-start.1 = (bf16[2,128,256]{2,1,0:T(8,128)(2,1)S(1)}, bf16[2,128,256]{2,1,0:T(8,128)(2,1)S(1)}, u32[]{:S(2)}, u32[]{:S(2)}) collective-permute-start(bf16[2,128,256]{2,1,0:T(8,128)(2,1)S(1)} %get-tuple-element.41), channel_id=1, source_target_pairs={{0,1},{1,0},{2,3},{3,2},{4,5},{5,4},{6,7},{7,6},{8,9},{9,8},{10,11... | collective-permute-start | bytes 393224 | tf_op jit(solution)/shard_map/ppermute | solution.py:278
  7.7 4.1 %local.1 = (f32[2,256,256]{2,1,0:T(8,128)S(1)}, f32[2,256,256]{2,1,0:T(8,128)S(1)}, f32[2,256,256]{2,1,0:T(8,128)S(1)}, f32[2,256,256]{2,1,0:T(8,128)S(1)}, f32[...) custom-call(s32[8,6]{1,0:T(8,128)} %nb_hbm.3, ...), custom_call_target="tpu_custom_call" | custom-call | flops 469762048 | bytes 3932160 | tf_op jit(solution)/shard_map/local/pallas_call | solution.py:282
  11.8 2.3 %collective-permute-done.refs_0_ = bf16[2,128,256]{2,1,0:T(8,128)(2,1)S(1)} collective-permute-done((bf16[2,128,256]{2,1,0:T(8,128)(2,1)S(1)}, bf16[2,128,256]{2,1,0:T(8,128)(2,1)S(1)}, u32[]{:S(2)}, u32[]{:S(2)}) %collective-permute-start) | collective-permute-done | bytes 131104 | tf_op jit(solution)/shard_map/ppermute | solution.py:278
  14.1 2.4 %collective-permute-done.2.refs_2_ = bf16[2,128,256]{2,1,0:T(8,128)(2,1)S(1)} collective-permute-done((bf16[2,128,256]{2,1,0:T(8,128)(2,1)S(1)}, bf16[2,128,256]{2,1,0:T(8,128)(2,1)S(1)}, u32[]{:S(2)}, u32[]{:S(2)}) %collective-permute-start.2) | collective-permute-done | bytes 131104 | tf_op jit(solution)/shard_map/ppermute | solution.py:278
  16.5 0.6 %send.1 = (bf16[2,2,256,256]{3,2,1,0:T(8,128)(2,1)S(1)}, bf16[2,256,256]{2,1,0:T(8,128)(2,1)S(1)}, bf16[3,256,256]{2,1,0:T(8,128)(2,1)S(1)}) custom-call(f32[2,256,256]{2,1,0:T(8,128)S(1)} %get-tuple-element.31.df_ref, f32[2,256,256]{2,1,0:T(8,128)S(1)} %get-tuple-element.32.dg_ref, f32[2,256,256]{2,1,0:T(8,128)S(1)} %get-tuple-element.33.direct_ref, ...), custom_call_target="tpu_custom_call" | custom-call | flops 201326592 | bytes 3932160 | tf_op jit(solution)/shard_map/send/pallas_call | solution.py:294
  17.5 1.4 %collective-permute-done.3.got_ref = bf16[3,256,256]{2,1,0:T(8,128)(2,1)S(1)} collective-permute-done((bf16[3,256,256]{2,1,0:T(8,128)(2,1)S(1)}, bf16[3,256,256]{2,1,0:T(8,128)(2,1)S(1)}, u32[]{:S(2)}, u32[]{:S(2)}) %collective-permute-start.3) | collective-permute-done | bytes 393248 | tf_op jit(solution)/shard_map/ppermute | solution.py:301
  18.9 1.6 %collective-permute-start.4 = (bf16[3,64,256]{2,1,0:T(8,128)(2,1)S(1)}, bf16[3,64,256]{2,1,0:T(8,128)(2,1)S(1)}, u32[]{:S(2)}, u32[]{:S(2)}) collective-permute-start(bf16[3,64,256]{2,1,0:T(8,128)(2,1)S(1)} %get-tuple-element.47), channel_id=1, source_target_pairs={{0,8},{1,9},{2,10},{3,11},{4,5},{5,4},{6,7},{7,6},{8,0},{9,1},{10,... | collective-permute-start | bytes 294920 | tf_op jit(solution)/shard_map/ppermute | solution.py:322
  20.5 1.5 %collective-permute-start.5 = (bf16[3,64,256]{2,1,0:T(8,128)(2,1)S(1)}, bf16[3,64,256]{2,1,0:T(8,128)(2,1)S(1)}, u32[]{:S(2)}, u32[]{:S(2)}) collective-permute-start(bf16[3,64,256]{2,1,0:T(8,128)(2,1)S(1)} %get-tuple-element.48), channel_id=1, source_target_pairs={{0,16},{1,17},{2,18},{3,19},{4,6},{5,7},{6,4},{7,5},{8,24},{9,25},... | collective-permute-start | bytes 294920 | tf_op jit(solution)/shard_map/ppermute | solution.py:322
  22.5 1.1 %collective-permute-done.4.refs_1_ = bf16[3,64,256]{2,1,0:T(8,128)(2,1)S(1)} collective-permute-done((bf16[3,64,256]{2,1,0:T(8,128)(2,1)S(1)}, bf16[3,64,256]{2,1,0:T(8,128)(2,1)S(1)}, u32[]{:S(2)}, u32[]{:S(2)}) %collective-permute-start.4) | collective-permute-done | bytes 98336 | tf_op jit(solution)/shard_map/ppermute | solution.py:322
  23.6 1.5 %collective-permute-done.5.refs_2_ = bf16[3,64,256]{2,1,0:T(8,128)(2,1)S(1)} collective-permute-done((bf16[3,64,256]{2,1,0:T(8,128)(2,1)S(1)}, bf16[3,64,256]{2,1,0:T(8,128)(2,1)S(1)}, u32[]{:S(2)}, u32[]{:S(2)}) %collective-permute-start.5) | collective-permute-done | bytes 98336 | tf_op jit(solution)/shard_map/ppermute | solution.py:322
  25.1 2.4 %collective-permute-done.6.refs_3_ = bf16[3,64,256]{2,1,0:T(8,128)(2,1)S(1)} collective-permute-done((bf16[3,64,256]{2,1,0:T(8,128)(2,1)S(1)}, bf16[3,64,256]{2,1,0:T(8,128)(2,1)S(1)}, u32[]{:S(2)}, u32[]{:S(2)}) %collective-permute-start.6) | collective-permute-done | bytes 98336 | tf_op jit(solution)/shard_map/ppermute | solution.py:322
  27.6 2.5 %collective-permute-start.9 = (bf16[3,64,256]{2,1,0:T(8,128)(2,1)S(1)}, bf16[3,64,256]{2,1,0:T(8,128)(2,1)S(1)}, u32[]{:S(2)}, u32[]{:S(2)}) collective-permute-start(bf16[3,64,256]{2,1,0:T(8,128)(2,1)S(1)} %add_first.1._.refs_0_), channel_id=1, source_target_pairs={{0,3},{1,2},{2,1},{3,0},{4,28},{5,29},{6,30},{7,31},{8,11},{9,10},... | collective-permute-start | bytes 294920 | tf_op jit(solution)/shard_map/ppermute | solution.py:324
  30.1 1.9 %collective-permute-start.8 = (bf16[3,64,256]{2,1,0:T(8,128)(2,1)S(1)}, bf16[3,64,256]{2,1,0:T(8,128)(2,1)S(1)}, u32[]{:S(2)}, u32[]{:S(2)}) collective-permute-start(bf16[3,64,256]{2,1,0:T(8,128)(2,1)S(1)} %add_first.1._.refs_0_), channel_id=1, source_target_pairs={{0,2},{1,3},{2,0},{3,1},{4,20},{5,21},{6,22},{7,23},{8,10},{9,11},... | collective-permute-start | bytes 294920 | tf_op jit(solution)/shard_map/ppermute | solution.py:324
  32.5 1.1 %inputs.1 = (bf16[2,256,256]{2,1,0:T(8,128)(2,1)}, f32[8,128]{1,0:T(8,128)S(1)}) custom-call(bf16[2,2,256,256]{3,2,1,0:T(8,128)(2,1)S(1)} %get-tuple-element.43.act_ref, bf16[2,256,256]{2,1,0:T(8,128)(2,1)S(1)} %bitcast.5, bf16[2,256,256]{2,1,0:T(8,128)(2,1)S(1)} %copy-done.1, bf16[2,256,256]{2,1,0:T(8,128)(2,1)S(1)} %copy-done.2, ...), custom_call_target="tpu_custom_call" | custom-call | flops 268435456 | bytes 2097152 | tf_op jit(solution)/shard_map/inputs/pallas_call | solution.py:325
  33.6 0.6 %collective-permute-done.9.refs_3_ = bf16[3,64,256]{2,1,0:T(8,128)(2,1)S(1)} collective-permute-done((bf16[3,64,256]{2,1,0:T(8,128)(2,1)S(1)}, bf16[3,64,256]{2,1,0:T(8,128)(2,1)S(1)}, u32[]{:S(2)}, u32[]{:S(2)}) %collective-permute-start.9) | collective-permute-done | bytes 98336 | tf_op jit(solution)/shard_map/ppermute | solution.py:324
  34.1 2.1 %collective-permute-done.8.refs_2_ = bf16[3,64,256]{2,1,0:T(8,128)(2,1)S(1)} collective-permute-done((bf16[3,64,256]{2,1,0:T(8,128)(2,1)S(1)}, bf16[3,64,256]{2,1,0:T(8,128)(2,1)S(1)}, u32[]{:S(2)}, u32[]{:S(2)}) %collective-permute-start.8) | collective-permute-done | bytes 98336 | tf_op jit(solution)/shard_map/ppermute | solution.py:324
  36.2 1.0 %collective-permute-done.7.refs_1_ = bf16[3,64,256]{2,1,0:T(8,128)(2,1)S(1)} collective-permute-done((bf16[3,64,256]{2,1,0:T(8,128)(2,1)S(1)}, bf16[3,64,256]{2,1,0:T(8,128)(2,1)S(1)}, u32[]{:S(2)}, u32[]{:S(2)}) %collective-permute-start.7) | collective-permute-done | bytes 98336 | tf_op jit(solution)/shard_map/ppermute | solution.py:324
  37.8 1.5 %collective-permute-start.13 = (bf16[3,64,256]{2,1,0:T(8,128)(2,1)S(1)}, bf16[3,64,256]{2,1,0:T(8,128)(2,1)S(1)}, u32[]{:S(2)}, u32[]{:S(2)}) collective-permute-start(bf16[3,64,256]{2,1,0:T(8,128)(2,1)S(1)} %add_second.1.refs_0_), channel_id=1, source_target_pairs={{0,16},{1,17},{2,18},{3,19},{4,6},{5,7},{6,4},{7,5},{8,24},{9,25},... | collective-permute-start | bytes 294920 | tf_op jit(solution)/shard_map/ppermute | solution.py:332
  39.4 1.5 %collective-permute-start.11 = (bf16[3,64,256]{2,1,0:T(8,128)(2,1)S(1)}, bf16[3,64,256]{2,1,0:T(8,128)(2,1)S(1)}, u32[]{:S(2)}, u32[]{:S(2)}) collective-permute-start(bf16[3,64,256]{2,1,0:T(8,128)(2,1)S(1)} %add_second.1.refs_0_), channel_id=1, source_target_pairs={{0,8},{1,9},{2,10},{3,11},{4,5},{5,4},{6,7},{7,6},{8,0},{9,1},{10,... | collective-permute-start | bytes 294920 | tf_op jit(solution)/shard_map/ppermute | solution.py:332
  40.9 2.1 %collective-permute-done.15.refs_3_ = bf16[3,64,256]{2,1,0:T(8,128)(2,1)S(1)} collective-permute-done((bf16[3,64,256]{2,1,0:T(8,128)(2,1)S(1)}, bf16[3,64,256]{2,1,0:T(8,128)(2,1)S(1)}, u32[]{:S(2)}, u32[]{:S(2)}) %collective-permute-start.15) | collective-permute-done | bytes 98336 | tf_op jit(solution)/shard_map/ppermute | solution.py:332
  44.0 1.0 %scale_own.1 = (f32[2,256,256]{2,1,0:T(8,128)}, f32[2,256,256]{2,1,0:T(8,128)}, f32[2,256,256]{2,1,0:T(8,128)}) custom-call(bf16[3,64,256]{2,1,0:T(8,128)(2,1)S(1)} %add_second.1.refs_0_, bf16[3,64,256]{2,1,0:T(8,128)(2,1)S(1)} %collective-permute-done.11.refs_1_, bf16[3,64,256]{2,1,0:T(8,128)(2,1)S(1)} %collective-permute-done.13.refs_2_, ...), custom_call_target="tpu_custom_call" | custom-call | tf_op jit(solution)/shard_map/scale_own/pallas_call | solution.py:337
  45.3 1.0 %scale_other.1 = (f32[2,256,256]{2,1,0:T(8,128)}, f32[2,256,256]{2,1,0:T(8,128)}, f32[2,256,256]{2,1,0:T(8,128)}) custom-call(bf16[3,64,256]{2,1,0:T(8,128)(2,1)S(1)} %collective-permute-done.10.refs_0_, bf16[3,64,256]{2,1,0:T(8,128)(2,1)S(1)} %collective-permute-done.12.refs_1_, ...), custom_call_target="tpu_custom_call", output_to_operand_aliasing={{0}: (4, {}), {1}: (5, {}), {2}: (6, {})} | custom-call | tf_op jit(solution)/shard_map/scale_other/pallas_call | solution.py:338
  (26 shorter events, 3.4 us)
Async XLA Ops:
  2.0 12.1 %collective-permute-start = (bf16[2,128,256]{2,1,0:T(8,128)(2,1)S(1)}, bf16[2,128,256]{2,1,0:T(8,128)(2,1)S(1)}, u32[]{:S(2)}, u32[]{:S(2)}) collective-permute-start(bf16[2,128,256]{2,1,0:T(8,128)(2,1)S(1)} %get-tuple-element.40), channel_id=1, source_target_pairs={{0,2},{1,3},{2,0},{3,1},{4,6},{5,7},{6,4},{7,5},{8,10},{9,11},{10,... | collective-permute-start | bytes 393224 | tf_op jit(solution)/shard_map/ppermute | solution.py:278
  6.1 8.0 %collective-permute-start.1 = (bf16[2,128,256]{2,1,0:T(8,128)(2,1)S(1)}, bf16[2,128,256]{2,1,0:T(8,128)(2,1)S(1)}, u32[]{:S(2)}, u32[]{:S(2)}) collective-permute-start(bf16[2,128,256]{2,1,0:T(8,128)(2,1)S(1)} %get-tuple-element.41), channel_id=1, source_target_pairs={{0,1},{1,0},{2,3},{3,2},{4,5},{5,4},{6,7},{7,6},{8,9},{9,8},{10,11... | collective-permute-start | bytes 393224 | tf_op jit(solution)/shard_map/ppermute | solution.py:278
  7.7 8.8 %collective-permute-start.2 = (bf16[2,128,256]{2,1,0:T(8,128)(2,1)S(1)}, bf16[2,128,256]{2,1,0:T(8,128)(2,1)S(1)}, u32[]{:S(2)}, u32[]{:S(2)}) collective-permute-start(bf16[2,128,256]{2,1,0:T(8,128)(2,1)S(1)} %get-tuple-element.42), channel_id=1, source_target_pairs={{0,3},{1,2},{2,1},{3,0},{4,7},{5,6},{6,5},{7,4},{8,11},{9,10},{10,... | collective-permute-start | bytes 393224 | tf_op jit(solution)/shard_map/ppermute | solution.py:278
  17.1 1.8 %collective-permute-start.3 = (bf16[3,256,256]{2,1,0:T(8,128)(2,1)S(1)}, bf16[3,256,256]{2,1,0:T(8,128)(2,1)S(1)}, u32[]{:S(2)}, u32[]{:S(2)}) collective-permute-start(bf16[3,256,256]{2,1,0:T(8,128)(2,1)S(1)} %get-tuple-element.45), channel_id=1, source_target_pairs={{0,4},{4,0},{8,12},{12,8},{16,20},{20,16},{24,28},{28,24},{1,5},{5... | collective-permute-start | bytes 1179656 | tf_op jit(solution)/shard_map/ppermute | solution.py:301
  18.9 13.6 %copy-start.2 = (bf16[2,256,256]{2,1,0:T(8,128)(2,1)S(1)}, bf16[2,256,256]{2,1,0:T(8,128)(2,1)}, u32[]{:S(2)}) copy-start(bf16[2,256,256]{2,1,0:T(8,128)(2,1)} %wg_ref.1) | copy-start | bytes 786436
  18.9 4.7 %collective-permute-start.4 = (bf16[3,64,256]{2,1,0:T(8,128)(2,1)S(1)}, bf16[3,64,256]{2,1,0:T(8,128)(2,1)S(1)}, u32[]{:S(2)}, u32[]{:S(2)}) collective-permute-start(bf16[3,64,256]{2,1,0:T(8,128)(2,1)S(1)} %get-tuple-element.47), channel_id=1, source_target_pairs={{0,8},{1,9},{2,10},{3,11},{4,5},{5,4},{6,7},{7,6},{8,0},{9,1},{10,... | collective-permute-start | bytes 294920 | tf_op jit(solution)/shard_map/ppermute | solution.py:322
  20.5 4.6 %collective-permute-start.5 = (bf16[3,64,256]{2,1,0:T(8,128)(2,1)S(1)}, bf16[3,64,256]{2,1,0:T(8,128)(2,1)S(1)}, u32[]{:S(2)}, u32[]{:S(2)}) collective-permute-start(bf16[3,64,256]{2,1,0:T(8,128)(2,1)S(1)} %get-tuple-element.48), channel_id=1, source_target_pairs={{0,16},{1,17},{2,18},{3,19},{4,6},{5,7},{6,4},{7,5},{8,24},{9,25},... | collective-permute-start | bytes 294920 | tf_op jit(solution)/shard_map/ppermute | solution.py:322
  22.0 5.5 %collective-permute-start.6 = (bf16[3,64,256]{2,1,0:T(8,128)(2,1)S(1)}, bf16[3,64,256]{2,1,0:T(8,128)(2,1)S(1)}, u32[]{:S(2)}, u32[]{:S(2)}) collective-permute-start(bf16[3,64,256]{2,1,0:T(8,128)(2,1)S(1)} %get-tuple-element.49), channel_id=1, source_target_pairs={{0,24},{1,25},{2,26},{3,27},{4,7},{5,6},{6,5},{7,4},{8,16},{9,17},... | collective-permute-start | bytes 294920 | tf_op jit(solution)/shard_map/ppermute | solution.py:322
  27.5 4.9 %copy-start = (bf16[1,2,256,256]{3,2,1,0:T(8,128)(2,1)S(1)}, bf16[1,2,256,256]{3,2,1,0:T(8,128)(2,1)}, u32[]{:S(2)}) copy-start(bf16[1,2,256,256]{3,2,1,0:T(8,128)(2,1)} %param.8) | copy-start | bytes 786436
  27.5 4.9 %copy-start.1 = (bf16[2,256,256]{2,1,0:T(8,128)(2,1)S(1)}, bf16[2,256,256]{2,1,0:T(8,128)(2,1)}, u32[]{:S(2)}) copy-start(bf16[2,256,256]{2,1,0:T(8,128)(2,1)} %wf_ref.1) | copy-start | bytes 786436
  27.6 6.5 %collective-permute-start.9 = (bf16[3,64,256]{2,1,0:T(8,128)(2,1)S(1)}, bf16[3,64,256]{2,1,0:T(8,128)(2,1)S(1)}, u32[]{:S(2)}, u32[]{:S(2)}) collective-permute-start(bf16[3,64,256]{2,1,0:T(8,128)(2,1)S(1)} %add_first.1._.refs_0_), channel_id=1, source_target_pairs={{0,3},{1,2},{2,1},{3,0},{4,28},{5,29},{6,30},{7,31},{8,11},{9,10},... | collective-permute-start | bytes 294920 | tf_op jit(solution)/shard_map/ppermute | solution.py:324
  30.1 6.2 %collective-permute-start.8 = (bf16[3,64,256]{2,1,0:T(8,128)(2,1)S(1)}, bf16[3,64,256]{2,1,0:T(8,128)(2,1)S(1)}, u32[]{:S(2)}, u32[]{:S(2)}) collective-permute-start(bf16[3,64,256]{2,1,0:T(8,128)(2,1)S(1)} %add_first.1._.refs_0_), channel_id=1, source_target_pairs={{0,2},{1,3},{2,0},{3,1},{4,20},{5,21},{6,22},{7,23},{8,10},{9,11},... | collective-permute-start | bytes 294920 | tf_op jit(solution)/shard_map/ppermute | solution.py:324
  32.0 5.3 %collective-permute-start.7 = (bf16[3,64,256]{2,1,0:T(8,128)(2,1)S(1)}, bf16[3,64,256]{2,1,0:T(8,128)(2,1)S(1)}, u32[]{:S(2)}, u32[]{:S(2)}) collective-permute-start(bf16[3,64,256]{2,1,0:T(8,128)(2,1)S(1)} %add_first.1._.refs_0_), channel_id=1, source_target_pairs={{0,1},{1,0},{2,3},{3,2},{4,12},{5,13},{6,14},{7,15},{8,9},{9,8},{1... | collective-permute-start | bytes 294920 | tf_op jit(solution)/shard_map/ppermute | solution.py:324
  37.3 5.7 %collective-permute-start.15 = (bf16[3,64,256]{2,1,0:T(8,128)(2,1)S(1)}, bf16[3,64,256]{2,1,0:T(8,128)(2,1)S(1)}, u32[]{:S(2)}, u32[]{:S(2)}) collective-permute-start(bf16[3,64,256]{2,1,0:T(8,128)(2,1)S(1)} %add_second.1.refs_0_), channel_id=1, source_target_pairs={{0,24},{1,25},{2,26},{3,27},{4,7},{5,6},{6,5},{7,4},{8,16},{9,17},... | collective-permute-start | bytes 294920 | tf_op jit(solution)/shard_map/ppermute | solution.py:332
  37.8 5.7 %collective-permute-start.13 = (bf16[3,64,256]{2,1,0:T(8,128)(2,1)S(1)}, bf16[3,64,256]{2,1,0:T(8,128)(2,1)S(1)}, u32[]{:S(2)}, u32[]{:S(2)}) collective-permute-start(bf16[3,64,256]{2,1,0:T(8,128)(2,1)S(1)} %add_second.1.refs_0_), channel_id=1, source_target_pairs={{0,16},{1,17},{2,18},{3,19},{4,6},{5,7},{6,4},{7,5},{8,24},{9,25},... | collective-permute-start | bytes 294920 | tf_op jit(solution)/shard_map/ppermute | solution.py:332
  39.4 4.6 %collective-permute-start.11 = (bf16[3,64,256]{2,1,0:T(8,128)(2,1)S(1)}, bf16[3,64,256]{2,1,0:T(8,128)(2,1)S(1)}, u32[]{:S(2)}, u32[]{:S(2)}) collective-permute-start(bf16[3,64,256]{2,1,0:T(8,128)(2,1)S(1)} %add_second.1.refs_0_), channel_id=1, source_target_pairs={{0,8},{1,9},{2,10},{3,11},{4,5},{5,4},{6,7},{7,6},{8,0},{9,1},{10,... | collective-permute-start | bytes 294920 | tf_op jit(solution)/shard_map/ppermute | solution.py:332
  40.8 4.2 %collective-permute-start.10 = (bf16[3,64,256]{2,1,0:T(8,128)(2,1)S(1)}, bf16[3,64,256]{2,1,0:T(8,128)(2,1)S(1)}, u32[]{:S(2)}, u32[]{:S(2)}) collective-permute-start(bf16[3,64,256]{2,1,0:T(8,128)(2,1)S(1)} %add_second.1.refs_0_), channel_id=1, source_target_pairs={{0,4},{4,0},{8,12},{12,8},{16,20},{20,16},{24,28},{28,24},{1,5},{5... | collective-permute-start | bytes 294920 | tf_op jit(solution)/shard_map/ppermute | solution.py:333
  43.0 2.0 %collective-permute-start.16 = (bf16[3,64,256]{2,1,0:T(8,128)(2,1)S(1)}, bf16[3,64,256]{2,1,0:T(8,128)(2,1)S(1)}, u32[]{:S(2)}, u32[]{:S(2)}) collective-permute-start(bf16[3,64,256]{2,1,0:T(8,128)(2,1)S(1)} %collective-permute-done.15.refs_3_), channel_id=1, source_target_pairs={{0,4},{4,0},{8,12},{12,8},{16,20},{20,16},{24,28},{28,24},{1,5},{5... | collective-permute-start | bytes 294920 | tf_op jit(solution)/shard_map/ppermute | solution.py:333
  43.5 1.5 %collective-permute-start.14 = (bf16[3,64,256]{2,1,0:T(8,128)(2,1)S(1)}, bf16[3,64,256]{2,1,0:T(8,128)(2,1)S(1)}, u32[]{:S(2)}, u32[]{:S(2)}) collective-permute-start(bf16[3,64,256]{2,1,0:T(8,128)(2,1)S(1)} %collective-permute-done.13.refs_2_), channel_id=1, source_target_pairs={{0,4},{4,0},{8,12},{12,8},{16,20},{20,16},{24,28},{28,24},{1,5},{5... | collective-permute-start | bytes 294920 | tf_op jit(solution)/shard_map/ppermute | solution.py:333
  44.0 1.3 %collective-permute-start.12 = (bf16[3,64,256]{2,1,0:T(8,128)(2,1)S(1)}, bf16[3,64,256]{2,1,0:T(8,128)(2,1)S(1)}, u32[]{:S(2)}, u32[]{:S(2)}) collective-permute-start(bf16[3,64,256]{2,1,0:T(8,128)(2,1)S(1)} %collective-permute-done.11.refs_1_), channel_id=1, source_target_pairs={{0,4},{4,0},{8,12},{12,8},{16,20},{20,16},{24,28},{28,24},{1,5},{5... | collective-permute-start | bytes 294920 | tf_op jit(solution)/shard_map/ppermute | solution.py:333

commit v6 on v5

--- a/solution.py
+++ b/solution.py
@@ -330,7 +330,8 @@
         functools.partial(add_body, ways), [shape(chunk, BF16)], [VM] * ways + [AN], "add_second"
     )(mine, *gots, token)
     chunks = [done] + [lax.ppermute(done, BOTH, pairs(p, True)) for p in range(1, ways)]
-    others = [lax.ppermute(part, "dp", swap) for part in chunks]
+    crossed = lax.ppermute(done, BOTH, [(i, j ^ regions) for i, j in pairs(1, True)])
+    others = [crossed if i == 1 else lax.ppermute(part, "dp", swap) for i, part in enumerate(chunks)]
     factor = 1.0 / math.sqrt(windows * dp * steps * sites * regions)
     results = [shape((2, chans, chans), F32)] * 3
     extra = dict(out_specs=[HB] * 3, scratch=[pltpu.VMEM((ways,) + chunk, F32), dma((ways, 3))])

time: 46.4 us -> 46.2 us (level)
  waiting for transfers between devices: 18.1 us -> 17 us
  starting transfers between devices: 17.8 us -> 18.6 us
    ppermute x3, waiting for transfers between devices: 3.11 us -> 2.26 us  [per_device(): lax.ppermute(done, BOTH, pairs(p, True))]
    ppermute x4, starting transfers between devices: 0.05 us -> 0.86 us  [the longest x3 0.86 us: per_device(): lax.ppermute(part, 'dp', swap)]
  transfers between devices with their start and end apart: 17 -> 17, of which waited for: 13 -> 12; matrix products, arithmetic and copies ran while one was open for 0% -> 0% of each run, Pallas kernels for 14% -> 14%
where the time goes in v6:
time: 46.2 us; the launch traced here: 46 us
  starting transfers between devices  18.6 us (40%)
  waiting for transfers between devices  17 us (37%)
  Pallas kernels  9.69 us (21%)
  between operations  0.74 us (2%)
    ppermute x3, starting transfers between devices, per_device(): lax.ppermute(part, 'region', [(r, r ^ p) for r in range(regions)])  5.68 us
    ppermute x3, waiting for transfers between devices, per_device(): lax.ppermute(part, BOTH, pairs(p, True))  5.04 us
    ppermute x3, starting transfers between devices, per_device(): gots = [lax.ppermute(mine, BOTH, pairs(p, False)) for p in range(1, ways)]  4.86 us
    ppermute x3, waiting for transfers between devices, per_device(): lax.ppermute(part, 'region', [(r, r ^ p) for r in range(regions)])  4.63 us
    pallas_call x1, Pallas kernels, per_device(): call(functools.partial(local_body, steps, order), [shape(x.shape, F32)] *...  4.11 us
    ppermute x3, waiting for transfers between devices, per_device(): gots = [lax.ppermute(mine, BOTH, pairs(p, False)) for p in range(1, ways)]  3.66 us
    ppermute x3, starting transfers between devices, per_device(): lax.ppermute(done, BOTH, pairs(p, True))  3.55 us
    ppermute x3, starting transfers between devices, per_device(): lax.ppermute(part, BOTH, pairs(p, True))  3.55 us
  transfers between devices with their start and end apart: 17, of which 12 were waited for; matrix products, arithmetic and copies ran while one was open for 0% of the time, Pallas kernels for 14%

profile of v6, /device:TPU:0, one launch (start us, length us, event | category | flops | bytes accessed | tf_op | source)
XLA Modules:
  0.0 46.0 jit_solution(2691919368892071319)
XLA Ops:
  0.6 1.4 %outgoing.1 = (bf16[2,128,256]{2,1,0:T(8,128)(2,1)S(1)}, bf16[2,128,256]{2,1,0:T(8,128)(2,1)S(1)}, bf16[2,128,256]{2,1,0:T(8,128)(2,1)S(1)}) custom-call(s32[8,6]{1,0:T(8,128)} %nb_hbm.3, bf16[2,256,256]{2,1,0:T(8,128)(2,1)} %bitcast.3, bf16[2,6,128,128]{3,2,1,0:T(8,128)(2,1)} %adj_hbm.3), custom_call_target="tpu_custom_call" | custom-call | flops 50331648 | bytes 524288 | tf_op jit(solution)/shard_map/outgoing/pallas_call | solution.py:268
  2.0 4.1 %collective-permute-start = (bf16[2,128,256]{2,1,0:T(8,128)(2,1)S(1)}, bf16[2,128,256]{2,1,0:T(8,128)(2,1)S(1)}, u32[]{:S(2)}, u32[]{:S(2)}) collective-permute-start(bf16[2,128,256]{2,1,0:T(8,128)(2,1)S(1)} %get-tuple-element.40), channel_id=1, source_target_pairs={{0,2},{1,3},{2,0},{3,1},{4,6},{5,7},{6,4},{7,5},{8,10},{9,11},{10,... | collective-permute-start | bytes 393224 | tf_op jit(solution)/shard_map/ppermute | solution.py:278
  6.1 1.6 %collective-permute-start.1 = (bf16[2,128,256]{2,1,0:T(8,128)(2,1)S(1)}, bf16[2,128,256]{2,1,0:T(8,128)(2,1)S(1)}, u32[]{:S(2)}, u32[]{:S(2)}) collective-permute-start(bf16[2,128,256]{2,1,0:T(8,128)(2,1)S(1)} %get-tuple-element.41), channel_id=1, source_target_pairs={{0,1},{1,0},{2,3},{3,2},{4,5},{5,4},{6,7},{7,6},{8,9},{9,8},{10,11... | collective-permute-start | bytes 393224 | tf_op jit(solution)/shard_map/ppermute | solution.py:278
  7.7 4.1 %local.1 = (f32[2,256,256]{2,1,0:T(8,128)S(1)}, f32[2,256,256]{2,1,0:T(8,128)S(1)}, f32[2,256,256]{2,1,0:T(8,128)S(1)}, f32[2,256,256]{2,1,0:T(8,128)S(1)}, f32[...) custom-call(s32[8,6]{1,0:T(8,128)} %nb_hbm.3, ...), custom_call_target="tpu_custom_call" | custom-call | flops 469762048 | bytes 3932160 | tf_op jit(solution)/shard_map/local/pallas_call | solution.py:282
  11.8 2.3 %collective-permute-done.refs_0_ = bf16[2,128,256]{2,1,0:T(8,128)(2,1)S(1)} collective-permute-done((bf16[2,128,256]{2,1,0:T(8,128)(2,1)S(1)}, bf16[2,128,256]{2,1,0:T(8,128)(2,1)S(1)}, u32[]{:S(2)}, u32[]{:S(2)}) %collective-permute-start) | collective-permute-done | bytes 131104 | tf_op jit(solution)/shard_map/ppermute | solution.py:278
  14.1 2.4 %collective-permute-done.2.refs_2_ = bf16[2,128,256]{2,1,0:T(8,128)(2,1)S(1)} collective-permute-done((bf16[2,128,256]{2,1,0:T(8,128)(2,1)S(1)}, bf16[2,128,256]{2,1,0:T(8,128)(2,1)S(1)}, u32[]{:S(2)}, u32[]{:S(2)}) %collective-permute-start.2) | collective-permute-done | bytes 131104 | tf_op jit(solution)/shard_map/ppermute | solution.py:278
  16.5 0.6 %send.1 = (bf16[2,2,256,256]{3,2,1,0:T(8,128)(2,1)S(1)}, bf16[2,256,256]{2,1,0:T(8,128)(2,1)S(1)}, bf16[3,256,256]{2,1,0:T(8,128)(2,1)S(1)}) custom-call(f32[2,256,256]{2,1,0:T(8,128)S(1)} %get-tuple-element.31.df_ref, f32[2,256,256]{2,1,0:T(8,128)S(1)} %get-tuple-element.32.dg_ref, f32[2,256,256]{2,1,0:T(8,128)S(1)} %get-tuple-element.33.direct_ref, ...), custom_call_target="tpu_custom_call" | custom-call | flops 201326592 | bytes 3932160 | tf_op jit(solution)/shard_map/send/pallas_call | solution.py:294
  17.5 1.4 %collective-permute-done.3.got_ref = bf16[3,256,256]{2,1,0:T(8,128)(2,1)S(1)} collective-permute-done((bf16[3,256,256]{2,1,0:T(8,128)(2,1)S(1)}, bf16[3,256,256]{2,1,0:T(8,128)(2,1)S(1)}, u32[]{:S(2)}, u32[]{:S(2)}) %collective-permute-start.3) | collective-permute-done | bytes 393248 | tf_op jit(solution)/shard_map/ppermute | solution.py:301
  18.9 1.6 %collective-permute-start.4 = (bf16[3,64,256]{2,1,0:T(8,128)(2,1)S(1)}, bf16[3,64,256]{2,1,0:T(8,128)(2,1)S(1)}, u32[]{:S(2)}, u32[]{:S(2)}) collective-permute-start(bf16[3,64,256]{2,1,0:T(8,128)(2,1)S(1)} %get-tuple-element.47), channel_id=1, source_target_pairs={{0,8},{1,9},{2,10},{3,11},{4,5},{5,4},{6,7},{7,6},{8,0},{9,1},{10,... | collective-permute-start | bytes 294920 | tf_op jit(solution)/shard_map/ppermute | solution.py:322
  20.5 1.5 %collective-permute-start.5 = (bf16[3,64,256]{2,1,0:T(8,128)(2,1)S(1)}, bf16[3,64,256]{2,1,0:T(8,128)(2,1)S(1)}, u32[]{:S(2)}, u32[]{:S(2)}) collective-permute-start(bf16[3,64,256]{2,1,0:T(8,128)(2,1)S(1)} %get-tuple-element.48), channel_id=1, source_target_pairs={{0,16},{1,17},{2,18},{3,19},{4,6},{5,7},{6,4},{7,5},{8,24},{9,25},... | collective-permute-start | bytes 294920 | tf_op jit(solution)/shard_map/ppermute | solution.py:322
  22.5 1.1 %collective-permute-done.4.refs_1_ = bf16[3,64,256]{2,1,0:T(8,128)(2,1)S(1)} collective-permute-done((bf16[3,64,256]{2,1,0:T(8,128)(2,1)S(1)}, bf16[3,64,256]{2,1,0:T(8,128)(2,1)S(1)}, u32[]{:S(2)}, u32[]{:S(2)}) %collective-permute-start.4) | collective-permute-done | bytes 98336 | tf_op jit(solution)/shard_map/ppermute | solution.py:322
  23.6 1.5 %collective-permute-done.5.refs_2_ = bf16[3,64,256]{2,1,0:T(8,128)(2,1)S(1)} collective-permute-done((bf16[3,64,256]{2,1,0:T(8,128)(2,1)S(1)}, bf16[3,64,256]{2,1,0:T(8,128)(2,1)S(1)}, u32[]{:S(2)}, u32[]{:S(2)}) %collective-permute-start.5) | collective-permute-done | bytes 98336 | tf_op jit(solution)/shard_map/ppermute | solution.py:322
  25.1 2.4 %collective-permute-done.6.refs_3_ = bf16[3,64,256]{2,1,0:T(8,128)(2,1)S(1)} collective-permute-done((bf16[3,64,256]{2,1,0:T(8,128)(2,1)S(1)}, bf16[3,64,256]{2,1,0:T(8,128)(2,1)S(1)}, u32[]{:S(2)}, u32[]{:S(2)}) %collective-permute-start.6) | collective-permute-done | bytes 98336 | tf_op jit(solution)/shard_map/ppermute | solution.py:322
  27.6 2.5 %collective-permute-start.9 = (bf16[3,64,256]{2,1,0:T(8,128)(2,1)S(1)}, bf16[3,64,256]{2,1,0:T(8,128)(2,1)S(1)}, u32[]{:S(2)}, u32[]{:S(2)}) collective-permute-start(bf16[3,64,256]{2,1,0:T(8,128)(2,1)S(1)} %add_first.1._.refs_0_), channel_id=1, source_target_pairs={{0,3},{1,2},{2,1},{3,0},{4,28},{5,29},{6,30},{7,31},{8,11},{9,10},... | collective-permute-start | bytes 294920 | tf_op jit(solution)/shard_map/ppermute | solution.py:324
  30.1 1.9 %collective-permute-start.8 = (bf16[3,64,256]{2,1,0:T(8,128)(2,1)S(1)}, bf16[3,64,256]{2,1,0:T(8,128)(2,1)S(1)}, u32[]{:S(2)}, u32[]{:S(2)}) collective-permute-start(bf16[3,64,256]{2,1,0:T(8,128)(2,1)S(1)} %add_first.1._.refs_0_), channel_id=1, source_target_pairs={{0,2},{1,3},{2,0},{3,1},{4,20},{5,21},{6,22},{7,23},{8,10},{9,11},... | collective-permute-start | bytes 294920 | tf_op jit(solution)/shard_map/ppermute | solution.py:324
  32.5 1.1 %inputs.1 = (bf16[2,256,256]{2,1,0:T(8,128)(2,1)}, f32[8,128]{1,0:T(8,128)S(1)}) custom-call(bf16[2,2,256,256]{3,2,1,0:T(8,128)(2,1)S(1)} %get-tuple-element.43.act_ref, bf16[2,256,256]{2,1,0:T(8,128)(2,1)S(1)} %bitcast.5, bf16[2,256,256]{2,1,0:T(8,128)(2,1)S(1)} %copy-done.1, bf16[2,256,256]{2,1,0:T(8,128)(2,1)S(1)} %copy-done.2, ...), custom_call_target="tpu_custom_call" | custom-call | flops 268435456 | bytes 2097152 | tf_op jit(solution)/shard_map/inputs/pallas_call | solution.py:325
  34.1 2.1 %collective-permute-done.8.refs_2_ = bf16[3,64,256]{2,1,0:T(8,128)(2,1)S(1)} collective-permute-done((bf16[3,64,256]{2,1,0:T(8,128)(2,1)S(1)}, bf16[3,64,256]{2,1,0:T(8,128)(2,1)S(1)}, u32[]{:S(2)}, u32[]{:S(2)}) %collective-permute-start.8) | collective-permute-done | bytes 98336 | tf_op jit(solution)/shard_map/ppermute | solution.py:324
  36.2 1.0 %collective-permute-done.7.refs_1_ = bf16[3,64,256]{2,1,0:T(8,128)(2,1)S(1)} collective-permute-done((bf16[3,64,256]{2,1,0:T(8,128)(2,1)S(1)}, bf16[3,64,256]{2,1,0:T(8,128)(2,1)S(1)}, u32[]{:S(2)}, u32[]{:S(2)}) %collective-permute-start.7) | collective-permute-done | bytes 98336 | tf_op jit(solution)/shard_map/ppermute | solution.py:324
  37.8 1.5 %collective-permute-start.12 = (bf16[3,64,256]{2,1,0:T(8,128)(2,1)S(1)}, bf16[3,64,256]{2,1,0:T(8,128)(2,1)S(1)}, u32[]{:S(2)}, u32[]{:S(2)}) collective-permute-start(bf16[3,64,256]{2,1,0:T(8,128)(2,1)S(1)} %add_second.1.refs_0_), channel_id=1, source_target_pairs={{0,16},{1,17},{2,18},{3,19},{4,6},{5,7},{6,4},{7,5},{8,24},{9,25},... | collective-permute-start | bytes 294920 | tf_op jit(solution)/shard_map/ppermute | solution.py:332
  39.4 1.5 %collective-permute-start.16 = (bf16[3,64,256]{2,1,0:T(8,128)(2,1)S(1)}, bf16[3,64,256]{2,1,0:T(8,128)(2,1)S(1)}, u32[]{:S(2)}, u32[]{:S(2)}) collective-permute-start(bf16[3,64,256]{2,1,0:T(8,128)(2,1)S(1)} %add_second.1.refs_0_), channel_id=1, source_target_pairs={{0,8},{1,9},{2,10},{3,11},{4,5},{5,4},{6,7},{7,6},{8,0},{9,1},{10,... | collective-permute-start | bytes 294920 | tf_op jit(solution)/shard_map/ppermute | solution.py:332
  40.9 0.9 %collective-permute-start.10 = (bf16[3,64,256]{2,1,0:T(8,128)(2,1)S(1)}, bf16[3,64,256]{2,1,0:T(8,128)(2,1)S(1)}, u32[]{:S(2)}, u32[]{:S(2)}) collective-permute-start(bf16[3,64,256]{2,1,0:T(8,128)(2,1)S(1)} %add_second.1.refs_0_), channel_id=1, source_target_pairs={{0,4},{4,0},{8,12},{12,8},{16,20},{20,16},{24,28},{28,24},{1,5},{5... | collective-permute-start | bytes 294920 | tf_op jit(solution)/shard_map/ppermute | solution.py:334
  41.7 1.3 %collective-permute-done.14.refs_3_ = bf16[3,64,256]{2,1,0:T(8,128)(2,1)S(1)} collective-permute-done((bf16[3,64,256]{2,1,0:T(8,128)(2,1)S(1)}, bf16[3,64,256]{2,1,0:T(8,128)(2,1)S(1)}, u32[]{:S(2)}, u32[]{:S(2)}) %collective-permute-start.14) | collective-permute-done | bytes 98336 | tf_op jit(solution)/shard_map/ppermute | solution.py:332
  44.0 1.0 %scale_own.1 = (f32[2,256,256]{2,1,0:T(8,128)}, f32[2,256,256]{2,1,0:T(8,128)}, f32[2,256,256]{2,1,0:T(8,128)}) custom-call(bf16[3,64,256]{2,1,0:T(8,128)(2,1)S(1)} %add_second.1.refs_0_, bf16[3,64,256]{2,1,0:T(8,128)(2,1)S(1)} %collective-permute-done.16.refs_1_, bf16[3,64,256]{2,1,0:T(8,128)(2,1)S(1)} %collective-permute-done.12.refs_2_, ...), custom_call_target="tpu_custom_call" | custom-call | tf_op jit(solution)/shard_map/scale_own/pallas_call | solution.py:338
  45.0 1.0 %scale_other.1 = (f32[2,256,256]{2,1,0:T(8,128)}, f32[2,256,256]{2,1,0:T(8,128)}, f32[2,256,256]{2,1,0:T(8,128)}) custom-call(bf16[3,64,256]{2,1,0:T(8,128)(2,1)S(1)} %collective-permute-done.10.refs_0_, bf16[3,64,256]{2,1,0:T(8,128)(2,1)S(1)} %collective-permute-done.11.refs_1_, ...), custom_call_target="tpu_custom_call", output_to_operand_aliasing={{0}: (4, {}), {1}: (5, {}), {2}: (6, {})} | custom-call | tf_op jit(solution)/shard_map/scale_other/pallas_call | solution.py:339
  (26 shorter events, 3.6 us)
Async XLA Ops:
  2.0 12.1 %collective-permute-start = (bf16[2,128,256]{2,1,0:T(8,128)(2,1)S(1)}, bf16[2,128,256]{2,1,0:T(8,128)(2,1)S(1)}, u32[]{:S(2)}, u32[]{:S(2)}) collective-permute-start(bf16[2,128,256]{2,1,0:T(8,128)(2,1)S(1)} %get-tuple-element.40), channel_id=1, source_target_pairs={{0,2},{1,3},{2,0},{3,1},{4,6},{5,7},{6,4},{7,5},{8,10},{9,11},{10,... | collective-permute-start | bytes 393224 | tf_op jit(solution)/shard_map/ppermute | solution.py:278
  6.1 8.0 %collective-permute-start.1 = (bf16[2,128,256]{2,1,0:T(8,128)(2,1)S(1)}, bf16[2,128,256]{2,1,0:T(8,128)(2,1)S(1)}, u32[]{:S(2)}, u32[]{:S(2)}) collective-permute-start(bf16[2,128,256]{2,1,0:T(8,128)(2,1)S(1)} %get-tuple-element.41), channel_id=1, source_target_pairs={{0,1},{1,0},{2,3},{3,2},{4,5},{5,4},{6,7},{7,6},{8,9},{9,8},{10,11... | collective-permute-start | bytes 393224 | tf_op jit(solution)/shard_map/ppermute | solution.py:278
  7.7 8.8 %collective-permute-start.2 = (bf16[2,128,256]{2,1,0:T(8,128)(2,1)S(1)}, bf16[2,128,256]{2,1,0:T(8,128)(2,1)S(1)}, u32[]{:S(2)}, u32[]{:S(2)}) collective-permute-start(bf16[2,128,256]{2,1,0:T(8,128)(2,1)S(1)} %get-tuple-element.42), channel_id=1, source_target_pairs={{0,3},{1,2},{2,1},{3,0},{4,7},{5,6},{6,5},{7,4},{8,11},{9,10},{10,... | collective-permute-start | bytes 393224 | tf_op jit(solution)/shard_map/ppermute | solution.py:278
  17.1 1.8 %collective-permute-start.3 = (bf16[3,256,256]{2,1,0:T(8,128)(2,1)S(1)}, bf16[3,256,256]{2,1,0:T(8,128)(2,1)S(1)}, u32[]{:S(2)}, u32[]{:S(2)}) collective-permute-start(bf16[3,256,256]{2,1,0:T(8,128)(2,1)S(1)} %get-tuple-element.45), channel_id=1, source_target_pairs={{0,4},{4,0},{8,12},{12,8},{16,20},{20,16},{24,28},{28,24},{1,5},{5... | collective-permute-start | bytes 1179656 | tf_op jit(solution)/shard_map/ppermute | solution.py:301
  18.9 13.6 %copy-start.2 = (bf16[2,256,256]{2,1,0:T(8,128)(2,1)S(1)}, bf16[2,256,256]{2,1,0:T(8,128)(2,1)}, u32[]{:S(2)}) copy-start(bf16[2,256,256]{2,1,0:T(8,128)(2,1)} %wg_ref.1) | copy-start | bytes 786436
  18.9 4.7 %collective-permute-start.4 = (bf16[3,64,256]{2,1,0:T(8,128)(2,1)S(1)}, bf16[3,64,256]{2,1,0:T(8,128)(2,1)S(1)}, u32[]{:S(2)}, u32[]{:S(2)}) collective-permute-start(bf16[3,64,256]{2,1,0:T(8,128)(2,1)S(1)} %get-tuple-element.47), channel_id=1, source_target_pairs={{0,8},{1,9},{2,10},{3,11},{4,5},{5,4},{6,7},{7,6},{8,0},{9,1},{10,... | collective-permute-start | bytes 294920 | tf_op jit(solution)/shard_map/ppermute | solution.py:322
  20.5 4.6 %collective-permute-start.5 = (bf16[3,64,256]{2,1,0:T(8,128)(2,1)S(1)}, bf16[3,64,256]{2,1,0:T(8,128)(2,1)S(1)}, u32[]{:S(2)}, u32[]{:S(2)}) collective-permute-start(bf16[3,64,256]{2,1,0:T(8,128)(2,1)S(1)} %get-tuple-element.48), channel_id=1, source_target_pairs={{0,16},{1,17},{2,18},{3,19},{4,6},{5,7},{6,4},{7,5},{8,24},{9,25},... | collective-permute-start | bytes 294920 | tf_op jit(solution)/shard_map/ppermute | solution.py:322
  22.0 5.5 %collective-permute-start.6 = (bf16[3,64,256]{2,1,0:T(8,128)(2,1)S(1)}, bf16[3,64,256]{2,1,0:T(8,128)(2,1)S(1)}, u32[]{:S(2)}, u32[]{:S(2)}) collective-permute-start(bf16[3,64,256]{2,1,0:T(8,128)(2,1)S(1)} %get-tuple-element.49), channel_id=1, source_target_pairs={{0,24},{1,25},{2,26},{3,27},{4,7},{5,6},{6,5},{7,4},{8,16},{9,17},... | collective-permute-start | bytes 294920 | tf_op jit(solution)/shard_map/ppermute | solution.py:322
  27.5 4.9 %copy-start = (bf16[1,2,256,256]{3,2,1,0:T(8,128)(2,1)S(1)}, bf16[1,2,256,256]{3,2,1,0:T(8,128)(2,1)}, u32[]{:S(2)}) copy-start(bf16[1,2,256,256]{3,2,1,0:T(8,128)(2,1)} %param.8) | copy-start | bytes 786436
  27.5 4.9 %copy-start.1 = (bf16[2,256,256]{2,1,0:T(8,128)(2,1)S(1)}, bf16[2,256,256]{2,1,0:T(8,128)(2,1)}, u32[]{:S(2)}) copy-start(bf16[2,256,256]{2,1,0:T(8,128)(2,1)} %wf_ref.1) | copy-start | bytes 786436
  27.6 6.5 %collective-permute-start.9 = (bf16[3,64,256]{2,1,0:T(8,128)(2,1)S(1)}, bf16[3,64,256]{2,1,0:T(8,128)(2,1)S(1)}, u32[]{:S(2)}, u32[]{:S(2)}) collective-permute-start(bf16[3,64,256]{2,1,0:T(8,128)(2,1)S(1)} %add_first.1._.refs_0_), channel_id=1, source_target_pairs={{0,3},{1,2},{2,1},{3,0},{4,28},{5,29},{6,30},{7,31},{8,11},{9,10},... | collective-permute-start | bytes 294920 | tf_op jit(solution)/shard_map/ppermute | solution.py:324
  30.1 6.2 %collective-permute-start.8 = (bf16[3,64,256]{2,1,0:T(8,128)(2,1)S(1)}, bf16[3,64,256]{2,1,0:T(8,128)(2,1)S(1)}, u32[]{:S(2)}, u32[]{:S(2)}) collective-permute-start(bf16[3,64,256]{2,1,0:T(8,128)(2,1)S(1)} %add_first.1._.refs_0_), channel_id=1, source_target_pairs={{0,2},{1,3},{2,0},{3,1},{4,20},{5,21},{6,22},{7,23},{8,10},{9,11},... | collective-permute-start | bytes 294920 | tf_op jit(solution)/shard_map/ppermute | solution.py:324
  32.0 5.3 %collective-permute-start.7 = (bf16[3,64,256]{2,1,0:T(8,128)(2,1)S(1)}, bf16[3,64,256]{2,1,0:T(8,128)(2,1)S(1)}, u32[]{:S(2)}, u32[]{:S(2)}) collective-permute-start(bf16[3,64,256]{2,1,0:T(8,128)(2,1)S(1)} %add_first.1._.refs_0_), channel_id=1, source_target_pairs={{0,1},{1,0},{2,3},{3,2},{4,12},{5,13},{6,14},{7,15},{8,9},{9,8},{1... | collective-permute-start | bytes 294920 | tf_op jit(solution)/shard_map/ppermute | solution.py:324
  37.3 5.7 %collective-permute-start.14 = (bf16[3,64,256]{2,1,0:T(8,128)(2,1)S(1)}, bf16[3,64,256]{2,1,0:T(8,128)(2,1)S(1)}, u32[]{:S(2)}, u32[]{:S(2)}) collective-permute-start(bf16[3,64,256]{2,1,0:T(8,128)(2,1)S(1)} %add_second.1.refs_0_), channel_id=1, source_target_pairs={{0,24},{1,25},{2,26},{3,27},{4,7},{5,6},{6,5},{7,4},{8,16},{9,17},... | collective-permute-start | bytes 294920 | tf_op jit(solution)/shard_map/ppermute | solution.py:332
  37.8 5.7 %collective-permute-start.12 = (bf16[3,64,256]{2,1,0:T(8,128)(2,1)S(1)}, bf16[3,64,256]{2,1,0:T(8,128)(2,1)S(1)}, u32[]{:S(2)}, u32[]{:S(2)}) collective-permute-start(bf16[3,64,256]{2,1,0:T(8,128)(2,1)S(1)} %add_second.1.refs_0_), channel_id=1, source_target_pairs={{0,16},{1,17},{2,18},{3,19},{4,6},{5,7},{6,4},{7,5},{8,24},{9,25},... | collective-permute-start | bytes 294920 | tf_op jit(solution)/shard_map/ppermute | solution.py:332
  39.4 4.6 %collective-permute-start.16 = (bf16[3,64,256]{2,1,0:T(8,128)(2,1)S(1)}, bf16[3,64,256]{2,1,0:T(8,128)(2,1)S(1)}, u32[]{:S(2)}, u32[]{:S(2)}) collective-permute-start(bf16[3,64,256]{2,1,0:T(8,128)(2,1)S(1)} %add_second.1.refs_0_), channel_id=1, source_target_pairs={{0,8},{1,9},{2,10},{3,11},{4,5},{5,4},{6,7},{7,6},{8,0},{9,1},{10,... | collective-permute-start | bytes 294920 | tf_op jit(solution)/shard_map/ppermute | solution.py:332
  40.8 4.1 %collective-permute-start.11 = (bf16[3,64,256]{2,1,0:T(8,128)(2,1)S(1)}, bf16[3,64,256]{2,1,0:T(8,128)(2,1)S(1)}, u32[]{:S(2)}, u32[]{:S(2)}) collective-permute-start(bf16[3,64,256]{2,1,0:T(8,128)(2,1)S(1)} %add_second.1.refs_0_), channel_id=1, source_target_pairs={{0,12},{1,13},{2,14},{3,15},{4,1},{5,0},{6,3},{7,2},{8,4},{9,5},{1... | collective-permute-start | bytes 294920 | tf_op jit(solution)/shard_map/ppermute | solution.py:333
  40.9 4.1 %collective-permute-start.10 = (bf16[3,64,256]{2,1,0:T(8,128)(2,1)S(1)}, bf16[3,64,256]{2,1,0:T(8,128)(2,1)S(1)}, u32[]{:S(2)}, u32[]{:S(2)}) collective-permute-start(bf16[3,64,256]{2,1,0:T(8,128)(2,1)S(1)} %add_second.1.refs_0_), channel_id=1, source_target_pairs={{0,4},{4,0},{8,12},{12,8},{16,20},{20,16},{24,28},{28,24},{1,5},{5... | collective-permute-start | bytes 294920 | tf_op jit(solution)/shard_map/ppermute | solution.py:334
  43.0 2.0 %collective-permute-start.15 = (bf16[3,64,256]{2,1,0:T(8,128)(2,1)S(1)}, bf16[3,64,256]{2,1,0:T(8,128)(2,1)S(1)}, u32[]{:S(2)}, u32[]{:S(2)}) collective-permute-start(bf16[3,64,256]{2,1,0:T(8,128)(2,1)S(1)} %collective-permute-done.14.refs_3_), channel_id=1, source_target_pairs={{0,4},{4,0},{8,12},{12,8},{16,20},{20,16},{24,28},{28,24},{1,5},{5... | collective-permute-start | bytes 294920 | tf_op jit(solution)/shard_map/ppermute | solution.py:334
  43.5 1.5 %collective-permute-start.13 = (bf16[3,64,256]{2,1,0:T(8,128)(2,1)S(1)}, bf16[3,64,256]{2,1,0:T(8,128)(2,1)S(1)}, u32[]{:S(2)}, u32[]{:S(2)}) collective-permute-start(bf16[3,64,256]{2,1,0:T(8,128)(2,1)S(1)} %collective-permute-done.12.refs_2_), channel_id=1, source_target_pairs={{0,4},{4,0},{8,12},{12,8},{16,20},{20,16},{24,28},{28,24},{1,5},{5... | collective-permute-start | bytes 294920 | tf_op jit(solution)/shard_map/ppermute | solution.py:334

commit v7 on v5

--- a/solution.py
+++ b/solution.py
@@ -155,6 +155,14 @@
     return functools.reduce(jnp.add, terms)
 
 
+def chunk_of(ref, mine, p, rows):
+    return ref[:, pl.ds(pl.multiple_of(jnp.bitwise_xor(mine, p) * rows, rows), rows), :]
+
+
+def swapped(ref):
+    return [0, *range(2, ref.shape[0] + 1)]
+
+
 def half_of(tap, steps, xt_ref, ht_ref, mix_ref, act_ref, sums_ref):
     if tap == 0:
         mix = mix_ref[...]
@@ -164,8 +172,8 @@
 
 
 def send_body(regions, steps, df_ref, dg_ref, direct_ref, local_ref, mix_ref, xt_ref, ht_ref, wt_ref, mask_ref, *refs):
-    arrived, (act_ref, sums_ref, send_ref) = refs[: regions - 1], refs[regions - 1 :]
-    lane, _, _ = lane_of()
+    arrived, (act_ref, sums_ref, cross_ref, rest_ref, made_ref) = refs[: regions - 1], refs[regions - 1 :]
+    lane, _, other = lane_of()
     total, sites, _ = local_ref.shape
     tiles = sites // TILE
     for t in range(total):
@@ -173,7 +181,7 @@
         for j in range(tiles):
             part = local_ref[t, j * TILE : (j + 1) * TILE, :]
             for s in range(regions - 1):
-                part += mask_ref[s, j, :1] * arrived[s][t].astype(F32)
+                part += (mask_ref[s, j, :1].astype(BF16) * arrived[s][t]).astype(F32)
             summed.append(part.astype(BF16))
         summed = jnp.concatenate(summed, axis=0)
         sums_ref[t] = summed
@@ -185,17 +193,23 @@
         @pl.when(lane == 1 - tap)
         def _():
             for i, part in enumerate(half_of(tap, steps, xt_ref, ht_ref, mix_ref, act_ref, sums_ref)):
-                send_ref[i] = part.astype(BF16)
-
-
-def keep_body(steps, mix_ref, xt_ref, ht_ref, act_ref, sums_ref, keep_ref):
-    lane, _, _ = lane_of()
+                made_ref[i] = part
+
+    rows = cross_ref.shape[1]
+    cross_ref[...] = chunk_of(made_ref, other, 1, rows).astype(BF16)
+    for i, p in enumerate(swapped(rest_ref)):
+        rest_ref[i] = chunk_of(made_ref, other, p, rows).astype(BF16)
+
+
+def keep_body(steps, mix_ref, xt_ref, ht_ref, act_ref, sums_ref, keep_ref, along_ref):
+    lane, mine, _ = lane_of()
     for tap in range(2):
 
         @pl.when(lane == tap)
         def _():
             for i, part in enumerate(half_of(tap, steps, xt_ref, ht_ref, mix_ref, act_ref, sums_ref)):
                 keep_ref[i] = part
+    along_ref[...] = chunk_of(keep_ref, mine, 1, along_ref.shape[1]).astype(BF16)
 
 
 def inputs_body(steps, act_ref, cot_ref, wf_ref, wg_ref, _, out_ref, token_ref):
@@ -209,23 +223,25 @@
         out_ref[t] = grad.astype(BF16)
 
 
-def split_body(ways, keep_ref, got_ref, own_ref, *sends):
+def split_body(keep_ref, got_ref, cross_ref, own_ref, *sends):
     _, mine, _ = lane_of()
-    rows = own_ref.shape[1]
-
-    def chunk(p):
-        place = pl.ds(pl.multiple_of(jnp.bitwise_xor(mine, p) * rows, rows), rows)
-        return keep_ref[:, place, :] + got_ref[:, place, :].astype(F32)
-
-    own_ref[...] = chunk(0)
-    for p, send in enumerate(sends, 1):
-        send[...] = chunk(p).astype(BF16)
+    sends[-1][...] = cross_ref[...]
+    for i, p in enumerate(swapped(got_ref)):
+        part = chunk_of(keep_ref, mine, p, own_ref.shape[1]) + got_ref[i].astype(F32)
+        if i == 0:
+            own_ref[...] = part
+        else:
+            sends[i - 1][...] = part.astype(BF16)
 
 
 def tree(parts):
     while len(parts) > 1:
         parts = [parts[i] + parts[i + 1] for i in range(0, len(parts), 2)]
     return parts[0]
+
+
+def sum_body(*refs):
+    refs[-1][...] = functools.reduce(jnp.add, [ref[...].astype(F32) for ref in refs[:-1]]).astype(BF16)
 
 
 def add_body(ways, *refs):
@@ -291,21 +307,20 @@
         ],
         flops=14 * block * chans, nbytes=30 * block,
     )(*in_hbm(neighbours, x, cot, w_filter, w_gate, w_mix, adjacency))
-    act_cot, sums, send = call(
+    rows = chans // ways
+    chunk = (3, rows, chans)
+    act_cot, sums, cross, rest = call(
         functools.partial(send_body, regions, steps),
-        [shape((2,) + x.shape, BF16), shape(x.shape, BF16), shape((3, chans, chans), BF16)],
-        [VM] * (9 + regions - 1), "send",
+        [shape((2,) + x.shape, BF16), shape(x.shape, BF16), shape(chunk, BF16), shape((ways - 1,) + chunk, BF16)],
+        [VM] * (9 + regions - 1), "send", scratch=[pltpu.VMEM((3, chans, chans), F32)],
         flops=6 * block * chans, nbytes=30 * block,
     )(d_filter, d_gate, direct, local, mix, xt, ht, wt, mask, *arrived)
     swap = [(i, i ^ 1) for i in range(dp)]
-    got = lax.ppermute(send, "dp", swap)
-    (keep,) = call(
-        functools.partial(keep_body, steps), [shape((3, chans, chans), F32)], [VM] * 5, "keep",
+    got = lax.ppermute(rest, "dp", swap)
+    keep, along = call(
+        functools.partial(keep_body, steps), [shape((3, chans, chans), F32), shape(chunk, BF16)], [VM] * 5, "keep",
         flops=6 * block * chans, nbytes=20 * block,
     )(mix, xt, ht, act_cot, sums)
-
-    rows = chans // ways
-    chunk = (3, rows, chans)
 
     def pairs(p, turn):
         result = []
@@ -315,12 +330,16 @@
                 result.append((d * regions + r, e * regions + q))
         return result
 
-    own, *sends = call(
-        functools.partial(split_body, ways),
-        [shape(chunk, F32)] + [shape(chunk, BF16)] * (ways - 1), [VM] * 2, "split",
-    )(keep, got)
-    gots = [lax.ppermute(part, BOTH, pairs(p, True)) for p, part in enumerate(sends, 1)]
-    (mine,) = call(functools.partial(add_body, ways), [shape(chunk, BF16)], [VM] * ways, "add_first")(own, *gots)
+    def crossed(p, turn):
+        return [(i, j ^ regions) for i, j in pairs(p, turn)]
+
+    gots = [lax.ppermute(along, BOTH, pairs(1, True))]
+    own, *sends, cross = call(
+        split_body, [shape(chunk, F32)] + [shape(chunk, BF16)] * (ways - 1), [VM] * 3, "split"
+    )(keep, got, cross)
+    gots += [lax.ppermute(part, BOTH, pairs(p, True)) for p, part in list(enumerate(sends, 2))[::-1]]
+    gots += [lax.ppermute(cross, BOTH, crossed(1, False))]
+    (mine,) = call(sum_body, [shape(chunk, BF16)], [VM] * (ways + 1), "add_first")(own, *gots)
     gots = [lax.ppermute(mine, BOTH, pairs(p, False)) for p in range(1, ways)]
     grad_inputs, token = call(
         functools.partial(inputs_body, steps), [shape(x.shape, BF16), shape((8, 128), F32)], [VM] * 4 + [AN], "inputs",
@@ -330,7 +349,8 @@
         functools.partial(add_body, ways), [shape(chunk, BF16)], [VM] * ways + [AN], "add_second"
     )(mine, *gots, token)
     chunks = [done] + [lax.ppermute(done, BOTH, pairs(p, True)) for p in range(1, ways)]
-    others = [lax.ppermute(part, "dp", swap) for part in chunks]
+    direct = lax.ppermute(done, BOTH, crossed(1, True))
+    others = [direct if i == 1 else lax.ppermute(part, "dp", swap) for i, part in enumerate(chunks)]
     factor = 1.0 / math.sqrt(windows * dp * steps * sites * regions)
     results = [shape((2, chans, chans), F32)] * 3
     extra = dict(out_specs=[HB] * 3, scratch=[pltpu.VMEM((ways,) + chunk, F32), dma((ways, 3))])

time: 46.4 us -> 45.9 us (0.989)
  waiting for transfers between devices: 18.1 us -> 14.8 us
  starting transfers between devices: 17.8 us -> 20.4 us
    ppermute x5 -> x7, starting transfers between devices: 0.13 us -> 4 us  [the longest x1 1.83 us: per_device(): gots += [lax.ppermute(cross, BOTH, crossed(1, False))]]
    ppermute x3 -> x2, waiting for transfers between devices: 5.04 us -> 2.28 us  [per_device(): lax.ppermute(part, BOTH, pairs(p, True))]
    ppermute x3 -> x2, starting transfers between devices: 3.55 us -> 2.67 us  [per_device(): lax.ppermute(part, BOTH, pairs(p, True))]
    ppermute x5 -> x7, waiting for transfers between devices: 1.61 us -> 0.92 us  [the longest x1 0.9 us: per_device(): gots += [lax.ppermute(cross, BOTH, crossed(1, False))]]
  transfers between devices with their start and end apart: 17 -> 18, of which waited for: 13 -> 10; matrix products, arithmetic and copies ran while one was open for 0% -> 0% of each run, Pallas kernels for 14% -> 14%
where the time goes in v7:
time: 45.9 us; the launch traced here: 45.7 us
  starting transfers between devices  20.4 us (44%)
  waiting for transfers between devices  14.8 us (32%)
  Pallas kernels  9.73 us (21%)
  between operations  0.74 us (2%)
    ppermute x3, starting transfers between devices, per_device(): lax.ppermute(part, 'region', [(r, r ^ p) for r in range(regions)])  5.68 us
    ppermute x3, waiting for transfers between devices, per_device(): lax.ppermute(part, 'region', [(r, r ^ p) for r in range(regions)])  4.63 us
    ppermute x3, starting transfers between devices, per_device(): gots = [lax.ppermute(mine, BOTH, pairs(p, False)) for p in range(1, ways)]  4.45 us
    pallas_call x1, Pallas kernels, per_device(): call(functools.partial(local_body, steps, order), [shape(x.shape, F32)] *...  4.11 us
    ppermute x3, waiting for transfers between devices, per_device(): gots = [lax.ppermute(mine, BOTH, pairs(p, False)) for p in range(1, ways)]  3.59 us
    ppermute x3, starting transfers between devices, per_device(): lax.ppermute(done, BOTH, pairs(p, True))  3.55 us
    ppermute x3, waiting for transfers between devices, per_device(): lax.ppermute(done, BOTH, pairs(p, True))  3.42 us
    ppermute x2, starting transfers between devices, per_device(): lax.ppermute(part, BOTH, pairs(p, True))  2.67 us
  transfers between devices with their start and end apart: 18, of which 10 were waited for; matrix products, arithmetic and copies ran while one was open for 0% of the time, Pallas kernels for 14%

profile of v7, /device:TPU:0, one launch (start us, length us, event | category | flops | bytes accessed | tf_op | source)
XLA Modules:
  0.0 45.7 jit_solution(8821675579139078801)
XLA Ops:
  0.6 1.4 %outgoing.1 = (bf16[2,128,256]{2,1,0:T(8,128)(2,1)S(1)}, bf16[2,128,256]{2,1,0:T(8,128)(2,1)S(1)}, bf16[2,128,256]{2,1,0:T(8,128)(2,1)S(1)}) custom-call(s32[8,6]{1,0:T(8,128)} %nb_hbm.3, bf16[2,256,256]{2,1,0:T(8,128)(2,1)} %bitcast.3, bf16[2,6,128,128]{3,2,1,0:T(8,128)(2,1)} %adj_hbm.3), custom_call_target="tpu_custom_call" | custom-call | flops 50331648 | bytes 524288 | tf_op jit(solution)/shard_map/outgoing/pallas_call | solution.py:284
  2.0 4.1 %collective-permute-start = (bf16[2,128,256]{2,1,0:T(8,128)(2,1)S(1)}, bf16[2,128,256]{2,1,0:T(8,128)(2,1)S(1)}, u32[]{:S(2)}, u32[]{:S(2)}) collective-permute-start(bf16[2,128,256]{2,1,0:T(8,128)(2,1)S(1)} %get-tuple-element.43), channel_id=1, source_target_pairs={{0,2},{1,3},{2,0},{3,1},{4,6},{5,7},{6,4},{7,5},{8,10},{9,11},{10,... | collective-permute-start | bytes 393224 | tf_op jit(solution)/shard_map/ppermute | solution.py:294
  6.1 1.6 %collective-permute-start.1 = (bf16[2,128,256]{2,1,0:T(8,128)(2,1)S(1)}, bf16[2,128,256]{2,1,0:T(8,128)(2,1)S(1)}, u32[]{:S(2)}, u32[]{:S(2)}) collective-permute-start(bf16[2,128,256]{2,1,0:T(8,128)(2,1)S(1)} %get-tuple-element.44), channel_id=1, source_target_pairs={{0,1},{1,0},{2,3},{3,2},{4,5},{5,4},{6,7},{7,6},{8,9},{9,8},{10,11... | collective-permute-start | bytes 393224 | tf_op jit(solution)/shard_map/ppermute | solution.py:294
  7.7 4.1 %local.1 = (f32[2,256,256]{2,1,0:T(8,128)S(1)}, f32[2,256,256]{2,1,0:T(8,128)S(1)}, f32[2,256,256]{2,1,0:T(8,128)S(1)}, f32[2,256,256]{2,1,0:T(8,128)S(1)}, f32[...) custom-call(s32[8,6]{1,0:T(8,128)} %nb_hbm.3, ...), custom_call_target="tpu_custom_call" | custom-call | flops 469762048 | bytes 3932160 | tf_op jit(solution)/shard_map/local/pallas_call | solution.py:298
  11.8 2.3 %collective-permute-done.refs_0_ = bf16[2,128,256]{2,1,0:T(8,128)(2,1)S(1)} collective-permute-done((bf16[2,128,256]{2,1,0:T(8,128)(2,1)S(1)}, bf16[2,128,256]{2,1,0:T(8,128)(2,1)S(1)}, u32[]{:S(2)}, u32[]{:S(2)}) %collective-permute-start) | collective-permute-done | bytes 131104 | tf_op jit(solution)/shard_map/ppermute | solution.py:294
  14.1 2.4 %collective-permute-done.2.refs_2_ = bf16[2,128,256]{2,1,0:T(8,128)(2,1)S(1)} collective-permute-done((bf16[2,128,256]{2,1,0:T(8,128)(2,1)S(1)}, bf16[2,128,256]{2,1,0:T(8,128)(2,1)S(1)}, u32[]{:S(2)}, u32[]{:S(2)}) %collective-permute-start.2) | collective-permute-done | bytes 131104 | tf_op jit(solution)/shard_map/ppermute | solution.py:294
  17.5 1.6 %collective-permute-start.4 = (bf16[3,64,256]{2,1,0:T(8,128)(2,1)S(1)}, bf16[3,64,256]{2,1,0:T(8,128)(2,1)S(1)}, u32[]{:S(2)}, u32[]{:S(2)}) collective-permute-start(bf16[3,64,256]{2,1,0:T(8,128)(2,1)S(1)} %get-tuple-element.52), channel_id=1, source_target_pairs={{0,8},{1,9},{2,10},{3,11},{4,5},{5,4},{6,7},{7,6},{8,0},{9,1},{10,... | collective-permute-start | bytes 294920 | tf_op jit(solution)/shard_map/ppermute | solution.py:336
  19.2 2.2 %collective-permute-start.5 = (bf16[3,64,256]{2,1,0:T(8,128)(2,1)S(1)}, bf16[3,64,256]{2,1,0:T(8,128)(2,1)S(1)}, u32[]{:S(2)}, u32[]{:S(2)}) collective-permute-start(bf16[3,64,256]{2,1,0:T(8,128)(2,1)S(1)} %get-tuple-element.53), channel_id=1, source_target_pairs={{0,24},{1,25},{2,26},{3,27},{4,7},{5,6},{6,5},{7,4},{8,16},{9,17},... | collective-permute-start | bytes 294920 | tf_op jit(solution)/shard_map/ppermute | solution.py:340
  21.8 1.8 %collective-permute-start.7 = (bf16[3,64,256]{2,1,0:T(8,128)(2,1)S(1)}, bf16[3,64,256]{2,1,0:T(8,128)(2,1)S(1)}, u32[]{:S(2)}, u32[]{:S(2)}) collective-permute-start(bf16[3,64,256]{2,1,0:T(8,128)(2,1)S(1)} %get-tuple-element.55), channel_id=1, source_target_pairs={{0,5},{1,4},{2,7},{3,6},{4,8},{5,9},{6,10},{7,11},{8,13},{9,12},{1... | collective-permute-start | bytes 294920 | tf_op jit(solution)/shard_map/ppermute | solution.py:341
  23.7 1.1 %collective-permute-done.5.refs_2_ = bf16[3,64,256]{2,1,0:T(8,128)(2,1)S(1)} collective-permute-done((bf16[3,64,256]{2,1,0:T(8,128)(2,1)S(1)}, bf16[3,64,256]{2,1,0:T(8,128)(2,1)S(1)}, u32[]{:S(2)}, u32[]{:S(2)}) %collective-permute-start.5) | collective-permute-done | bytes 98336 | tf_op jit(solution)/shard_map/ppermute | solution.py:340
  24.7 1.2 %collective-permute-done.6.refs_3_ = bf16[3,64,256]{2,1,0:T(8,128)(2,1)S(1)} collective-permute-done((bf16[3,64,256]{2,1,0:T(8,128)(2,1)S(1)}, bf16[3,64,256]{2,1,0:T(8,128)(2,1)S(1)}, u32[]{:S(2)}, u32[]{:S(2)}) %collective-permute-start.6) | collective-permute-done | bytes 98336 | tf_op jit(solution)/shard_map/ppermute | solution.py:340
  26.0 0.9 %collective-permute-done.7.refs_4_ = bf16[3,64,256]{2,1,0:T(8,128)(2,1)S(1)} collective-permute-done((bf16[3,64,256]{2,1,0:T(8,128)(2,1)S(1)}, bf16[3,64,256]{2,1,0:T(8,128)(2,1)S(1)}, u32[]{:S(2)}, u32[]{:S(2)}) %collective-permute-start.7) | collective-permute-done | bytes 98336 | tf_op jit(solution)/shard_map/ppermute | solution.py:341
  26.9 2.5 %collective-permute-start.10 = (bf16[3,64,256]{2,1,0:T(8,128)(2,1)S(1)}, bf16[3,64,256]{2,1,0:T(8,128)(2,1)S(1)}, u32[]{:S(2)}, u32[]{:S(2)}) collective-permute-start(bf16[3,64,256]{2,1,0:T(8,128)(2,1)S(1)} %add_first.1._.refs_0_), channel_id=1, source_target_pairs={{0,3},{1,2},{2,1},{3,0},{4,28},{5,29},{6,30},{7,31},{8,11},{9,10},... | collective-permute-start | bytes 294920 | tf_op jit(solution)/shard_map/ppermute | solution.py:343
  29.4 1.0 %collective-permute-start.9 = (bf16[3,64,256]{2,1,0:T(8,128)(2,1)S(1)}, bf16[3,64,256]{2,1,0:T(8,128)(2,1)S(1)}, u32[]{:S(2)}, u32[]{:S(2)}) collective-permute-start(bf16[3,64,256]{2,1,0:T(8,128)(2,1)S(1)} %add_first.1._.refs_0_), channel_id=1, source_target_pairs={{0,2},{1,3},{2,0},{3,1},{4,20},{5,21},{6,22},{7,23},{8,10},{9,11},... | collective-permute-start | bytes 294920 | tf_op jit(solution)/shard_map/ppermute | solution.py:343
  30.4 1.0 %collective-permute-start.8 = (bf16[3,64,256]{2,1,0:T(8,128)(2,1)S(1)}, bf16[3,64,256]{2,1,0:T(8,128)(2,1)S(1)}, u32[]{:S(2)}, u32[]{:S(2)}) collective-permute-start(bf16[3,64,256]{2,1,0:T(8,128)(2,1)S(1)} %add_first.1._.refs_0_), channel_id=1, source_target_pairs={{0,1},{1,0},{2,3},{3,2},{4,12},{5,13},{6,14},{7,15},{8,9},{9,8},{1... | collective-permute-start | bytes 294920 | tf_op jit(solution)/shard_map/ppermute | solution.py:343
  31.4 1.1 %inputs.1 = (bf16[2,256,256]{2,1,0:T(8,128)(2,1)}, f32[8,128]{1,0:T(8,128)S(1)}) custom-call(bf16[2,2,256,256]{3,2,1,0:T(8,128)(2,1)S(1)} %get-tuple-element.46.act_ref, bf16[2,256,256]{2,1,0:T(8,128)(2,1)S(1)} %bitcast.5, bf16[2,256,256]{2,1,0:T(8,128)(2,1)S(1)} %copy-done.1, bf16[2,256,256]{2,1,0:T(8,128)(2,1)S(1)} %copy-done.2, ...), custom_call_target="tpu_custom_call" | custom-call | flops 268435456 | bytes 2097152 | tf_op jit(solution)/shard_map/inputs/pallas_call | solution.py:344
  32.5 1.0 %collective-permute-done.10.refs_3_ = bf16[3,64,256]{2,1,0:T(8,128)(2,1)S(1)} collective-permute-done((bf16[3,64,256]{2,1,0:T(8,128)(2,1)S(1)}, bf16[3,64,256]{2,1,0:T(8,128)(2,1)S(1)}, u32[]{:S(2)}, u32[]{:S(2)}) %collective-permute-start.10) | collective-permute-done | bytes 98336 | tf_op jit(solution)/shard_map/ppermute | solution.py:343
  33.5 2.6 %collective-permute-done.9.refs_2_ = bf16[3,64,256]{2,1,0:T(8,128)(2,1)S(1)} collective-permute-done((bf16[3,64,256]{2,1,0:T(8,128)(2,1)S(1)}, bf16[3,64,256]{2,1,0:T(8,128)(2,1)S(1)}, u32[]{:S(2)}, u32[]{:S(2)}) %collective-permute-start.9) | collective-permute-done | bytes 98336 | tf_op jit(solution)/shard_map/ppermute | solution.py:343
  36.1 2.4 %collective-permute-start.15 = (bf16[3,64,256]{2,1,0:T(8,128)(2,1)S(1)}, bf16[3,64,256]{2,1,0:T(8,128)(2,1)S(1)}, u32[]{:S(2)}, u32[]{:S(2)}) collective-permute-start(bf16[3,64,256]{2,1,0:T(8,128)(2,1)S(1)} %add_second.1.refs_0_), channel_id=1, source_target_pairs={{0,24},{1,25},{2,26},{3,27},{4,7},{5,6},{6,5},{7,4},{8,16},{9,17},... | collective-permute-start | bytes 294920 | tf_op jit(solution)/shard_map/ppermute | solution.py:351
  39.0 0.6 %collective-permute-start.17 = (bf16[3,64,256]{2,1,0:T(8,128)(2,1)S(1)}, bf16[3,64,256]{2,1,0:T(8,128)(2,1)S(1)}, u32[]{:S(2)}, u32[]{:S(2)}) collective-permute-start(bf16[3,64,256]{2,1,0:T(8,128)(2,1)S(1)} %add_second.1.refs_0_), channel_id=1, source_target_pairs={{0,8},{1,9},{2,10},{3,11},{4,5},{5,4},{6,7},{7,6},{8,0},{9,1},{10,... | collective-permute-start | bytes 294920 | tf_op jit(solution)/shard_map/ppermute | solution.py:351
  40.2 1.5 %collective-permute-done.15.refs_3_ = bf16[3,64,256]{2,1,0:T(8,128)(2,1)S(1)} collective-permute-done((bf16[3,64,256]{2,1,0:T(8,128)(2,1)S(1)}, bf16[3,64,256]{2,1,0:T(8,128)(2,1)S(1)}, u32[]{:S(2)}, u32[]{:S(2)}) %collective-permute-start.15) | collective-permute-done | bytes 98336 | tf_op jit(solution)/shard_map/ppermute | solution.py:351
  41.7 1.4 %collective-permute-done.13.refs_2_ = bf16[3,64,256]{2,1,0:T(8,128)(2,1)S(1)} collective-permute-done((bf16[3,64,256]{2,1,0:T(8,128)(2,1)S(1)}, bf16[3,64,256]{2,1,0:T(8,128)(2,1)S(1)}, u32[]{:S(2)}, u32[]{:S(2)}) %collective-permute-start.13) | collective-permute-done | bytes 98336 | tf_op jit(solution)/shard_map/ppermute | solution.py:351
  43.7 1.0 %scale_own.1 = (f32[2,256,256]{2,1,0:T(8,128)}, f32[2,256,256]{2,1,0:T(8,128)}, f32[2,256,256]{2,1,0:T(8,128)}) custom-call(bf16[3,64,256]{2,1,0:T(8,128)(2,1)S(1)} %add_second.1.refs_0_, bf16[3,64,256]{2,1,0:T(8,128)(2,1)S(1)} %collective-permute-done.17.refs_1_, bf16[3,64,256]{2,1,0:T(8,128)(2,1)S(1)} %collective-permute-done.13.refs_2_, ...), custom_call_target="tpu_custom_call" | custom-call | tf_op jit(solution)/shard_map/scale_own/pallas_call | solution.py:357
  44.7 1.0 %scale_other.1 = (f32[2,256,256]{2,1,0:T(8,128)}, f32[2,256,256]{2,1,0:T(8,128)}, f32[2,256,256]{2,1,0:T(8,128)}) custom-call(bf16[3,64,256]{2,1,0:T(8,128)(2,1)S(1)} %collective-permute-done.11.refs_0_, bf16[3,64,256]{2,1,0:T(8,128)(2,1)S(1)} %collective-permute-done.12.refs_1_, ...), custom_call_target="tpu_custom_call", output_to_operand_aliasing={{0}: (4, {}), {1}: (5, {}), {2}: (6, {})} | custom-call | tf_op jit(solution)/shard_map/scale_other/pallas_call | solution.py:358
  (28 shorter events, 3.3 us)
Async XLA Ops:
  2.0 12.1 %collective-permute-start = (bf16[2,128,256]{2,1,0:T(8,128)(2,1)S(1)}, bf16[2,128,256]{2,1,0:T(8,128)(2,1)S(1)}, u32[]{:S(2)}, u32[]{:S(2)}) collective-permute-start(bf16[2,128,256]{2,1,0:T(8,128)(2,1)S(1)} %get-tuple-element.43), channel_id=1, source_target_pairs={{0,2},{1,3},{2,0},{3,1},{4,6},{5,7},{6,4},{7,5},{8,10},{9,11},{10,... | collective-permute-start | bytes 393224 | tf_op jit(solution)/shard_map/ppermute | solution.py:294
  6.1 8.0 %collective-permute-start.1 = (bf16[2,128,256]{2,1,0:T(8,128)(2,1)S(1)}, bf16[2,128,256]{2,1,0:T(8,128)(2,1)S(1)}, u32[]{:S(2)}, u32[]{:S(2)}) collective-permute-start(bf16[2,128,256]{2,1,0:T(8,128)(2,1)S(1)} %get-tuple-element.44), channel_id=1, source_target_pairs={{0,1},{1,0},{2,3},{3,2},{4,5},{5,4},{6,7},{7,6},{8,9},{9,8},{10,11... | collective-permute-start | bytes 393224 | tf_op jit(solution)/shard_map/ppermute | solution.py:294
  7.7 8.8 %collective-permute-start.2 = (bf16[2,128,256]{2,1,0:T(8,128)(2,1)S(1)}, bf16[2,128,256]{2,1,0:T(8,128)(2,1)S(1)}, u32[]{:S(2)}, u32[]{:S(2)}) collective-permute-start(bf16[2,128,256]{2,1,0:T(8,128)(2,1)S(1)} %get-tuple-element.45), channel_id=1, source_target_pairs={{0,3},{1,2},{2,1},{3,0},{4,7},{5,6},{6,5},{7,4},{8,11},{9,10},{10,... | collective-permute-start | bytes 393224 | tf_op jit(solution)/shard_map/ppermute | solution.py:294
  17.1 2.0 %collective-permute-start.3 = (bf16[3,3,64,256]{3,2,1,0:T(8,128)(2,1)S(1)}, bf16[3,3,64,256]{3,2,1,0:T(8,128)(2,1)S(1)}, u32[]{:S(2)}, u32[]{:S(2)}) collective-permute-start(bf16[3,3,64,256]{3,2,1,0:T(8,128)(2,1)S(1)} %get-tuple-element.49), channel_id=1, source_target_pairs={{0,4},{4,0},{8,12},{12,8},{16,20},{20,16},{24,28},{28,24},{1,5},{5... | collective-permute-start | bytes 884744 | tf_op jit(solution)/shard_map/ppermute | solution.py:319
  17.5 6.1 %collective-permute-start.4 = (bf16[3,64,256]{2,1,0:T(8,128)(2,1)S(1)}, bf16[3,64,256]{2,1,0:T(8,128)(2,1)S(1)}, u32[]{:S(2)}, u32[]{:S(2)}) collective-permute-start(bf16[3,64,256]{2,1,0:T(8,128)(2,1)S(1)} %get-tuple-element.52), channel_id=1, source_target_pairs={{0,8},{1,9},{2,10},{3,11},{4,5},{5,4},{6,7},{7,6},{8,0},{9,1},{10,... | collective-permute-start | bytes 294920 | tf_op jit(solution)/shard_map/ppermute | solution.py:336
  19.1 12.3 %copy-start.2 = (bf16[2,256,256]{2,1,0:T(8,128)(2,1)S(1)}, bf16[2,256,256]{2,1,0:T(8,128)(2,1)}, u32[]{:S(2)}) copy-start(bf16[2,256,256]{2,1,0:T(8,128)(2,1)} %wg_ref.1) | copy-start | bytes 786436
  19.2 5.6 %collective-permute-start.5 = (bf16[3,64,256]{2,1,0:T(8,128)(2,1)S(1)}, bf16[3,64,256]{2,1,0:T(8,128)(2,1)S(1)}, u32[]{:S(2)}, u32[]{:S(2)}) collective-permute-start(bf16[3,64,256]{2,1,0:T(8,128)(2,1)S(1)} %get-tuple-element.53), channel_id=1, source_target_pairs={{0,24},{1,25},{2,26},{3,27},{4,7},{5,6},{6,5},{7,4},{8,16},{9,17},... | collective-permute-start | bytes 294920 | tf_op jit(solution)/shard_map/ppermute | solution.py:340
  21.3 4.6 %collective-permute-start.6 = (bf16[3,64,256]{2,1,0:T(8,128)(2,1)S(1)}, bf16[3,64,256]{2,1,0:T(8,128)(2,1)S(1)}, u32[]{:S(2)}, u32[]{:S(2)}) collective-permute-start(bf16[3,64,256]{2,1,0:T(8,128)(2,1)S(1)} %get-tuple-element.54), channel_id=1, source_target_pairs={{0,16},{1,17},{2,18},{3,19},{4,6},{5,7},{6,4},{7,5},{8,24},{9,25},... | collective-permute-start | bytes 294920 | tf_op jit(solution)/shard_map/ppermute | solution.py:340
  21.8 5.0 %collective-permute-start.7 = (bf16[3,64,256]{2,1,0:T(8,128)(2,1)S(1)}, bf16[3,64,256]{2,1,0:T(8,128)(2,1)S(1)}, u32[]{:S(2)}, u32[]{:S(2)}) collective-permute-start(bf16[3,64,256]{2,1,0:T(8,128)(2,1)S(1)} %get-tuple-element.55), channel_id=1, source_target_pairs={{0,5},{1,4},{2,7},{3,6},{4,8},{5,9},{6,10},{7,11},{8,13},{9,12},{1... | collective-permute-start | bytes 294920 | tf_op jit(solution)/shard_map/ppermute | solution.py:341
  26.9 4.5 %copy-start = (bf16[1,2,256,256]{3,2,1,0:T(8,128)(2,1)S(1)}, bf16[1,2,256,256]{3,2,1,0:T(8,128)(2,1)}, u32[]{:S(2)}) copy-start(bf16[1,2,256,256]{3,2,1,0:T(8,128)(2,1)} %param.8) | copy-start | bytes 786436
  26.9 4.5 %copy-start.1 = (bf16[2,256,256]{2,1,0:T(8,128)(2,1)S(1)}, bf16[2,256,256]{2,1,0:T(8,128)(2,1)}, u32[]{:S(2)}) copy-start(bf16[2,256,256]{2,1,0:T(8,128)(2,1)} %wf_ref.1) | copy-start | bytes 786436
  26.9 6.6 %collective-permute-start.10 = (bf16[3,64,256]{2,1,0:T(8,128)(2,1)S(1)}, bf16[3,64,256]{2,1,0:T(8,128)(2,1)S(1)}, u32[]{:S(2)}, u32[]{:S(2)}) collective-permute-start(bf16[3,64,256]{2,1,0:T(8,128)(2,1)S(1)} %add_first.1._.refs_0_), channel_id=1, source_target_pairs={{0,3},{1,2},{2,1},{3,0},{4,28},{5,29},{6,30},{7,31},{8,11},{9,10},... | collective-permute-start | bytes 294920 | tf_op jit(solution)/shard_map/ppermute | solution.py:343
  29.4 6.7 %collective-permute-start.9 = (bf16[3,64,256]{2,1,0:T(8,128)(2,1)S(1)}, bf16[3,64,256]{2,1,0:T(8,128)(2,1)S(1)}, u32[]{:S(2)}, u32[]{:S(2)}) collective-permute-start(bf16[3,64,256]{2,1,0:T(8,128)(2,1)S(1)} %add_first.1._.refs_0_), channel_id=1, source_target_pairs={{0,2},{1,3},{2,0},{3,1},{4,20},{5,21},{6,22},{7,23},{8,10},{9,11},... | collective-permute-start | bytes 294920 | tf_op jit(solution)/shard_map/ppermute | solution.py:343
  30.4 5.7 %collective-permute-start.8 = (bf16[3,64,256]{2,1,0:T(8,128)(2,1)S(1)}, bf16[3,64,256]{2,1,0:T(8,128)(2,1)S(1)}, u32[]{:S(2)}, u32[]{:S(2)}) collective-permute-start(bf16[3,64,256]{2,1,0:T(8,128)(2,1)S(1)} %add_first.1._.refs_0_), channel_id=1, source_target_pairs={{0,1},{1,0},{2,3},{3,2},{4,12},{5,13},{6,14},{7,15},{8,9},{9,8},{1... | collective-permute-start | bytes 294920 | tf_op jit(solution)/shard_map/ppermute | solution.py:343
  36.1 5.6 %collective-permute-start.15 = (bf16[3,64,256]{2,1,0:T(8,128)(2,1)S(1)}, bf16[3,64,256]{2,1,0:T(8,128)(2,1)S(1)}, u32[]{:S(2)}, u32[]{:S(2)}) collective-permute-start(bf16[3,64,256]{2,1,0:T(8,128)(2,1)S(1)} %add_second.1.refs_0_), channel_id=1, source_target_pairs={{0,24},{1,25},{2,26},{3,27},{4,7},{5,6},{6,5},{7,4},{8,16},{9,17},... | collective-permute-start | bytes 294920 | tf_op jit(solution)/shard_map/ppermute | solution.py:351
  38.5 4.6 %collective-permute-start.13 = (bf16[3,64,256]{2,1,0:T(8,128)(2,1)S(1)}, bf16[3,64,256]{2,1,0:T(8,128)(2,1)S(1)}, u32[]{:S(2)}, u32[]{:S(2)}) collective-permute-start(bf16[3,64,256]{2,1,0:T(8,128)(2,1)S(1)} %add_second.1.refs_0_), channel_id=1, source_target_pairs={{0,16},{1,17},{2,18},{3,19},{4,6},{5,7},{6,4},{7,5},{8,24},{9,25},... | collective-permute-start | bytes 294920 | tf_op jit(solution)/shard_map/ppermute | solution.py:351
  39.0 4.6 %collective-permute-start.17 = (bf16[3,64,256]{2,1,0:T(8,128)(2,1)S(1)}, bf16[3,64,256]{2,1,0:T(8,128)(2,1)S(1)}, u32[]{:S(2)}, u32[]{:S(2)}) collective-permute-start(bf16[3,64,256]{2,1,0:T(8,128)(2,1)S(1)} %add_second.1.refs_0_), channel_id=1, source_target_pairs={{0,8},{1,9},{2,10},{3,11},{4,5},{5,4},{6,7},{7,6},{8,0},{9,1},{10,... | collective-permute-start | bytes 294920 | tf_op jit(solution)/shard_map/ppermute | solution.py:351
  39.7 5.0 %collective-permute-start.12 = (bf16[3,64,256]{2,1,0:T(8,128)(2,1)S(1)}, bf16[3,64,256]{2,1,0:T(8,128)(2,1)S(1)}, u32[]{:S(2)}, u32[]{:S(2)}) collective-permute-start(bf16[3,64,256]{2,1,0:T(8,128)(2,1)S(1)} %add_second.1.refs_0_), channel_id=1, source_target_pairs={{0,12},{1,13},{2,14},{3,15},{4,1},{5,0},{6,3},{7,2},{8,4},{9,5},{1... | collective-permute-start | bytes 294920 | tf_op jit(solution)/shard_map/ppermute | solution.py:352
  39.7 5.0 %collective-permute-start.11 = (bf16[3,64,256]{2,1,0:T(8,128)(2,1)S(1)}, bf16[3,64,256]{2,1,0:T(8,128)(2,1)S(1)}, u32[]{:S(2)}, u32[]{:S(2)}) collective-permute-start(bf16[3,64,256]{2,1,0:T(8,128)(2,1)S(1)} %add_second.1.refs_0_), channel_id=1, source_target_pairs={{0,4},{4,0},{8,12},{12,8},{16,20},{20,16},{24,28},{28,24},{1,5},{5... | collective-permute-start | bytes 294920 | tf_op jit(solution)/shard_map/ppermute | solution.py:353
  41.7 3.0 %collective-permute-start.16 = (bf16[3,64,256]{2,1,0:T(8,128)(2,1)S(1)}, bf16[3,64,256]{2,1,0:T(8,128)(2,1)S(1)}, u32[]{:S(2)}, u32[]{:S(2)}) collective-permute-start(bf16[3,64,256]{2,1,0:T(8,128)(2,1)S(1)} %collective-permute-done.15.refs_3_), channel_id=1, source_target_pairs={{0,4},{4,0},{8,12},{12,8},{16,20},{20,16},{24,28},{28,24},{1,5},{5... | collective-permute-start | bytes 294920 | tf_op jit(solution)/shard_map/ppermute | solution.py:353
  43.2 1.5 %collective-permute-start.14 = (bf16[3,64,256]{2,1,0:T(8,128)(2,1)S(1)}, bf16[3,64,256]{2,1,0:T(8,128)(2,1)S(1)}, u32[]{:S(2)}, u32[]{:S(2)}) collective-permute-start(bf16[3,64,256]{2,1,0:T(8,128)(2,1)S(1)} %collective-permute-done.13.refs_2_), channel_id=1, source_target_pairs={{0,4},{4,0},{8,12},{12,8},{16,20},{20,16},{24,28},{28,24},{1,5},{5... | collective-permute-start | bytes 294920 | tf_op jit(solution)/shard_map/ppermute | solution.py:353

commit v8 on v7

--- a/solution.py
+++ b/solution.py
@@ -340,7 +340,7 @@
     gots += [lax.ppermute(part, BOTH, pairs(p, True)) for p, part in list(enumerate(sends, 2))[::-1]]
     gots += [lax.ppermute(cross, BOTH, crossed(1, False))]
     (mine,) = call(sum_body, [shape(chunk, BF16)], [VM] * (ways + 1), "add_first")(own, *gots)
-    gots = [lax.ppermute(mine, BOTH, pairs(p, False)) for p in range(1, ways)]
+    gots = [lax.ppermute(mine, BOTH, pairs(p, False)) for p in range(1, ways)[::-1]][::-1]
     grad_inputs, token = call(
         functools.partial(inputs_body, steps), [shape(x.shape, BF16), shape((8, 128), F32)], [VM] * 4 + [AN], "inputs",
         flops=8 * block * chans, nbytes=16 * block,
@@ -348,7 +348,8 @@
     (done,) = call(
         functools.partial(add_body, ways), [shape(chunk, BF16)], [VM] * ways + [AN], "add_second"
     )(mine, *gots, token)
-    chunks = [done] + [lax.ppermute(done, BOTH, pairs(p, True)) for p in range(1, ways)]
+    near = {p: lax.ppermute(done, BOTH, pairs(p, True)) for p in [*range(2, ways), 1][::-1]}
+    chunks = [done] + [near[p] for p in range(1, ways)]
     direct = lax.ppermute(done, BOTH, crossed(1, True))
     others = [direct if i == 1 else lax.ppermute(part, "dp", swap) for i, part in enumerate(chunks)]
     factor = 1.0 / math.sqrt(windows * dp * steps * sites * regions)

time: 45.9 us -> 45.9 us (level)
  no operation moved by 1% of the time
where the time goes in v8:
time: 45.9 us; the launch traced here: 45.7 us
  starting transfers between devices  20.4 us (44%)
  waiting for transfers between devices  14.8 us (32%)
  Pallas kernels  9.73 us (21%)
  between operations  0.74 us (2%)
    ppermute x3, starting transfers between devices, per_device(): lax.ppermute(part, 'region', [(r, r ^ p) for r in range(regions)])  5.68 us
    ppermute x3, waiting for transfers between devices, per_device(): lax.ppermute(part, 'region', [(r, r ^ p) for r in range(regions)])  4.63 us
    ppermute x3, starting transfers between devices, per_device(): lax.ppermute(mine, BOTH, pairs(p, False))  4.45 us
    pallas_call x1, Pallas kernels, per_device(): call(functools.partial(local_body, steps, order), [shape(x.shape, F32)] *...  4.11 us
    ppermute x3, waiting for transfers between devices, per_device(): lax.ppermute(mine, BOTH, pairs(p, False))  3.59 us
    ppermute x3, starting transfers between devices, per_device(): lax.ppermute(done, BOTH, pairs(p, True))  3.55 us
    ppermute x3, waiting for transfers between devices, per_device(): lax.ppermute(done, BOTH, pairs(p, True))  3.42 us
    ppermute x2, starting transfers between devices, per_device(): lax.ppermute(part, BOTH, pairs(p, True))  2.67 us
  transfers between devices with their start and end apart: 18, of which 10 were waited for; matrix products, arithmetic and copies ran while one was open for 0% of the time, Pallas kernels for 14%

profile of v8, /device:TPU:0, one launch (start us, length us, event | category | flops | bytes accessed | tf_op | source)
XLA Modules:
  0.0 45.7 jit_solution(8821675579139078801)
XLA Ops:
  0.6 1.4 %outgoing.1 = (bf16[2,128,256]{2,1,0:T(8,128)(2,1)S(1)}, bf16[2,128,256]{2,1,0:T(8,128)(2,1)S(1)}, bf16[2,128,256]{2,1,0:T(8,128)(2,1)S(1)}) custom-call(s32[8,6]{1,0:T(8,128)} %nb_hbm.3, bf16[2,256,256]{2,1,0:T(8,128)(2,1)} %bitcast.3, bf16[2,6,128,128]{3,2,1,0:T(8,128)(2,1)} %adj_hbm.3), custom_call_target="tpu_custom_call" | custom-call | flops 50331648 | bytes 524288 | tf_op jit(solution)/shard_map/outgoing/pallas_call | solution.py:284
  2.0 4.1 %collective-permute-start = (bf16[2,128,256]{2,1,0:T(8,128)(2,1)S(1)}, bf16[2,128,256]{2,1,0:T(8,128)(2,1)S(1)}, u32[]{:S(2)}, u32[]{:S(2)}) collective-permute-start(bf16[2,128,256]{2,1,0:T(8,128)(2,1)S(1)} %get-tuple-element.43), channel_id=1, source_target_pairs={{0,2},{1,3},{2,0},{3,1},{4,6},{5,7},{6,4},{7,5},{8,10},{9,11},{10,... | collective-permute-start | bytes 393224 | tf_op jit(solution)/shard_map/ppermute | solution.py:294
  6.1 1.6 %collective-permute-start.1 = (bf16[2,128,256]{2,1,0:T(8,128)(2,1)S(1)}, bf16[2,128,256]{2,1,0:T(8,128)(2,1)S(1)}, u32[]{:S(2)}, u32[]{:S(2)}) collective-permute-start(bf16[2,128,256]{2,1,0:T(8,128)(2,1)S(1)} %get-tuple-element.44), channel_id=1, source_target_pairs={{0,1},{1,0},{2,3},{3,2},{4,5},{5,4},{6,7},{7,6},{8,9},{9,8},{10,11... | collective-permute-start | bytes 393224 | tf_op jit(solution)/shard_map/ppermute | solution.py:294
  7.7 4.1 %local.1 = (f32[2,256,256]{2,1,0:T(8,128)S(1)}, f32[2,256,256]{2,1,0:T(8,128)S(1)}, f32[2,256,256]{2,1,0:T(8,128)S(1)}, f32[2,256,256]{2,1,0:T(8,128)S(1)}, f32[...) custom-call(s32[8,6]{1,0:T(8,128)} %nb_hbm.3, ...), custom_call_target="tpu_custom_call" | custom-call | flops 469762048 | bytes 3932160 | tf_op jit(solution)/shard_map/local/pallas_call | solution.py:298
  11.8 2.3 %collective-permute-done.refs_0_ = bf16[2,128,256]{2,1,0:T(8,128)(2,1)S(1)} collective-permute-done((bf16[2,128,256]{2,1,0:T(8,128)(2,1)S(1)}, bf16[2,128,256]{2,1,0:T(8,128)(2,1)S(1)}, u32[]{:S(2)}, u32[]{:S(2)}) %collective-permute-start) | collective-permute-done | bytes 131104 | tf_op jit(solution)/shard_map/ppermute | solution.py:294
  14.1 2.4 %collective-permute-done.2.refs_2_ = bf16[2,128,256]{2,1,0:T(8,128)(2,1)S(1)} collective-permute-done((bf16[2,128,256]{2,1,0:T(8,128)(2,1)S(1)}, bf16[2,128,256]{2,1,0:T(8,128)(2,1)S(1)}, u32[]{:S(2)}, u32[]{:S(2)}) %collective-permute-start.2) | collective-permute-done | bytes 131104 | tf_op jit(solution)/shard_map/ppermute | solution.py:294
  17.5 1.6 %collective-permute-start.4 = (bf16[3,64,256]{2,1,0:T(8,128)(2,1)S(1)}, bf16[3,64,256]{2,1,0:T(8,128)(2,1)S(1)}, u32[]{:S(2)}, u32[]{:S(2)}) collective-permute-start(bf16[3,64,256]{2,1,0:T(8,128)(2,1)S(1)} %get-tuple-element.52), channel_id=1, source_target_pairs={{0,8},{1,9},{2,10},{3,11},{4,5},{5,4},{6,7},{7,6},{8,0},{9,1},{10,... | collective-permute-start | bytes 294920 | tf_op jit(solution)/shard_map/ppermute | solution.py:336
  19.2 2.2 %collective-permute-start.5 = (bf16[3,64,256]{2,1,0:T(8,128)(2,1)S(1)}, bf16[3,64,256]{2,1,0:T(8,128)(2,1)S(1)}, u32[]{:S(2)}, u32[]{:S(2)}) collective-permute-start(bf16[3,64,256]{2,1,0:T(8,128)(2,1)S(1)} %get-tuple-element.53), channel_id=1, source_target_pairs={{0,24},{1,25},{2,26},{3,27},{4,7},{5,6},{6,5},{7,4},{8,16},{9,17},... | collective-permute-start | bytes 294920 | tf_op jit(solution)/shard_map/ppermute | solution.py:340
  21.8 1.8 %collective-permute-start.7 = (bf16[3,64,256]{2,1,0:T(8,128)(2,1)S(1)}, bf16[3,64,256]{2,1,0:T(8,128)(2,1)S(1)}, u32[]{:S(2)}, u32[]{:S(2)}) collective-permute-start(bf16[3,64,256]{2,1,0:T(8,128)(2,1)S(1)} %get-tuple-element.55), channel_id=1, source_target_pairs={{0,5},{1,4},{2,7},{3,6},{4,8},{5,9},{6,10},{7,11},{8,13},{9,12},{1... | collective-permute-start | bytes 294920 | tf_op jit(solution)/shard_map/ppermute | solution.py:341
  23.7 1.1 %collective-permute-done.5.refs_2_ = bf16[3,64,256]{2,1,0:T(8,128)(2,1)S(1)} collective-permute-done((bf16[3,64,256]{2,1,0:T(8,128)(2,1)S(1)}, bf16[3,64,256]{2,1,0:T(8,128)(2,1)S(1)}, u32[]{:S(2)}, u32[]{:S(2)}) %collective-permute-start.5) | collective-permute-done | bytes 98336 | tf_op jit(solution)/shard_map/ppermute | solution.py:340
  24.7 1.2 %collective-permute-done.6.refs_3_ = bf16[3,64,256]{2,1,0:T(8,128)(2,1)S(1)} collective-permute-done((bf16[3,64,256]{2,1,0:T(8,128)(2,1)S(1)}, bf16[3,64,256]{2,1,0:T(8,128)(2,1)S(1)}, u32[]{:S(2)}, u32[]{:S(2)}) %collective-permute-start.6) | collective-permute-done | bytes 98336 | tf_op jit(solution)/shard_map/ppermute | solution.py:340
  26.0 0.9 %collective-permute-done.7.refs_4_ = bf16[3,64,256]{2,1,0:T(8,128)(2,1)S(1)} collective-permute-done((bf16[3,64,256]{2,1,0:T(8,128)(2,1)S(1)}, bf16[3,64,256]{2,1,0:T(8,128)(2,1)S(1)}, u32[]{:S(2)}, u32[]{:S(2)}) %collective-permute-start.7) | collective-permute-done | bytes 98336 | tf_op jit(solution)/shard_map/ppermute | solution.py:341
  26.9 2.5 %collective-permute-start.10 = (bf16[3,64,256]{2,1,0:T(8,128)(2,1)S(1)}, bf16[3,64,256]{2,1,0:T(8,128)(2,1)S(1)}, u32[]{:S(2)}, u32[]{:S(2)}) collective-permute-start(bf16[3,64,256]{2,1,0:T(8,128)(2,1)S(1)} %add_first.1._.refs_0_), channel_id=1, source_target_pairs={{0,3},{1,2},{2,1},{3,0},{4,28},{5,29},{6,30},{7,31},{8,11},{9,10},... | collective-permute-start | bytes 294920 | tf_op jit(solution)/shard_map/ppermute | solution.py:343
  29.4 1.0 %collective-permute-start.9 = (bf16[3,64,256]{2,1,0:T(8,128)(2,1)S(1)}, bf16[3,64,256]{2,1,0:T(8,128)(2,1)S(1)}, u32[]{:S(2)}, u32[]{:S(2)}) collective-permute-start(bf16[3,64,256]{2,1,0:T(8,128)(2,1)S(1)} %add_first.1._.refs_0_), channel_id=1, source_target_pairs={{0,2},{1,3},{2,0},{3,1},{4,20},{5,21},{6,22},{7,23},{8,10},{9,11},... | collective-permute-start | bytes 294920 | tf_op jit(solution)/shard_map/ppermute | solution.py:343
  30.4 1.0 %collective-permute-start.8 = (bf16[3,64,256]{2,1,0:T(8,128)(2,1)S(1)}, bf16[3,64,256]{2,1,0:T(8,128)(2,1)S(1)}, u32[]{:S(2)}, u32[]{:S(2)}) collective-permute-start(bf16[3,64,256]{2,1,0:T(8,128)(2,1)S(1)} %add_first.1._.refs_0_), channel_id=1, source_target_pairs={{0,1},{1,0},{2,3},{3,2},{4,12},{5,13},{6,14},{7,15},{8,9},{9,8},{1... | collective-permute-start | bytes 294920 | tf_op jit(solution)/shard_map/ppermute | solution.py:343
  31.4 1.1 %inputs.1 = (bf16[2,256,256]{2,1,0:T(8,128)(2,1)}, f32[8,128]{1,0:T(8,128)S(1)}) custom-call(bf16[2,2,256,256]{3,2,1,0:T(8,128)(2,1)S(1)} %get-tuple-element.46.act_ref, bf16[2,256,256]{2,1,0:T(8,128)(2,1)S(1)} %bitcast.5, bf16[2,256,256]{2,1,0:T(8,128)(2,1)S(1)} %copy-done.1, bf16[2,256,256]{2,1,0:T(8,128)(2,1)S(1)} %copy-done.2, ...), custom_call_target="tpu_custom_call" | custom-call | flops 268435456 | bytes 2097152 | tf_op jit(solution)/shard_map/inputs/pallas_call | solution.py:344
  32.5 1.0 %collective-permute-done.10.refs_3_ = bf16[3,64,256]{2,1,0:T(8,128)(2,1)S(1)} collective-permute-done((bf16[3,64,256]{2,1,0:T(8,128)(2,1)S(1)}, bf16[3,64,256]{2,1,0:T(8,128)(2,1)S(1)}, u32[]{:S(2)}, u32[]{:S(2)}) %collective-permute-start.10) | collective-permute-done | bytes 98336 | tf_op jit(solution)/shard_map/ppermute | solution.py:343
  33.5 2.6 %collective-permute-done.9.refs_2_ = bf16[3,64,256]{2,1,0:T(8,128)(2,1)S(1)} collective-permute-done((bf16[3,64,256]{2,1,0:T(8,128)(2,1)S(1)}, bf16[3,64,256]{2,1,0:T(8,128)(2,1)S(1)}, u32[]{:S(2)}, u32[]{:S(2)}) %collective-permute-start.9) | collective-permute-done | bytes 98336 | tf_op jit(solution)/shard_map/ppermute | solution.py:343
  36.1 2.4 %collective-permute-start.15 = (bf16[3,64,256]{2,1,0:T(8,128)(2,1)S(1)}, bf16[3,64,256]{2,1,0:T(8,128)(2,1)S(1)}, u32[]{:S(2)}, u32[]{:S(2)}) collective-permute-start(bf16[3,64,256]{2,1,0:T(8,128)(2,1)S(1)} %add_second.1.refs_0_), channel_id=1, source_target_pairs={{0,24},{1,25},{2,26},{3,27},{4,7},{5,6},{6,5},{7,4},{8,16},{9,17},... | collective-permute-start | bytes 294920 | tf_op jit(solution)/shard_map/ppermute | solution.py:351
  39.0 0.6 %collective-permute-start.17 = (bf16[3,64,256]{2,1,0:T(8,128)(2,1)S(1)}, bf16[3,64,256]{2,1,0:T(8,128)(2,1)S(1)}, u32[]{:S(2)}, u32[]{:S(2)}) collective-permute-start(bf16[3,64,256]{2,1,0:T(8,128)(2,1)S(1)} %add_second.1.refs_0_), channel_id=1, source_target_pairs={{0,8},{1,9},{2,10},{3,11},{4,5},{5,4},{6,7},{7,6},{8,0},{9,1},{10,... | collective-permute-start | bytes 294920 | tf_op jit(solution)/shard_map/ppermute | solution.py:351
  40.2 1.5 %collective-permute-done.15.refs_3_ = bf16[3,64,256]{2,1,0:T(8,128)(2,1)S(1)} collective-permute-done((bf16[3,64,256]{2,1,0:T(8,128)(2,1)S(1)}, bf16[3,64,256]{2,1,0:T(8,128)(2,1)S(1)}, u32[]{:S(2)}, u32[]{:S(2)}) %collective-permute-start.15) | collective-permute-done | bytes 98336 | tf_op jit(solution)/shard_map/ppermute | solution.py:351
  41.7 1.4 %collective-permute-done.13.refs_2_ = bf16[3,64,256]{2,1,0:T(8,128)(2,1)S(1)} collective-permute-done((bf16[3,64,256]{2,1,0:T(8,128)(2,1)S(1)}, bf16[3,64,256]{2,1,0:T(8,128)(2,1)S(1)}, u32[]{:S(2)}, u32[]{:S(2)}) %collective-permute-start.13) | collective-permute-done | bytes 98336 | tf_op jit(solution)/shard_map/ppermute | solution.py:351
  43.7 1.0 %scale_own.1 = (f32[2,256,256]{2,1,0:T(8,128)}, f32[2,256,256]{2,1,0:T(8,128)}, f32[2,256,256]{2,1,0:T(8,128)}) custom-call(bf16[3,64,256]{2,1,0:T(8,128)(2,1)S(1)} %add_second.1.refs_0_, bf16[3,64,256]{2,1,0:T(8,128)(2,1)S(1)} %collective-permute-done.17.refs_1_, bf16[3,64,256]{2,1,0:T(8,128)(2,1)S(1)} %collective-permute-done.13.refs_2_, ...), custom_call_target="tpu_custom_call" | custom-call | tf_op jit(solution)/shard_map/scale_own/pallas_call | solution.py:358
  44.7 1.0 %scale_other.1 = (f32[2,256,256]{2,1,0:T(8,128)}, f32[2,256,256]{2,1,0:T(8,128)}, f32[2,256,256]{2,1,0:T(8,128)}) custom-call(bf16[3,64,256]{2,1,0:T(8,128)(2,1)S(1)} %collective-permute-done.11.refs_0_, bf16[3,64,256]{2,1,0:T(8,128)(2,1)S(1)} %collective-permute-done.12.refs_1_, ...), custom_call_target="tpu_custom_call", output_to_operand_aliasing={{0}: (4, {}), {1}: (5, {}), {2}: (6, {})} | custom-call | tf_op jit(solution)/shard_map/scale_other/pallas_call | solution.py:359
  (28 shorter events, 3.3 us)
Async XLA Ops:
  2.0 12.1 %collective-permute-start = (bf16[2,128,256]{2,1,0:T(8,128)(2,1)S(1)}, bf16[2,128,256]{2,1,0:T(8,128)(2,1)S(1)}, u32[]{:S(2)}, u32[]{:S(2)}) collective-permute-start(bf16[2,128,256]{2,1,0:T(8,128)(2,1)S(1)} %get-tuple-element.43), channel_id=1, source_target_pairs={{0,2},{1,3},{2,0},{3,1},{4,6},{5,7},{6,4},{7,5},{8,10},{9,11},{10,... | collective-permute-start | bytes 393224 | tf_op jit(solution)/shard_map/ppermute | solution.py:294
  6.1 8.0 %collective-permute-start.1 = (bf16[2,128,256]{2,1,0:T(8,128)(2,1)S(1)}, bf16[2,128,256]{2,1,0:T(8,128)(2,1)S(1)}, u32[]{:S(2)}, u32[]{:S(2)}) collective-permute-start(bf16[2,128,256]{2,1,0:T(8,128)(2,1)S(1)} %get-tuple-element.44), channel_id=1, source_target_pairs={{0,1},{1,0},{2,3},{3,2},{4,5},{5,4},{6,7},{7,6},{8,9},{9,8},{10,11... | collective-permute-start | bytes 393224 | tf_op jit(solution)/shard_map/ppermute | solution.py:294
  7.7 8.8 %collective-permute-start.2 = (bf16[2,128,256]{2,1,0:T(8,128)(2,1)S(1)}, bf16[2,128,256]{2,1,0:T(8,128)(2,1)S(1)}, u32[]{:S(2)}, u32[]{:S(2)}) collective-permute-start(bf16[2,128,256]{2,1,0:T(8,128)(2,1)S(1)} %get-tuple-element.45), channel_id=1, source_target_pairs={{0,3},{1,2},{2,1},{3,0},{4,7},{5,6},{6,5},{7,4},{8,11},{9,10},{10,... | collective-permute-start | bytes 393224 | tf_op jit(solution)/shard_map/ppermute | solution.py:294
  17.1 2.0 %collective-permute-start.3 = (bf16[3,3,64,256]{3,2,1,0:T(8,128)(2,1)S(1)}, bf16[3,3,64,256]{3,2,1,0:T(8,128)(2,1)S(1)}, u32[]{:S(2)}, u32[]{:S(2)}) collective-permute-start(bf16[3,3,64,256]{3,2,1,0:T(8,128)(2,1)S(1)} %get-tuple-element.49), channel_id=1, source_target_pairs={{0,4},{4,0},{8,12},{12,8},{16,20},{20,16},{24,28},{28,24},{1,5},{5... | collective-permute-start | bytes 884744 | tf_op jit(solution)/shard_map/ppermute | solution.py:319
  17.5 6.1 %collective-permute-start.4 = (bf16[3,64,256]{2,1,0:T(8,128)(2,1)S(1)}, bf16[3,64,256]{2,1,0:T(8,128)(2,1)S(1)}, u32[]{:S(2)}, u32[]{:S(2)}) collective-permute-start(bf16[3,64,256]{2,1,0:T(8,128)(2,1)S(1)} %get-tuple-element.52), channel_id=1, source_target_pairs={{0,8},{1,9},{2,10},{3,11},{4,5},{5,4},{6,7},{7,6},{8,0},{9,1},{10,... | collective-permute-start | bytes 294920 | tf_op jit(solution)/shard_map/ppermute | solution.py:336
  19.1 12.3 %copy-start.2 = (bf16[2,256,256]{2,1,0:T(8,128)(2,1)S(1)}, bf16[2,256,256]{2,1,0:T(8,128)(2,1)}, u32[]{:S(2)}) copy-start(bf16[2,256,256]{2,1,0:T(8,128)(2,1)} %wg_ref.1) | copy-start | bytes 786436
  19.2 5.6 %collective-permute-start.5 = (bf16[3,64,256]{2,1,0:T(8,128)(2,1)S(1)}, bf16[3,64,256]{2,1,0:T(8,128)(2,1)S(1)}, u32[]{:S(2)}, u32[]{:S(2)}) collective-permute-start(bf16[3,64,256]{2,1,0:T(8,128)(2,1)S(1)} %get-tuple-element.53), channel_id=1, source_target_pairs={{0,24},{1,25},{2,26},{3,27},{4,7},{5,6},{6,5},{7,4},{8,16},{9,17},... | collective-permute-start | bytes 294920 | tf_op jit(solution)/shard_map/ppermute | solution.py:340
  21.3 4.6 %collective-permute-start.6 = (bf16[3,64,256]{2,1,0:T(8,128)(2,1)S(1)}, bf16[3,64,256]{2,1,0:T(8,128)(2,1)S(1)}, u32[]{:S(2)}, u32[]{:S(2)}) collective-permute-start(bf16[3,64,256]{2,1,0:T(8,128)(2,1)S(1)} %get-tuple-element.54), channel_id=1, source_target_pairs={{0,16},{1,17},{2,18},{3,19},{4,6},{5,7},{6,4},{7,5},{8,24},{9,25},... | collective-permute-start | bytes 294920 | tf_op jit(solution)/shard_map/ppermute | solution.py:340
  21.8 5.0 %collective-permute-start.7 = (bf16[3,64,256]{2,1,0:T(8,128)(2,1)S(1)}, bf16[3,64,256]{2,1,0:T(8,128)(2,1)S(1)}, u32[]{:S(2)}, u32[]{:S(2)}) collective-permute-start(bf16[3,64,256]{2,1,0:T(8,128)(2,1)S(1)} %get-tuple-element.55), channel_id=1, source_target_pairs={{0,5},{1,4},{2,7},{3,6},{4,8},{5,9},{6,10},{7,11},{8,13},{9,12},{1... | collective-permute-start | bytes 294920 | tf_op jit(solution)/shard_map/ppermute | solution.py:341
  26.9 4.5 %copy-start = (bf16[1,2,256,256]{3,2,1,0:T(8,128)(2,1)S(1)}, bf16[1,2,256,256]{3,2,1,0:T(8,128)(2,1)}, u32[]{:S(2)}) copy-start(bf16[1,2,256,256]{3,2,1,0:T(8,128)(2,1)} %param.8) | copy-start | bytes 786436
  26.9 4.5 %copy-start.1 = (bf16[2,256,256]{2,1,0:T(8,128)(2,1)S(1)}, bf16[2,256,256]{2,1,0:T(8,128)(2,1)}, u32[]{:S(2)}) copy-start(bf16[2,256,256]{2,1,0:T(8,128)(2,1)} %wf_ref.1) | copy-start | bytes 786436
  26.9 6.6 %collective-permute-start.10 = (bf16[3,64,256]{2,1,0:T(8,128)(2,1)S(1)}, bf16[3,64,256]{2,1,0:T(8,128)(2,1)S(1)}, u32[]{:S(2)}, u32[]{:S(2)}) collective-permute-start(bf16[3,64,256]{2,1,0:T(8,128)(2,1)S(1)} %add_first.1._.refs_0_), channel_id=1, source_target_pairs={{0,3},{1,2},{2,1},{3,0},{4,28},{5,29},{6,30},{7,31},{8,11},{9,10},... | collective-permute-start | bytes 294920 | tf_op jit(solution)/shard_map/ppermute | solution.py:343
  29.4 6.7 %collective-permute-start.9 = (bf16[3,64,256]{2,1,0:T(8,128)(2,1)S(1)}, bf16[3,64,256]{2,1,0:T(8,128)(2,1)S(1)}, u32[]{:S(2)}, u32[]{:S(2)}) collective-permute-start(bf16[3,64,256]{2,1,0:T(8,128)(2,1)S(1)} %add_first.1._.refs_0_), channel_id=1, source_target_pairs={{0,2},{1,3},{2,0},{3,1},{4,20},{5,21},{6,22},{7,23},{8,10},{9,11},... | collective-permute-start | bytes 294920 | tf_op jit(solution)/shard_map/ppermute | solution.py:343
  30.4 5.7 %collective-permute-start.8 = (bf16[3,64,256]{2,1,0:T(8,128)(2,1)S(1)}, bf16[3,64,256]{2,1,0:T(8,128)(2,1)S(1)}, u32[]{:S(2)}, u32[]{:S(2)}) collective-permute-start(bf16[3,64,256]{2,1,0:T(8,128)(2,1)S(1)} %add_first.1._.refs_0_), channel_id=1, source_target_pairs={{0,1},{1,0},{2,3},{3,2},{4,12},{5,13},{6,14},{7,15},{8,9},{9,8},{1... | collective-permute-start | bytes 294920 | tf_op jit(solution)/shard_map/ppermute | solution.py:343
  36.1 5.6 %collective-permute-start.15 = (bf16[3,64,256]{2,1,0:T(8,128)(2,1)S(1)}, bf16[3,64,256]{2,1,0:T(8,128)(2,1)S(1)}, u32[]{:S(2)}, u32[]{:S(2)}) collective-permute-start(bf16[3,64,256]{2,1,0:T(8,128)(2,1)S(1)} %add_second.1.refs_0_), channel_id=1, source_target_pairs={{0,24},{1,25},{2,26},{3,27},{4,7},{5,6},{6,5},{7,4},{8,16},{9,17},... | collective-permute-start | bytes 294920 | tf_op jit(solution)/shard_map/ppermute | solution.py:351
  38.5 4.6 %collective-permute-start.13 = (bf16[3,64,256]{2,1,0:T(8,128)(2,1)S(1)}, bf16[3,64,256]{2,1,0:T(8,128)(2,1)S(1)}, u32[]{:S(2)}, u32[]{:S(2)}) collective-permute-start(bf16[3,64,256]{2,1,0:T(8,128)(2,1)S(1)} %add_second.1.refs_0_), channel_id=1, source_target_pairs={{0,16},{1,17},{2,18},{3,19},{4,6},{5,7},{6,4},{7,5},{8,24},{9,25},... | collective-permute-start | bytes 294920 | tf_op jit(solution)/shard_map/ppermute | solution.py:351
  39.0 4.6 %collective-permute-start.17 = (bf16[3,64,256]{2,1,0:T(8,128)(2,1)S(1)}, bf16[3,64,256]{2,1,0:T(8,128)(2,1)S(1)}, u32[]{:S(2)}, u32[]{:S(2)}) collective-permute-start(bf16[3,64,256]{2,1,0:T(8,128)(2,1)S(1)} %add_second.1.refs_0_), channel_id=1, source_target_pairs={{0,8},{1,9},{2,10},{3,11},{4,5},{5,4},{6,7},{7,6},{8,0},{9,1},{10,... | collective-permute-start | bytes 294920 | tf_op jit(solution)/shard_map/ppermute | solution.py:351
  39.7 5.0 %collective-permute-start.12 = (bf16[3,64,256]{2,1,0:T(8,128)(2,1)S(1)}, bf16[3,64,256]{2,1,0:T(8,128)(2,1)S(1)}, u32[]{:S(2)}, u32[]{:S(2)}) collective-permute-start(bf16[3,64,256]{2,1,0:T(8,128)(2,1)S(1)} %add_second.1.refs_0_), channel_id=1, source_target_pairs={{0,12},{1,13},{2,14},{3,15},{4,1},{5,0},{6,3},{7,2},{8,4},{9,5},{1... | collective-permute-start | bytes 294920 | tf_op jit(solution)/shard_map/ppermute | solution.py:353
  39.7 5.0 %collective-permute-start.11 = (bf16[3,64,256]{2,1,0:T(8,128)(2,1)S(1)}, bf16[3,64,256]{2,1,0:T(8,128)(2,1)S(1)}, u32[]{:S(2)}, u32[]{:S(2)}) collective-permute-start(bf16[3,64,256]{2,1,0:T(8,128)(2,1)S(1)} %add_second.1.refs_0_), channel_id=1, source_target_pairs={{0,4},{4,0},{8,12},{12,8},{16,20},{20,16},{24,28},{28,24},{1,5},{5... | collective-permute-start | bytes 294920 | tf_op jit(solution)/shard_map/ppermute | solution.py:354
  41.7 3.0 %collective-permute-start.16 = (bf16[3,64,256]{2,1,0:T(8,128)(2,1)S(1)}, bf16[3,64,256]{2,1,0:T(8,128)(2,1)S(1)}, u32[]{:S(2)}, u32[]{:S(2)}) collective-permute-start(bf16[3,64,256]{2,1,0:T(8,128)(2,1)S(1)} %collective-permute-done.15.refs_3_), channel_id=1, source_target_pairs={{0,4},{4,0},{8,12},{12,8},{16,20},{20,16},{24,28},{28,24},{1,5},{5... | collective-permute-start | bytes 294920 | tf_op jit(solution)/shard_map/ppermute | solution.py:354
  43.2 1.5 %collective-permute-start.14 = (bf16[3,64,256]{2,1,0:T(8,128)(2,1)S(1)}, bf16[3,64,256]{2,1,0:T(8,128)(2,1)S(1)}, u32[]{:S(2)}, u32[]{:S(2)}) collective-permute-start(bf16[3,64,256]{2,1,0:T(8,128)(2,1)S(1)} %collective-permute-done.13.refs_2_), channel_id=1, source_target_pairs={{0,4},{4,0},{8,12},{12,8},{16,20},{20,16},{24,28},{28,24},{1,5},{5... | collective-permute-start | bytes 294920 | tf_op jit(solution)/shard_map/ppermute | solution.py:354
